TPU v7x, 32 devices: a whole 2x2x4 slice. The times are simulated.
32 devices in a mesh: dev: 32 (over z, y, x, core).
Axes of the slice: x: 2, y: 2, z: 4, core: 2. Of those that a mesh axis runs over, the one named last changes fastest.
Arguments:
- cotangent: bfloat16 [8192, 2048], P('dev'), may hold values from -6 to 6
- hot_table: bfloat16 [2048, 128], replicated, may hold values from -6 to 6
- cold_table: float32 [65536, 128], P('dev'), may hold values from -6 to 6
- cold_m: float32 [65536, 128], P('dev'), may hold values from -0.75 to 0.75
- cold_v: float32 [65536, 128], P('dev'), may hold values from 0.0001 to 0.01
- cross_down: bfloat16 [2048, 512], replicated, may hold values from -0.125 to 0.125
- cross_up: bfloat16 [512, 2048], replicated, may hold values from -0.25 to 0.25
- cross_bias: float32 [2048], replicated, may hold values from -6 to 6
- dense_master: float32 [2048, 1024], P('dev'), may hold values from -0.4375 to 0.4375
- dense_m: float32 [2048, 1024], P('dev'), may hold values from -6 to 6
- dense_v: float32 [2048, 1024], P('dev'), may hold values from 1 to 30
- hot_ids: int32 [8192, 16], P('dev'), may hold values from 0 to 2047
- lookup_slot: int32 [8192, 16], P('dev'), may hold values from -1 to 3071, as said below
- fetch_rows: int32 [32, 32, 96], P('dev'), may hold values from 0 to 2047, as said below
Outputs:
- hot_grad: float32 [2048, 128], replicated
- bias_grad: float32 [2048], replicated
- cold_new: float32 [65536, 128], P('dev')
- cold_m_new: float32 [65536, 128], P('dev')
- cold_v_new: float32 [65536, 128], P('dev')
- master_new: float32 [2048, 1024], P('dev')
- dense_m_new: float32 [2048, 1024], P('dev')
- dense_v_new: float32 [2048, 1024], P('dev')
- new_weights: bfloat16 [2048, 1024], replicated
Inputs may be any that keep to these rules, and one draw needn't show every extreme that they name: `lookup_slot`: -1 marks a hot lookup; any other value o * 96 + s reads slot s of the list that the lookup's device sends to owner o. For each device and owner the slots read are 0 to c - 1 for some c of at most 96, each read by exactly one lookup of that device; every device reads 96 slots from some owner, and some owner is read 96 slots by every device. `fetch_rows`: slots that no lookup reads still name rows.
All inputs are finite; a program needn't handle non-finite values.
Results may differ from a plain program's by a relative error of at most 0.0055.
Values may be sent and summed in bfloat16 or wider, within the bound.
No kernel may reach another device: no remote copies, remote signals or barrier semaphores. Data moves between devices by JAX's collectives and lax.ppermute only.
A program may use at most 128 MiB of HBM per device.

v0:
```python
import jax
import jax.numpy as jnp
from jax import lax
from jax.sharding import PartitionSpec as P

first_decay = 0.9
second_decay = 0.999
adam_epsilon = 1e-08
learn_rate = 0.01
first_fix = 1.0 - (0.9**10) ** 10
second_fix = 1.0 - (0.999**10) ** 10


def adam_update(params, moment_one, moment_two, gradient):
    moment_one = first_decay * moment_one + (1.0 - first_decay) * gradient
    moment_two = second_decay * moment_two + (1.0 - second_decay) * gradient * gradient
    params = params - learn_rate * (moment_one / first_fix) / (
        jnp.sqrt(moment_two / second_fix) + adam_epsilon
    )
    return (params, moment_one, moment_two)


def body(
    cotangent,
    hot_table,
    cold_table,
    cold_m,
    cold_v,
    cross_down,
    cross_up,
    cross_bias,
    dense_master,
    dense_m,
    dense_v,
    hot_ids,
    lookup_slot,
    fetch_rows,
):
    devices = lax.axis_size("dev")
    sample_count, fields = hot_ids.shape
    slab_rows, emb_width = cold_table.shape
    hot_rows = hot_table.shape[0]
    capacity = fetch_rows.shape[2]
    cross_width = cross_down.shape[0]
    shard_rows = dense_master.shape[0]
    scale_mean = 1.0 / devices
    requests = lax.all_to_all(fetch_rows, "dev", split_axis=1, concat_axis=0, tiled=True)
    request_flat = requests.reshape(devices * capacity)
    picked = jnp.take(cold_table, request_flat, axis=0).astype(jnp.bfloat16)
    fetched = lax.all_to_all(
        picked.reshape(devices, capacity, emb_width), "dev", split_axis=0, concat_axis=0, tiled=True
    )
    fetched_flat = fetched.reshape(devices * capacity, emb_width)
    is_hot = lookup_slot < 0
    cold_pos = jnp.maximum(lookup_slot, 0)
    chosen = jnp.where(
        is_hot[..., None],
        jnp.take(hot_table, hot_ids, axis=0),
        jnp.take(fetched_flat, cold_pos, axis=0),
    )
    inputs = chosen.reshape(sample_count, cross_width)
    latent = jnp.dot(inputs, cross_down, preferred_element_type=jnp.float32).astype(jnp.bfloat16)
    mixing = jnp.dot(latent, cross_up, preferred_element_type=jnp.float32) + cross_bias
    grad_f32 = cotangent.astype(jnp.float32)
    grad_mix = (grad_f32 * inputs.astype(jnp.float32)).astype(jnp.bfloat16)
    grad_latent = lax.dot_general(
        grad_mix, cross_up, (((1,), (1,)), ((), ())), preferred_element_type=jnp.float32
    ).astype(jnp.bfloat16)
    back_part = lax.dot_general(
        grad_latent, cross_down, (((1,), (1,)), ((), ())), preferred_element_type=jnp.float32
    )
    grad_input = grad_f32 * (mixing + 1.0) + back_part
    per_lookup = grad_input.reshape(sample_count * fields, emb_width)
    cold_target = jnp.where(is_hot, devices * capacity, lookup_slot).reshape(-1)
    cold_part = (
        jnp.zeros((devices * capacity, emb_width), jnp.float32)
        .at[cold_target]
        .add(per_lookup, mode="drop")
    )
    returned = lax.all_to_all(
        cold_part.reshape(devices, capacity, emb_width).astype(jnp.bfloat16),
        "dev",
        split_axis=0,
        concat_axis=0,
        tiled=True,
    ).astype(jnp.float32)
    cold_sum = (
        jnp.zeros((slab_rows, emb_width), jnp.float32)
        .at[request_flat]
        .add(returned.reshape(devices * capacity, emb_width))
    )
    cold_new, cold_m_new, cold_v_new = adam_update(
        cold_table, cold_m, cold_v, cold_sum * scale_mean
    )
    hot_target = jnp.where(is_hot, hot_ids, hot_rows).reshape(-1)
    hot_part = (
        jnp.zeros((hot_rows, emb_width), jnp.float32).at[hot_target].add(per_lookup, mode="drop")
    )
    bias_part = jnp.sum(grad_mix.astype(jnp.float32), axis=0)
    down_part = lax.dot_general(
        inputs, grad_latent, (((0,), (0,)), ((), ())), preferred_element_type=jnp.float32
    )
    up_part = lax.dot_general(
        grad_mix, latent, (((0,), (0,)), ((), ())), preferred_element_type=jnp.float32
    )
    dense_total, hot_sum, bias_sum = lax.psum(
        (jnp.concatenate([down_part, up_part], axis=1), hot_part, bias_part), "dev"
    )
    dense_own = lax.dynamic_slice_in_dim(
        dense_total, lax.axis_index("dev") * shard_rows, shard_rows, 0
    )
    master_new, dense_m_new, dense_v_new = adam_update(
        dense_master, dense_m, dense_v, dense_own * scale_mean
    )
    new_weights = lax.all_gather(master_new.astype(jnp.bfloat16), "dev", axis=0, tiled=True)
    return (
        hot_sum * scale_mean,
        bias_sum * scale_mean,
        cold_new,
        cold_m_new,
        cold_v_new,
        master_new,
        dense_m_new,
        dense_v_new,
        new_weights,
    )


def solution(mesh):
    return jax.shard_map(
        body,
        mesh=mesh,
        in_specs=(
            P("dev", None),
            P(),
            P("dev", None),
            P("dev", None),
            P("dev", None),
            P(),
            P(),
            P(),
            P("dev", None),
            P("dev", None),
            P("dev", None),
            P("dev", None),
            P("dev", None),
            P("dev", None, None),
        ),
        out_specs=(
            P(),
            P(),
            P("dev", None),
            P("dev", None),
            P("dev", None),
            P("dev", None),
            P("dev", None),
            P("dev", None),
            P(),
        ),
        check_vma=False,
    )
```

profile of v0, /device:TPU:0, one launch (start us, length us, event | category | flops | bytes accessed | tf_op | source)
XLA Modules:
  0.0 432.6 jit_solution(10667510595496123884)
XLA Ops:
  7.2 7.3 %all-to-all-start = ((s32[1,32,96]{2,0,1:T(1,128)}), s32[1,32,96]{2,0,1:T(1,128)S(1)}, u32[]{:S(2)}, u32[]{:S(2)}) async-start(s32[1,32,96]{2,0,1:T(1,128)} %bitcast.44), calls=%async_computation | async-start | bytes 32768 | tf_op jit(solution)/shard_map/all_to_all | solution.py:47
  15.2 1.3 broadcast_select_fusion
  19.5 2.1 all-to-all-done
  23.5 9.5 %gather_fusion.1 = bf16[3072,128]{1,0:T(8,128)(2,1)S(1)} fusion(f32[2048,128]{1,0:T(8,128)} %param.16, s32[3072]{0:T(1024)S(1)} %broadcast_clamp_fusion.2), kind=kCustom, calls=%fused_computation.1 | custom fusion | bytes 1585152 | tf_op jit(solution)/shard_map/jit(_take)/gather | solution.py:49
  33.1 1.3 select_convert_fusion
  34.4 3.7 all-to-all-start.1
  44.1 15.0 %gather_fusion = bf16[4096,128]{1,0:T(8,128)(2,1)} fusion(bf16[2048,128]{1,0:T(8,128)(2,1)S(1)} %copy-done.2, s32[4096]{0:T(1024)S(1)} %broadcast_clamp_fusion.1), kind=kCustom, calls=%fused_computation | custom fusion | bytes 2113536 | tf_op jit(solution)/shard_map/jit(_take)/gather | solution.py:58
  59.2 15.0 %gather_fusion.2 = bf16[4096,128]{1,0:T(8,128)(2,1)} fusion(bf16[3072,128]{1,0:T(8,128)(2,1)S(1)} %bitcast.32, s32[4096]{0:T(1024)S(1)} %broadcast_clamp_fusion), kind=kCustom, calls=%fused_computation.2 | custom fusion | bytes 2113536 | tf_op jit(solution)/shard_map/jit(_take)/gather | solution.py:59
  74.3 5.5 %select_select_fusion = bf16[256,16,128]{2,1,0:T(8,128)(2,1)S(1)} fusion(bf16[256,16,128]{2,1,0:T(8,128)(2,1)} %bitcast.39, bf16[256,16,128]{2,1,0:T(8,128)(2,1)} %bitcast.38, pred[256,16]{1,0:T(8,128)(4,1)S(1)} %copy-done.12, pred[256,16]{1,0:T(8,128)(4,1)S(1)} %copy-done.13, pred[256,16]{1,0:T(8,128)(4,1)S(1)} %copy-done.14), kind=kLoop, calls=%fused_computation.25 | loop fusion | flops 1572864 | bytes 3158016 | tf_op jit(solution)/shard_map/jit(_where)/select_n | solution.py:56
  81.8 2.8 fusion.15
  85.4 2.7 fusion.5
  88.9 1.5 reshape.213
  90.4 8.2 %pad_maximum_fusion = f32[2048,1024]{1,0:T(8,128)} fusion(f32[2048,512]{1,0:T(8,128)} %fusion.15, f32[2048,512]{1,0:T(8,128)} %fusion.5), kind=kLoop, calls=%fused_computation.6 | loop fusion | flops 2097152 | bytes 16777216 | tf_op jit(solution)/shard_map/concatenate | solution.py:107
  98.6 23.6 %scatter_custom_fusion = f32[2048,128]{1,0:T(8,128)} fusion(s32[4096]{0:T(1024)S(1)} %bitcast.45, f32[4096,128]{1,0:T(8,128)} %reshape.213, f32[]{:T(128)} %constant.31.clone.1), kind=kCustom, calls=%fused_computation.32 | custom fusion | flops 524288 | bytes 1049088 | tf_op jit(solution)/shard_map/scatter-add | solution.py:97
  122.3 192.6 %all-reduce.3.cloned.1.call-done = (f32[2048,128]{1,0:T(8,128)}, f32[2048,1024]{1,0:T(8,128)}) async-done(((f32[2048,128]{1,0:T(8,128)}, f32[2048,1024]{1,0:T(8,128)}), (f32[2048,128]{1,0:T(8,128)}, f32[2048,1024]{1,0:T(8,128)})) %all-reduce.3.cloned.1.call-update) | async-done | bytes 9437200 | tf_op jit(solution)/shard_map/psum | solution.py:106
  314.9 2.0 fusion.18
  317.2 23.9 %scatter_custom_fusion.1 = f32[3072,128]{1,0:T(8,128)} fusion(s32[4096]{0:T(1024)S(1)} %bitcast.46, f32[4096,128]{1,0:T(8,128)} %reshape.213, f32[]{:T(128)} %constant.31.clone.1), kind=kCustom, calls=%fused_computation.28 | custom fusion | flops 524288 | bytes 1573376 | tf_op jit(solution)/shard_map/scatter-add | solution.py:78
  341.0 2.5 convert_element_type.39
  343.5 4.8 %all-to-all-start.2 = ((bf16[32,96,128]{2,1,0:T(8,128)(2,1)}), bf16[32,96,128]{2,1,0:T(8,128)(2,1)}, u32[]{:S(2)}, u32[]{:S(2)}) async-start(bf16[32,96,128]{2,1,0:T(8,128)(2,1)} %bitcast.9), calls=%async_computation.2 | async-start | bytes 1572864 | tf_op jit(solution)/shard_map/all_to_all | solution.py:80
  348.8 49.5 %psum.22 = f32[2048]{0:T(1024)S(1)} all-reduce(f32[2048]{0:T(1024)S(1)} %convert_reduce_fusion), channel_id=1, replica_groups=mesh['dev'=32] {'dev'}, use_global_device_ids=true, to_apply=%region_3.4 | all-reduce | flops 2048 | bytes 16384 | tf_op jit(solution)/shard_map/psum | solution.py:106
  398.9 17.6 %scatter_custom_fusion.2 = f32[2048,128]{1,0:T(8,128)S(1)} fusion(s32[3072]{0:T(1024)} %bitcast.43, bf16[3072,128]{1,0:T(8,128)(2,1)} %bitcast.11, f32[]{:T(128)} %constant.31.clone.1), kind=kCustom, calls=%fused_computation.14 | custom fusion | flops 786432 | bytes 1835520 | tf_op jit(solution)/shard_map/scatter-add | solution.py:90
  416.5 3.4 divide_subtract_fusion
  419.9 1.0 broadcast_multiply_fusion
  420.9 4.8 %copy.106 = bf16[2048,1024]{1,0:T(8,128)(2,1)} copy(bf16[2048,1024]{1,0:T(8,128)(2,1)} %all-gather.2.cloned.1.call-done) | data formatting | bytes 8388608
  (77 shorter events, 16.4 us)
Async XLA Ops:
  7.2 73.4 %copy-start = (bf16[512,2048]{1,0:T(8,128)(2,1)S(1)}, bf16[512,2048]{1,0:T(8,128)(2,1)}, u32[]{:S(2)}) copy-start(bf16[512,2048]{1,0:T(8,128)(2,1)} %param.20) | copy-start | bytes 6291460
  7.2 14.4 %all-to-all-start = ((s32[1,32,96]{2,0,1:T(1,128)}), s32[1,32,96]{2,0,1:T(1,128)S(1)}, u32[]{:S(2)}, u32[]{:S(2)}) async-start(s32[1,32,96]{2,0,1:T(1,128)} %bitcast.44), calls=%async_computation | async-start | bytes 32768 | tf_op jit(solution)/shard_map/all_to_all | solution.py:47
  33.1 5.1 %copy-start.17 = (s32[256,16]{0,1:T(8,128)S(1)}, s32[256,16]{0,1:T(8,128)}, u32[]{:S(2)}) copy-start(s32[256,16]{0,1:T(8,128)} %param.25) | copy-start | bytes 49156
  33.1 11.0 %copy-start.2 = (bf16[2048,128]{1,0:T(8,128)(2,1)S(1)}, bf16[2048,128]{1,0:T(8,128)(2,1)}, u32[]{:S(2)}) copy-start(bf16[2048,128]{1,0:T(8,128)(2,1)} %param.15) | copy-start | bytes 1572868
  34.4 24.8 %all-to-all-start.1 = ((bf16[32,96,128]{2,1,0:T(8,128)(2,1)}), bf16[32,96,128]{2,1,0:T(8,128)(2,1)S(1)}, u32[]{:S(2)}, u32[]{:S(2)}) async-start(bf16[32,96,128]{2,1,0:T(8,128)(2,1)} %select_convert_fusion), calls=%async_computation.1 | async-start | bytes 1572864 | tf_op jit(solution)/shard_map/all_to_all | solution.py:50
  38.1 276.8 %all-reduce.3.cloned.1.call-start = ((), (), s32[]{:S(2)}) async-start(), calls=%async_computation.4 | async-start | bytes 18874368 | tf_op jit(solution)/shard_map/psum | solution.py:106
  44.1 15.0 %copy-start.16 = (s32[4096]{0:T(1024)S(1)}, s32[4096]{0:T(1024)}, u32[]{:S(2)}) copy-start(s32[4096]{0:T(1024)} %reshape.195) | copy-start | bytes 49156
  44.1 15.1 %copy-start.15 = (s32[4096,1]{0,1:T(1,128)S(1)}, s32[4096,1]{0,1:T(1,128)}, u32[]{:S(2)}) copy-start(s32[4096,1]{0,1:T(1,128)} %reshape.167) | copy-start | bytes 49156
  59.2 15.1 %copy-start.12 = (pred[256,16]{1,0:T(8,128)(4,1)S(1)}, pred[256,16]{1,0:T(8,128)(4,1)}, u32[]{:S(2)}) copy-start(pred[256,16]{1,0:T(8,128)(4,1)} %copy.81) | copy-start | bytes 12292
  59.2 15.1 %copy-start.13 = (pred[256,16]{1,0:T(8,128)(4,1)S(1)}, pred[256,16]{1,0:T(8,128)(4,1)}, u32[]{:S(2)}) copy-start(pred[256,16]{1,0:T(8,128)(4,1)} %copy.79) | copy-start | bytes 12292
  59.2 15.1 %copy-start.14 = (pred[256,16]{1,0:T(8,128)(4,1)S(1)}, pred[256,16]{1,0:T(8,128)(4,1)}, u32[]{:S(2)}) copy-start(pred[256,16]{1,0:T(8,128)(4,1)} %copy.78) | copy-start | bytes 12292
  74.3 5.6 %copy-start.6 = (bf16[2048,512]{1,0:T(8,128)(2,1)S(1)}, bf16[2048,512]{1,0:T(8,128)(2,1)}, u32[]{:S(2)}) copy-start(bf16[2048,512]{1,0:T(8,128)(2,1)} %param.19) | copy-start | bytes 6291460
  79.8 1.2 copy-start.4
  81.8 2.8 copy-start.19
  122.2 192.7 %copy-start.9 = (f32[64,1024]{1,0:T(8,128)S(1)}, f32[64,1024]{1,0:T(8,128)}, u32[]{:S(2)}) copy-start(f32[64,1024]{1,0:T(8,128)} %param.22) | copy-start | bytes 786436
  122.2 192.7 %copy-start.10 = (f32[64,1024]{1,0:T(8,128)S(1)}, f32[64,1024]{1,0:T(8,128)}, u32[]{:S(2)}) copy-start(f32[64,1024]{1,0:T(8,128)} %param.23) | copy-start | bytes 786436
  122.2 192.7 %copy-start.11 = (f32[64,1024]{1,0:T(8,128)S(1)}, f32[64,1024]{1,0:T(8,128)}, u32[]{:S(2)}) copy-start(f32[64,1024]{1,0:T(8,128)} %param.24) | copy-start | bytes 786436
  122.2 298.7 %all-gather.2.cloned.1.call-start = ((), (), s32[]{:S(2)}) async-start(), calls=%async_computation.3 | async-start | bytes 4325376 | tf_op jit(solution)/shard_map/all_gather | solution.py:115
  341.0 7.2 %copy-start.5 = (bf16[256,2048]{1,0:T(8,128)(2,1)S(1)}, bf16[256,2048]{1,0:T(8,128)(2,1)}, u32[]{:S(2)}) copy-start(bf16[256,2048]{1,0:T(8,128)(2,1)} %param.14) | copy-start | bytes 3145732
  343.5 55.4 %all-to-all-start.2 = ((bf16[32,96,128]{2,1,0:T(8,128)(2,1)}), bf16[32,96,128]{2,1,0:T(8,128)(2,1)}, u32[]{:S(2)}, u32[]{:S(2)}) async-start(bf16[32,96,128]{2,1,0:T(8,128)(2,1)} %bitcast.9), calls=%async_computation.2 | async-start | bytes 1572864 | tf_op jit(solution)/shard_map/all_to_all | solution.py:80
  348.2 68.2 %copy-start.3 = (f32[2048,128]{1,0:T(8,128)S(1)}, f32[2048,128]{1,0:T(8,128)}, u32[]{:S(2)}) copy-start(f32[2048,128]{1,0:T(8,128)} %param.16) | copy-start | bytes 3145732
  348.7 67.7 %copy-start.7 = (f32[2048,128]{1,0:T(8,128)S(1)}, f32[2048,128]{1,0:T(8,128)}, u32[]{:S(2)}) copy-start(f32[2048,128]{1,0:T(8,128)} %param.17) | copy-start | bytes 3145732
  416.5 3.4 copy-start.8
  420.9 4.8 %copy-start.1 = (bf16[512,2048]{1,0:T(8,128)(2,1)S(1)}, bf16[512,2048]{1,0:T(8,128)(2,1)}, u32[]{:S(2)}) copy-start(bf16[512,2048]{1,0:T(8,128)(2,1)} %param.20) | copy-start | bytes 6291460
  (1 other events, 0.6 us)
Sparse Core Ops, SparseCore 0:
  122.4 192.4 all-reduce.2
  318.2 66.7 all-gather.1
where the time goes:
time: 434 us; the launch traced here: 433 us
  waiting for transfers between devices  195 us (45%)
  other arithmetic  94.9 us (22%)
  local copies, waits for them, and re-layouts  54.6 us (13%)
  blocking collectives  49.5 us (11%)
  starting transfers between devices  15.9 us (4%)
  between operations  14.4 us (3%)
  matrix products  8.51 us (2%)
    psum x1, waiting for transfers between devices, body(): lax.psum((jnp.concatenate([down_part, up_part], axis=1), hot_part, bias_p...  193 us
    psum x1, blocking collectives, body(): lax.psum((jnp.concatenate([down_part, up_part], axis=1), hot_part, bias_p...  49.5 us
    scatter-add x1, other arithmetic, body(): cold_part = jnp.zeros((devices * capacity, emb_width), jnp.float32).at[co...  23.9 us
    scatter-add x1, other arithmetic, body(): jnp.zeros((hot_rows, emb_width), jnp.float32).at[hot_target]  23.6 us
    scatter-add x1, other arithmetic, body(): cold_sum = jnp.zeros((slab_rows, emb_width), jnp.float32).at[request_flat...  17.6 us
    gather x1, local copies, waits for them, and re-layouts, body(): jnp.take(hot_table, hot_ids, axis=0)  15 us
    gather x1, local copies, waits for them, and re-layouts, body(): jnp.take(fetched_flat, cold_pos, axis=0)  15 us
    gather x1, local copies, waits for them, and re-layouts, body(): picked = jnp.take(cold_table, request_flat, axis=0).astype(jnp.bfloat16)  9.54 us
  transfers between devices with their start and end apart: 5, of which 2 were waited for; matrix products, arithmetic and copies ran while one was open for 17% of the time, Pallas kernels for 0%

commit v1 on v0

v1 whole, which is shorter than its diff:
```python
import functools

import jax
import jax.numpy as jnp
from jax import lax
from jax.experimental import pallas as pl
from jax.experimental.pallas import tpu as pltpu
from jax.sharding import PartitionSpec as P

first_decay = 0.9
second_decay = 0.999
adam_epsilon = 1e-08
learn_rate = 0.01
first_fix = 1.0 - (0.9**10) ** 10
second_fix = 1.0 - (0.999**10) ** 10

LANES = 128
f32 = jnp.float32
bf16 = jnp.bfloat16


def adam_update(params, moment_one, moment_two, gradient):
    moment_one = first_decay * moment_one + (1.0 - first_decay) * gradient
    moment_two = second_decay * moment_two + (1.0 - second_decay) * gradient * gradient
    params = params - learn_rate * (moment_one / first_fix) / (
        jnp.sqrt(moment_two / second_fix) + adam_epsilon
    )
    return (params, moment_one, moment_two)


def call(kernel, outs, args, flops, name, smem=(), scratch=(), vmem=48 << 20):
    specs = [
        pl.BlockSpec(memory_space=pltpu.SMEM if i in smem else pltpu.VMEM)
        for i in range(len(args))
    ]
    moved = sum(a.size * a.dtype.itemsize for a in list(args) + list(outs))
    return pl.pallas_call(
        kernel,
        out_shape=outs,
        in_specs=specs,
        out_specs=[pl.BlockSpec(memory_space=pltpu.VMEM)] * len(outs),
        scratch_shapes=list(scratch),
        compiler_params=pltpu.CompilerParams(vmem_limit_bytes=vmem),
        cost_estimate=pl.CostEstimate(flops=flops, bytes_accessed=moved, transcendentals=0),
        name=name,
    )(*args)


def one_hot(mask):
    return jnp.where(mask, 1.0, 0.0).astype(bf16)


def owner_pick_kernel(req_ref, table_ref, out_ref, half):
    half[...] = table_ref[...].astype(bf16)
    rows = table_ref.shape[0]
    lists = req_ref.shape[0]
    columns = jnp.transpose(req_ref[...])
    step = 4 if lists % 4 == 0 else 1
    for first in range(0, lists, step):
        parts = []
        for i in range(first, first + step):
            spread = columns[:, i : i + 1]
            parts.append(
                one_hot(spread == lax.broadcasted_iota(jnp.int32, (LANES, rows), 1))
            )
        hot = jnp.concatenate(parts, axis=0)
        out_ref[first * LANES : (first + step) * LANES, :] = jnp.dot(
            hot, half[...], preferred_element_type=f32
        ).astype(bf16)


def hot_pick_kernel(ids_ref, slot_ref, table_ref, out_ref):
    samples, fields = ids_ref.shape
    rows, width = table_ref.shape
    index = jnp.where(slot_ref[...] < 0, ids_ref[...], -1)
    for f in range(fields):
        hot = one_hot(
            index[:, f : f + 1] == lax.broadcasted_iota(jnp.int32, (samples, rows), 1)
        )
        out_ref[:, f * width : (f + 1) * width] = jnp.dot(
            hot, table_ref[...], preferred_element_type=f32
        ).astype(bf16)


def forward_kernel(
    side_ref,
    slot_ref,
    fetched_ref,
    hot_ref,
    cot_ref,
    down_ref,
    up_ref,
    latent_ref,
    grad_latent_ref,
    bias_ref,
    keep_down_ref,
    send_down_ref,
    keep_up_ref,
    send_up_ref,
    x0,
    gm,
):
    samples, fields = slot_ref.shape
    slots, width = fetched_ref.shape
    index = slot_ref[...]
    for f in range(fields):
        cols = slice(f * width, (f + 1) * width)
        hot = one_hot(
            index[:, f : f + 1] == lax.broadcasted_iota(jnp.int32, (samples, slots), 1)
        )
        cold = jnp.dot(hot, fetched_ref[...], preferred_element_type=f32)
        picked = (cold + hot_ref[:, cols].astype(f32)).astype(bf16)
        x0[:, cols] = picked
        mix = cot_ref[:, cols].astype(f32) * picked.astype(f32)
        mix = mix.astype(bf16)
        gm[:, cols] = mix
        bias_ref[:, cols] = jnp.sum(mix.astype(f32), axis=0, keepdims=True)
    latent = jnp.dot(x0[...], down_ref[...], preferred_element_type=f32).astype(bf16)
    latent_ref[...] = latent
    grad_latent = lax.dot_general(
        gm[...], up_ref[...], (((1,), (1,)), ((), ())), preferred_element_type=f32
    ).astype(bf16)
    grad_latent_ref[...] = grad_latent
    chips, shard, _ = keep_down_ref.shape
    side = side_ref[0]
    block = max(2 * shard, 256)
    for keep_ref, send_ref, left, right in (
        (keep_down_ref, send_down_ref, x0, grad_latent),
        (keep_up_ref, send_up_ref, gm, latent),
    ):
        for first in range(0, chips * 2 * shard, block):
            part = lax.dot_general(
                left[:, first : first + block],
                right,
                (((0,), (0,)), ((), ())),
                preferred_element_type=f32,
            )
            for j in range(block // (2 * shard)):
                one = part[2 * j * shard : (2 * j + 1) * shard]
                two = part[(2 * j + 1) * shard : (2 * j + 2) * shard]
                at = first // (2 * shard) + j
                keep_ref[at] = jnp.where(side == 0, one, two).astype(bf16)
                send_ref[at] = jnp.where(side == 0, two, one).astype(bf16)


def backward_kernel(
    slot_rows_ref,
    id_rows_ref,
    cot_ref,
    latent_ref,
    grad_latent_ref,
    down_ref,
    up_ref,
    bias_ref,
    cold_ref,
    hot_ref,
    grads,
):
    fields, samples = slot_rows_ref.shape
    slots, width = cold_ref.shape
    hot_rows = hot_ref.shape[0]
    latent = latent_ref[...]
    grad_latent = grad_latent_ref[...]
    for f in range(fields):
        cols = slice(f * width, (f + 1) * width)
        mixing = (
            jnp.dot(latent, up_ref[:, cols], preferred_element_type=f32) + bias_ref[:, cols]
        )
        back = lax.dot_general(
            grad_latent, down_ref[cols, :], (((1,), (1,)), ((), ())), preferred_element_type=f32
        )
        grad = cot_ref[:, cols].astype(f32) * (mixing + 1.0) + back
        high = grad.astype(bf16)
        rows = slice(f * samples, (f + 1) * samples)
        grads[rows, :width] = high
        grads[rows, width:] = (grad - high.astype(f32)).astype(bf16)
    slot_rows = slot_rows_ref[...]
    id_rows = jnp.where(slot_rows < 0, id_rows_ref[...], -1)
    block = 256
    for rows_of, total, ref, wide in (
        (slot_rows, slots, cold_ref, False),
        (id_rows, hot_rows, hot_ref, True),
    ):
        for first in range(0, total, block):
            place = lax.broadcasted_iota(jnp.int32, (block, samples), 0) + first
            hot = jnp.concatenate(
                [one_hot(rows_of[f : f + 1, :] == place) for f in range(fields)], axis=1
            )
            if wide:
                both = jnp.dot(hot, grads[...], preferred_element_type=f32)
                result = both[:, :width] + both[:, width:]
            else:
                result = jnp.dot(hot, grads[:, :width], preferred_element_type=f32)
            ref[first : first + block, :] = result.astype(bf16)


def cold_adam_kernel(
    scale, req_ref, ret_ref, table_ref, m_ref, v_ref, new_ref, m_new_ref, v_new_ref
):
    lists = req_ref.shape[0]
    block = table_ref.shape[0]
    place = lax.broadcasted_iota(jnp.int32, (block, LANES), 0) + pl.program_id(0) * block
    hot = jnp.concatenate(
        [one_hot(req_ref[i : i + 1, :] == place) for i in range(lists)], axis=1
    )
    total = jnp.dot(hot, ret_ref[...], preferred_element_type=f32) * scale
    new, m_new, v_new = adam_update(table_ref[...], m_ref[...], v_ref[...], total)
    new_ref[...] = new
    m_new_ref[...] = m_new
    v_new_ref[...] = v_new


def cold_adam(req, returned, table, m, v, scale):
    rows, width = table.shape
    block = 256
    tile = pl.BlockSpec((block, width), lambda i: (i, 0))
    whole = lambda a: pl.BlockSpec(a.shape, lambda i: (0, 0))
    like = jax.ShapeDtypeStruct(table.shape, f32)
    return pl.pallas_call(
        functools.partial(cold_adam_kernel, scale),
        grid=(rows // block,),
        in_specs=[whole(req), whole(returned), tile, tile, tile],
        out_specs=[tile] * 3,
        out_shape=[like] * 3,
        compiler_params=pltpu.CompilerParams(vmem_limit_bytes=48 << 20),
        cost_estimate=pl.CostEstimate(
            flops=4 * rows * width * returned.shape[0],
            bytes_accessed=24 * rows * width,
            transcendentals=0,
        ),
        name="cold_adam",
    )(req, returned, table, m, v)


def split_levels(devices):
    cores = 2 if devices % 2 == 0 else 1
    chips = devices // cores
    bits = chips.bit_length() - 1
    if chips != 1 << bits:
        return (chips, 1, 1, cores)
    low = bits // 3
    mid = (bits - low) // 2
    return (1 << (bits - low - mid), 1 << mid, 1 << low, cores)


def body(
    sizes,
    cotangent,
    hot_table,
    cold_table,
    cold_m,
    cold_v,
    cross_down,
    cross_up,
    cross_bias,
    dense_master,
    dense_m,
    dense_v,
    hot_ids,
    lookup_slot,
    fetch_rows,
):
    devices = lax.axis_size("dev")
    sample_count, fields = hot_ids.shape
    slab_rows, emb_width = cold_table.shape
    hot_rows = hot_table.shape[0]
    capacity = fetch_rows.shape[2]
    cross_width, rank = cross_down.shape
    shard = dense_master.shape[0]
    scale_mean = 1.0 / devices
    slots = devices * capacity
    SDS = jax.ShapeDtypeStruct

    me = lax.axis_index("dev")
    strides = [1] * 4
    for i in (2, 1, 0):
        strides[i] = strides[i + 1] * sizes[i + 1]
    digits = [(me // strides[i]) % sizes[i] for i in range(4)]

    def exchange(value, level, k):
        size, stride = sizes[level], strides[level]
        pairs = []
        for d in range(devices):
            digit = (d // stride) % size
            pairs.append((d, d + ((digit + k) % size - digit) * stride))
        return lax.ppermute(value, "dev", pairs)

    def reduce_over(value, level, axis):
        size, digit = sizes[level], digits[level]
        total = lax.dynamic_index_in_dim(value, digit, axis, keepdims=False).astype(f32)
        for k in range(1, size):
            out = lax.dynamic_index_in_dim(value, (digit + k) % size, axis, keepdims=False)
            total = total + exchange(out.astype(bf16), level, k).astype(f32)
        return total

    def reduce_chips(value, order):
        left = [0, 1, 2]
        for level in order:
            value = reduce_over(value, level, left.index(level))
            left.remove(level)
        return value

    def gather_over(value, level, axis):
        size, digit = sizes[level], digits[level]
        parts = [value] + [exchange(value, level, k) for k in range(1, size)]
        if size == 1:
            return jnp.expand_dims(value, axis)
        if size == 2:
            first = jnp.where(digit == 0, parts[0], parts[1])
            second = jnp.where(digit == 0, parts[1], parts[0])
            return jnp.stack([first, second], axis)
        stacked = jnp.stack(parts[::-1] + parts[:0:-1], axis)
        return lax.dynamic_slice_in_dim(stacked, size - 1 - digit, size, axis)

    def gather_chips(value, order):
        have = []
        for level in order:
            have = sorted(have + [level])
            value = gather_over(value, level, have.index(level))
        return value

    requests = lax.all_to_all(fetch_rows, "dev", split_axis=1, concat_axis=0, tiled=True)
    req = requests.reshape(slots // LANES, LANES)
    (picked,) = call(
        owner_pick_kernel,
        [SDS((slots, emb_width), bf16)],
        [req, cold_table],
        4 * slots * slab_rows * emb_width,
        "owner_pick",
        scratch=[pltpu.VMEM((slab_rows, emb_width), bf16)],
    )
    fetched = lax.all_to_all(
        picked.reshape(devices, capacity, emb_width), "dev", split_axis=0, concat_axis=0, tiled=True
    ).reshape(slots, emb_width)
    (hot_x0,) = call(
        hot_pick_kernel,
        [SDS((sample_count, cross_width), bf16)],
        [hot_ids, lookup_slot, hot_table],
        4 * sample_count * fields * hot_rows * emb_width,
        "hot_pick",
    )
    chips = devices // sizes[3]
    part = SDS((chips, shard, rank), bf16)
    latent, grad_latent, bias_part, keep_down, send_down, keep_up, send_up = call(
        forward_kernel,
        [
            SDS((sample_count, rank), bf16),
            SDS((sample_count, rank), bf16),
            SDS((1, cross_width), f32),
            part,
            part,
            part,
            part,
        ],
        [
            digits[3].astype(jnp.int32).reshape(1),
            lookup_slot,
            fetched,
            hot_x0,
            cotangent,
            cross_down,
            cross_up,
        ],
        4 * sample_count * fields * slots * emb_width,
        "forward",
        smem=(0,),
        scratch=[pltpu.VMEM((sample_count, cross_width), bf16)] * 2,
    )
    cold_part, hot_part = call(
        backward_kernel,
        [SDS((slots, emb_width), bf16), SDS((hot_rows, emb_width), bf16)],
        [
            lookup_slot.T,
            hot_ids.T,
            cotangent,
            latent,
            grad_latent,
            cross_down,
            cross_up,
            cross_bias.reshape(1, cross_width),
        ],
        4 * sample_count * fields * (slots + hot_rows) * emb_width,
        "backward",
        scratch=[pltpu.VMEM((sample_count * fields, 2 * emb_width), bf16)],
    )
    returned = lax.all_to_all(
        cold_part.reshape(devices, capacity, emb_width),
        "dev",
        split_axis=0,
        concat_axis=0,
        tiled=True,
    ).reshape(slots, emb_width)

    chip_dims = sizes[:3]

    def chip_sum(keep, send):
        total = keep.astype(f32) + exchange(send, 3, 1).astype(f32)
        return total.reshape(chip_dims + total.shape[1:])

    down_own = reduce_chips(chip_sum(keep_down, send_down), (2, 1, 0))
    up_own = reduce_chips(chip_sum(keep_up, send_up), (1, 2, 0))

    own_hot = hot_rows // devices
    own_bias = cross_width // devices
    extra = 16
    bias_rows = jnp.pad(
        bias_part.reshape(devices, 1, own_bias).astype(bf16),
        ((0, 0), (0, extra - 1), (0, emb_width - own_bias)),
    )
    small = jnp.concatenate(
        [hot_part.reshape(devices, own_hot, emb_width), bias_rows], axis=1
    ).reshape(sizes + (own_hot + extra, emb_width))
    small_own = reduce_chips(reduce_over(small, 3, 3), (1, 2, 0))

    master_new, dense_m_new, dense_v_new = adam_update(
        dense_master,
        dense_m,
        dense_v,
        jnp.concatenate([down_own, up_own], axis=1) * scale_mean,
    )
    weights = master_new.astype(bf16)
    down_all = gather_over(gather_chips(weights[:, :rank], (0, 1, 2)), 3, 3)
    up_all = gather_over(gather_chips(weights[:, rank:], (0, 2, 1)), 3, 3)
    new_weights = jnp.concatenate([down_all, up_all], axis=5).reshape(cross_width, 2 * rank)
    small_all = gather_over(gather_chips((small_own * scale_mean).astype(bf16), (0, 1, 2)), 3, 3)
    small_all = small_all.reshape(devices, own_hot + extra, emb_width).astype(f32)
    hot_grad = small_all[:, :own_hot].reshape(hot_rows, emb_width)
    bias_grad = small_all[:, own_hot, :own_bias].reshape(cross_width)

    cold_new, cold_m_new, cold_v_new = cold_adam(
        req, returned, cold_table, cold_m, cold_v, scale_mean
    )
    return (
        hot_grad,
        bias_grad,
        cold_new,
        cold_m_new,
        cold_v_new,
        master_new,
        dense_m_new,
        dense_v_new,
        new_weights,
    )


def solution(mesh):
    sizes = split_levels(mesh.shape["dev"])
    return jax.shard_map(
        functools.partial(body, sizes),
        mesh=mesh,
        in_specs=(
            P("dev", None),
            P(),
            P("dev", None),
            P("dev", None),
            P("dev", None),
            P(),
            P(),
            P(),
            P("dev", None),
            P("dev", None),
            P("dev", None),
            P("dev", None),
            P("dev", None),
            P("dev", None, None),
        ),
        out_specs=(
            P(),
            P(),
            P("dev", None),
            P("dev", None),
            P("dev", None),
            P("dev", None),
            P("dev", None),
            P("dev", None),
            P(),
        ),
        check_vma=False,
    )
```

time: 434 us -> 221 us (0.51)
  waiting for transfers between devices: 195 us -> 81.3 us
  other arithmetic: 94.9 us -> 12.1 us
  Pallas kernels: 0 us -> 44.2 us
  local copies, waits for them, and re-layouts: 54.6 us -> 14.8 us
  blocking collectives: 49.5 us -> 14.4 us
  starting transfers between devices: 15.9 us -> 48.6 us
  between operations: 14.4 us -> 1.79 us
  matrix products: 8.51 us -> 0 us
    psum x1 -> x0, waiting for transfers between devices: 193 us -> none  [body(): lax.psum((jnp.concatenate([down_part, up_part], axis=1), hot_part, bias_p...]
    ppermute x0 -> x36, waiting for transfers between devices: none -> 67.8 us  [exchange(): return lax.ppermute(value, 'dev', pairs)]
    scatter-add x3 -> x0, other arithmetic: 65.1 us -> none  [the longest x1 23.9 us: body(): cold_part = jnp.zeros((devices * capacity, emb_width), jnp.float32).at[co...]
    psum x1 -> x0, blocking collectives: 49.5 us -> none  [body(): lax.psum((jnp.concatenate([down_part, up_part], axis=1), hot_part, bias_p...]
    pallas_call x0 -> x5, Pallas kernels: none -> 44.2 us  [the longest x4 38.2 us: call(): pl.pallas_call(kernel, out_shape=outs, in_specs=specs, out_specs=[pl.Bloc...]
    ppermute x0 -> x36, starting transfers between devices: none -> 43.2 us  [exchange(): return lax.ppermute(value, 'dev', pairs)]
    gather x3 -> x0, local copies, waits for them, and re-layouts: 39.6 us -> none  [the longest x1 15 us: body(): jnp.take(hot_table, hot_ids, axis=0)]
    all_to_all x0 -> x1, blocking collectives: none -> 14.4 us  [body(): lax.all_to_all(fetch_rows, 'dev', split_axis=1, concat_axis=0, tiled=True)]
  transfers between devices with their start and end apart: 5 -> 38, of which waited for: 2 -> 22; matrix products, arithmetic and copies ran while one was open for 17% -> 5% of each run, Pallas kernels for 0% -> 5%
where the time goes in v1:
time: 221 us; the launch traced here: 217 us
  waiting for transfers between devices  81.3 us (37%)
  starting transfers between devices  48.6 us (22%)
  Pallas kernels  44.2 us (20%)
  local copies, waits for them, and re-layouts  14.8 us (7%)
  blocking collectives  14.4 us (7%)
  other arithmetic  12.1 us (5%)
    ppermute x36, waiting for transfers between devices, exchange(): return lax.ppermute(value, 'dev', pairs)  67.8 us
    ppermute x36, starting transfers between devices, exchange(): return lax.ppermute(value, 'dev', pairs)  43.2 us
    pallas_call x4, Pallas kernels, call(): pl.pallas_call(kernel, out_shape=outs, in_specs=specs, out_specs=[pl.Bloc...  38.2 us
    all_to_all x1, blocking collectives, body(): lax.all_to_all(fetch_rows, 'dev', split_axis=1, concat_axis=0, tiled=True)  14.4 us
    all_to_all x1, waiting for transfers between devices, body(): lax.all_to_all(picked.reshape(devices, capacity, emb_width), 'dev', split...  13.6 us
    unnamed x63, local copies, waits for them, and re-layouts  9.32 us
    pallas_call x1, Pallas kernels, cold_adam(): pl.pallas_call(functools.partial(cold_adam_kernel, scale), grid=(rows //...  6.04 us
    another operation x16, other arithmetic, gather_over(): return jnp.stack([first, second], axis)  5.77 us
  transfers between devices with their start and end apart: 38, of which 22 were waited for; matrix products, arithmetic and copies ran while one was open for 5% of the time, Pallas kernels for 5%

profile of v1, /device:TPU:0, one launch (start us, length us, event | category | flops | bytes accessed | tf_op | source)
XLA Modules:
  0.0 217.2 jit_solution(14429664974274417440)
XLA Ops:
  0.6 14.4 %all_to_all.19 = s32[1,32,96]{2,0,1:T(1,128)S(1)} all-to-all(s32[1,32,96]{2,0,1:T(1,128)} %bitcast.182), channel_id=1, replica_groups=mesh['dev'=32] {'dev'}, dimensions={1} | all-to-all | bytes 24576 | tf_op jit(solution)/shard_map/all_to_all | solution.py:322
  17.5 4.6 %owner_pick.1 = bf16[3072,128]{1,0:T(8,128)(2,1)} custom-call(s32[24,128]{1,0:T(8,128)S(1)} %reshape.95.req_ref, f32[2048,128]{1,0:T(8,128)S(1)} %copy-done.4), custom_call_target="tpu_custom_call" | custom-call | flops 3221225472 | bytes 1847296 | tf_op jit(solution)/shard_map/owner_pick/pallas_call | solution.py:37
  22.1 2.8 %all-to-all-start.1 = ((bf16[32,96,128]{2,1,0:T(8,128)(2,1)}), bf16[32,96,128]{2,1,0:T(8,128)(2,1)S(1)}, u32[]{:S(2)}, u32[]{:S(2)}) async-start(bf16[32,96,128]{2,1,0:T(8,128)(2,1)} %bitcast.4), calls=%async_computation.1 | async-start | bytes 1572864 | tf_op jit(solution)/shard_map/all_to_all | solution.py:332
  26.2 4.6 %hot_pick.1.hot_ref = bf16[256,2048]{1,0:T(8,128)(2,1)S(1)} custom-call(s32[256,16]{1,0:T(8,128)S(1)} %copy.78.ids_ref, s32[256,16]{1,0:T(8,128)S(1)} %copy.80.slot_ref, bf16[2048,128]{1,0:T(8,128)(2,1)S(1)} %copy-done.8), custom_call_target="tpu_custom_call" | custom-call | flops 4294967296 | bytes 1605632 | tf_op jit(solution)/shard_map/hot_pick/pallas_call | solution.py:37
  31.8 13.6 %all-to-all-done.1 = bf16[32,96,128]{2,1,0:T(8,128)(2,1)S(1)} async-done(((bf16[32,96,128]{2,1,0:T(8,128)(2,1)}), bf16[32,96,128]{2,1,0:T(8,128)(2,1)S(1)}, u32[]{:S(2)}, u32[]{:S(2)}) %all-to-all-start.1) | async-done | bytes 786464 | tf_op jit(solution)/shard_map/all_to_all | solution.py:332
  45.3 13.8 %forward.1 = (bf16[256,512]{1,0:T(8,128)(2,1)S(1)}, bf16[256,512]{1,0:T(8,128)(2,1)S(1)}, f32[1,2048]{1,0:T(1,128)S(1)}, bf16[16,64,512]{2,1,0:T(8,128)(2,1)S(1)...) custom-call(s32[1]{0:T(128)} %bitcast.2.side_ref, ...), custom_call_target="tpu_custom_call" | custom-call | flops 6442450944 | bytes 11821060 | tf_op jit(solution)/shard_map/forward/pallas_call | solution.py:37
  63.7 15.3 %backward.1 = (bf16[3072,128]{1,0:T(8,128)(2,1)}, bf16[2048,128]{1,0:T(8,128)(2,1)S(1)}) custom-call(s32[16,256]{1,0:T(8,128)S(1)} %bitcast.171, s32[16,256]{1,0:T(8,128)S(1)} %bitcast.172, bf16[256,2048]{1,0:T(8,128)(2,1)S(1)} %copy-done.3, bf16[256,512]{1,0:T(8,128)(2,1)S(1)} %get-tuple-element.21.latent_ref, bf16[256,512]{1,0:T(8,128)(2,1)S(1)} %copy-done.12, ...), custom_call_target="tpu_custom_call" | custom-call | flops 10737418240 | bytes 7118848 | tf_op jit(solution)/shard_map/backward/pallas_call | solution.py:37
  82.5 4.7 %collective-permute-done.1 = bf16[4,2,80,128]{3,2,0,1:T(8,128)(2,1)S(1)} collective-permute-done((bf16[4,2,80,128]{3,2,0,1:T(8,128)(2,1)S(1)}, bf16[4,2,80,128]{3,2,0,1:T(8,128)(2,1)S(1)}, u32[]{:S(2)}, u32[]{:S(2)}) %collective-permute-start.1) | collective-permute-done | bytes 163872 | tf_op jit(solution)/shard_map/ppermute | solution.py:286
  88.9 2.9 %collective-permute-done.2 = bf16[4,80,128]{2,1,0:T(8,128)(2,1)S(1)} collective-permute-done((bf16[4,80,128]{2,1,0:T(8,128)(2,1)S(1)}, bf16[4,80,128]{2,1,0:T(8,128)(2,1)S(1)}, u32[]{:S(2)}, u32[]{:S(2)}) %collective-permute-start.2) | collective-permute-done | bytes 81952 | tf_op jit(solution)/shard_map/ppermute | solution.py:286
  93.6 2.7 %collective-permute-start.5 = (bf16[80,128]{1,0:T(8,128)(2,1)S(1)}, bf16[80,128]{1,0:T(8,128)(2,1)S(1)}, u32[]{:S(2)}, u32[]{:S(2)}) collective-permute-start(bf16[80,128]{1,0:T(8,128)(2,1)S(1)} %get-tuple-element.64), channel_id=1, source_target_pairs={{0,24},{1,25},{2,26},{3,27},{4,28},{5,29},{6,30},{7,31},{8,0},{9,1... | collective-permute-start | bytes 61448 | tf_op jit(solution)/shard_map/ppermute | solution.py:286
  98.3 3.7 %collective-permute-start.6 = (bf16[80,128]{1,0:T(8,128)(2,1)S(1)}, bf16[80,128]{1,0:T(8,128)(2,1)S(1)}, u32[]{:S(2)}, u32[]{:S(2)}) collective-permute-start(bf16[80,128]{1,0:T(8,128)(2,1)S(1)} %fusion.21), channel_id=1, source_target_pairs={{0,24},{1,25},{2,26},{3,27},{4,28},{5,29},{6,30},{7,31},{8,0},{9,1... | collective-permute-start | bytes 61448 | tf_op jit(solution)/shard_map/ppermute | solution.py:286
  103.5 3.8 %collective-permute-done.7 = bf16[80,128]{1,0:T(8,128)(2,1)S(1)} collective-permute-done((bf16[80,128]{1,0:T(8,128)(2,1)S(1)}, bf16[80,128]{1,0:T(8,128)(2,1)S(1)}, u32[]{:S(2)}, u32[]{:S(2)}) %collective-permute-start.7) | collective-permute-done | bytes 20512 | tf_op jit(solution)/shard_map/ppermute | solution.py:286
  109.4 2.6 %all-to-all-start.2 = ((bf16[32,96,128]{2,1,0:T(8,128)(2,1)}), bf16[32,96,128]{2,1,0:T(8,128)(2,1)S(1)}, u32[]{:S(2)}, u32[]{:S(2)}) async-start(bf16[32,96,128]{2,1,0:T(8,128)(2,1)} %bitcast.35), calls=%async_computation.2 | async-start | bytes 1572864 | tf_op jit(solution)/shard_map/all_to_all | solution.py:386
  119.5 6.1 %collective-permute-done.10 = bf16[4,2,80,128]{3,2,1,0:T(8,128)(2,1)S(1)} collective-permute-done((bf16[4,2,80,128]{3,2,1,0:T(8,128)(2,1)S(1)}, bf16[4,2,80,128]{3,2,1,0:T(8,128)(2,1)S(1)}, u32[]{:S(2)}, u32[]{:S(2)}) %collective-permute-start.10) | collective-permute-done | bytes 163872 | tf_op jit(solution)/shard_map/ppermute | solution.py:286
  125.6 12.3 %collective-permute-done.13 = bf16[4,2,64,512]{3,2,0,1:T(8,128)(2,1)S(1)} collective-permute-done((bf16[4,2,64,512]{3,2,0,1:T(8,128)(2,1)S(1)}, bf16[4,2,64,512]{3,2,0,1:T(8,128)(2,1)S(1)}, u32[]{:S(2)}, u32[]{:S(2)}) %collective-permute-start.13) | collective-permute-done | bytes 524320 | tf_op jit(solution)/shard_map/ppermute | solution.py:286
  140.6 5.5 %collective-permute-done.14 = bf16[4,64,512]{2,1,0:T(8,128)(2,1)S(1)} collective-permute-done((bf16[4,64,512]{2,1,0:T(8,128)(2,1)S(1)}, bf16[4,64,512]{2,1,0:T(8,128)(2,1)S(1)}, u32[]{:S(2)}, u32[]{:S(2)}) %collective-permute-start.14) | collective-permute-done | bytes 262176 | tf_op jit(solution)/shard_map/ppermute | solution.py:286
  152.9 2.8 %collective-permute-start.23 = (bf16[64,512]{1,0:T(8,128)(2,1)S(1)}, bf16[64,512]{1,0:T(8,128)(2,1)S(1)}, u32[]{:S(2)}, u32[]{:S(2)}) collective-permute-start(bf16[64,512]{1,0:T(8,128)(2,1)S(1)} %get-tuple-element.57), channel_id=1, source_target_pairs={{0,24},{1,25},{2,26},{3,27},{4,28},{5,29},{6,30},{7,31},{8,0},{9,1... | collective-permute-start | bytes 196616 | tf_op jit(solution)/shard_map/ppermute | solution.py:286
  161.0 3.1 %collective-permute-start.30 = (bf16[64,512]{1,0:T(8,128)(2,1)S(1)}, bf16[64,512]{1,0:T(8,128)(2,1)S(1)}, u32[]{:S(2)}, u32[]{:S(2)}) collective-permute-start(bf16[64,512]{1,0:T(8,128)(2,1)S(1)} %get-tuple-element.69), channel_id=1, source_target_pairs={{0,24},{1,25},{2,26},{3,27},{4,28},{5,29},{6,30},{7,31},{8,0},{9,1... | collective-permute-start | bytes 196616 | tf_op jit(solution)/shard_map/ppermute | solution.py:286
  164.9 3.3 %collective-permute-start.24 = (bf16[64,512]{1,0:T(8,128)(2,1)S(1)}, bf16[64,512]{1,0:T(8,128)(2,1)S(1)}, u32[]{:S(2)}, u32[]{:S(2)}) collective-permute-start(bf16[64,512]{1,0:T(8,128)(2,1)S(1)} %get-tuple-element.68), channel_id=1, source_target_pairs={{0,24},{1,25},{2,26},{3,27},{4,28},{5,29},{6,30},{7,31},{8,0},{9,1... | collective-permute-start | bytes 196616 | tf_op jit(solution)/shard_map/ppermute | solution.py:286
  169.3 3.2 %collective-permute-done.24 = bf16[64,512]{1,0:T(8,128)(2,1)S(1)} collective-permute-done((bf16[64,512]{1,0:T(8,128)(2,1)S(1)}, bf16[64,512]{1,0:T(8,128)(2,1)S(1)}, u32[]{:S(2)}, u32[]{:S(2)}) %collective-permute-start.24) | collective-permute-done | bytes 65568 | tf_op jit(solution)/shard_map/ppermute | solution.py:286
  175.3 3.2 %collective-permute-done.26 = bf16[64,512]{1,0:T(8,128)(2,1)S(1)} collective-permute-done((bf16[64,512]{1,0:T(8,128)(2,1)S(1)}, bf16[64,512]{1,0:T(8,128)(2,1)S(1)}, u32[]{:S(2)}, u32[]{:S(2)}) %collective-permute-start.26) | collective-permute-done | bytes 65568 | tf_op jit(solution)/shard_map/ppermute | solution.py:286
  180.9 4.9 %collective-permute-done.27 = bf16[4,64,512]{2,1,0:T(8,128)(2,1)S(1)} collective-permute-done((bf16[4,64,512]{2,1,0:T(8,128)(2,1)S(1)}, bf16[4,64,512]{2,1,0:T(8,128)(2,1)S(1)}, u32[]{:S(2)}, u32[]{:S(2)}) %collective-permute-start.27) | collective-permute-done | bytes 262176 | tf_op jit(solution)/shard_map/ppermute | solution.py:286
  188.3 10.1 %collective-permute-done.28 = bf16[4,2,64,512]{3,2,0,1:T(8,128)(2,1)S(1)} collective-permute-done((bf16[4,2,64,512]{3,2,0,1:T(8,128)(2,1)S(1)}, bf16[4,2,64,512]{3,2,0,1:T(8,128)(2,1)S(1)}, u32[]{:S(2)}, u32[]{:S(2)}) %collective-permute-start.28) | collective-permute-done | bytes 524320 | tf_op jit(solution)/shard_map/ppermute | solution.py:286
  204.7 6.0 %cold_adam.1 = (f32[2048,128]{1,0:T(8,128)}, f32[2048,128]{1,0:T(8,128)}, f32[2048,128]{1,0:T(8,128)}) custom-call(s32[24,128]{1,0:T(8,128)S(1)} %reshape.95.req_ref, bf16[3072,128]{1,0:T(8,128)(2,1)S(1)} %bitcast.168, f32[2048,128]{1,0:T(8,128)S(1)} %copy-done.5, f32[2048,128]{1,0:T(8,128)S(1)} %copy-done.6, f32[2048,128]{1,0:T(8,128)S(1)} %copy-done.7), custom_call_target="tpu_custom_call" | custom-call | flops 3221225472 | bytes 6291456 | tf_op jit(solution)/shard_map/cold_adam/pallas_call | solution.py:219
  (179 shorter events, 65.5 us)
Async XLA Ops:
  22.1 23.2 %all-to-all-start.1 = ((bf16[32,96,128]{2,1,0:T(8,128)(2,1)}), bf16[32,96,128]{2,1,0:T(8,128)(2,1)S(1)}, u32[]{:S(2)}, u32[]{:S(2)}) async-start(bf16[32,96,128]{2,1,0:T(8,128)(2,1)} %bitcast.4), calls=%async_computation.1 | async-start | bytes 1572864 | tf_op jit(solution)/shard_map/all_to_all | solution.py:332
  102.0 12.0 %collective-permute-start.12 = (bf16[16,64,512]{2,1,0:T(8,128)(2,1)}, bf16[16,64,512]{2,1,0:T(8,128)(2,1)}, u32[]{:S(2)}, u32[]{:S(2)}) collective-permute-start(bf16[16,64,512]{2,1,0:T(8,128)(2,1)} %get-tuple-element.30), channel_id=1, source_target_pairs={{0,1},{1,0},{2,3},{3,2},{4,5},{5,4},{6,7},{7,6},{8,9},{9,8},{10,11... | collective-permute-start | bytes 3145736 | tf_op jit(solution)/shard_map/ppermute | solution.py:286
  102.0 14.6 %collective-permute-start.18 = (bf16[16,64,512]{2,1,0:T(8,128)(2,1)}, bf16[16,64,512]{2,1,0:T(8,128)(2,1)}, u32[]{:S(2)}, u32[]{:S(2)}) collective-permute-start(bf16[16,64,512]{2,1,0:T(8,128)(2,1)} %get-tuple-element.32), channel_id=1, source_target_pairs={{0,1},{1,0},{2,3},{3,2},{4,5},{5,4},{6,7},{7,6},{8,9},{9,8},{10,11... | collective-permute-start | bytes 3145736 | tf_op jit(solution)/shard_map/ppermute | solution.py:286
  109.4 94.1 %all-to-all-start.2 = ((bf16[32,96,128]{2,1,0:T(8,128)(2,1)}), bf16[32,96,128]{2,1,0:T(8,128)(2,1)S(1)}, u32[]{:S(2)}, u32[]{:S(2)}) async-start(bf16[32,96,128]{2,1,0:T(8,128)(2,1)} %bitcast.35), calls=%async_computation.2 | async-start | bytes 1572864 | tf_op jit(solution)/shard_map/all_to_all | solution.py:386
  112.7 12.9 %collective-permute-start.10 = (bf16[4,2,80,128]{3,2,1,0:T(8,128)(2,1)S(1)}, bf16[4,2,80,128]{3,2,1,0:T(8,128)(2,1)S(1)}, u32[]{:S(2)}, u32[]{:S(2)}) collective-permute-start(bf16[4,2,80,128]{3,2,1,0:T(8,128)(2,1)S(1)} %pad_maximum_fusion.7), channel_id=1, source_target_pairs={{0,2},{1,3},{2,0},{3,1},{4,6},{5,7},{6,4},{7,5},{8,10},{9,11},{10,... | collective-permute-start | bytes 491528 | tf_op jit(solution)/shard_map/ppermute | solution.py:286
  115.6 22.3 %collective-permute-start.13 = (bf16[4,2,64,512]{3,2,0,1:T(8,128)(2,1)S(1)}, bf16[4,2,64,512]{3,2,0,1:T(8,128)(2,1)S(1)}, u32[]{:S(2)}, u32[]{:S(2)}) collective-permute-start(bf16[4,2,64,512]{3,2,0,1:T(8,128)(2,1)S(1)} %fusion), channel_id=1, source_target_pairs={{0,2},{1,3},{2,0},{3,1},{4,6},{5,7},{6,4},{7,5},{8,10},{9,11},{10,... | collective-permute-start | bytes 1572872 | tf_op jit(solution)/shard_map/ppermute | solution.py:286
  118.3 21.5 %collective-permute-start.19 = (bf16[4,2,64,512]{3,2,0,1:T(8,128)(2,1)S(1)}, bf16[4,2,64,512]{3,2,0,1:T(8,128)(2,1)S(1)}, u32[]{:S(2)}, u32[]{:S(2)}) collective-permute-start(bf16[4,2,64,512]{3,2,0,1:T(8,128)(2,1)S(1)} %fusion.1), channel_id=1, source_target_pairs={{0,4},{1,5},{2,6},{3,7},{4,0},{5,1},{6,2},{7,3},{8,12},{9,13},{10,... | collective-permute-start | bytes 1572872 | tf_op jit(solution)/shard_map/ppermute | solution.py:286
  138.2 7.9 %collective-permute-start.14 = (bf16[4,64,512]{2,1,0:T(8,128)(2,1)S(1)}, bf16[4,64,512]{2,1,0:T(8,128)(2,1)S(1)}, u32[]{:S(2)}, u32[]{:S(2)}) collective-permute-start(bf16[4,64,512]{2,1,0:T(8,128)(2,1)S(1)} %fusion.4), channel_id=1, source_target_pairs={{0,4},{1,5},{2,6},{3,7},{4,0},{5,1},{6,2},{7,3},{8,12},{9,13},{10,... | collective-permute-start | bytes 786440 | tf_op jit(solution)/shard_map/ppermute | solution.py:286
  140.0 11.7 %collective-permute-start.20 = (bf16[4,64,512]{2,1,0:T(8,128)(2,1)S(1)}, bf16[4,64,512]{2,1,0:T(8,128)(2,1)S(1)}, u32[]{:S(2)}, u32[]{:S(2)}) collective-permute-start(bf16[4,64,512]{2,1,0:T(8,128)(2,1)S(1)} %fusion.5), channel_id=1, source_target_pairs={{0,2},{1,3},{2,0},{3,1},{4,6},{5,7},{6,4},{7,5},{8,10},{9,11},{10,... | collective-permute-start | bytes 786440 | tf_op jit(solution)/shard_map/ppermute | solution.py:286
  147.8 7.9 %collective-permute-start.16 = (bf16[64,512]{1,0:T(8,128)(2,1)S(1)}, bf16[64,512]{1,0:T(8,128)(2,1)S(1)}, u32[]{:S(2)}, u32[]{:S(2)}) collective-permute-start(bf16[64,512]{1,0:T(8,128)(2,1)S(1)} %get-tuple-element.55), channel_id=1, source_target_pairs={{0,16},{1,17},{2,18},{3,19},{4,20},{5,21},{6,22},{7,23},{8,24},{9,... | collective-permute-start | bytes 196616 | tf_op jit(solution)/shard_map/ppermute | solution.py:286
  152.5 7.5 %collective-permute-start.22 = (bf16[64,512]{1,0:T(8,128)(2,1)S(1)}, bf16[64,512]{1,0:T(8,128)(2,1)S(1)}, u32[]{:S(2)}, u32[]{:S(2)}) collective-permute-start(bf16[64,512]{1,0:T(8,128)(2,1)S(1)} %get-tuple-element.58), channel_id=1, source_target_pairs={{0,16},{1,17},{2,18},{3,19},{4,20},{5,21},{6,22},{7,23},{8,24},{9,... | collective-permute-start | bytes 196616 | tf_op jit(solution)/shard_map/ppermute | solution.py:286
  152.9 7.0 %collective-permute-start.23 = (bf16[64,512]{1,0:T(8,128)(2,1)S(1)}, bf16[64,512]{1,0:T(8,128)(2,1)S(1)}, u32[]{:S(2)}, u32[]{:S(2)}) collective-permute-start(bf16[64,512]{1,0:T(8,128)(2,1)S(1)} %get-tuple-element.57), channel_id=1, source_target_pairs={{0,24},{1,25},{2,26},{3,27},{4,28},{5,29},{6,30},{7,31},{8,0},{9,1... | collective-permute-start | bytes 196616 | tf_op jit(solution)/shard_map/ppermute | solution.py:286
  161.0 7.2 %collective-permute-start.30 = (bf16[64,512]{1,0:T(8,128)(2,1)S(1)}, bf16[64,512]{1,0:T(8,128)(2,1)S(1)}, u32[]{:S(2)}, u32[]{:S(2)}) collective-permute-start(bf16[64,512]{1,0:T(8,128)(2,1)S(1)} %get-tuple-element.69), channel_id=1, source_target_pairs={{0,24},{1,25},{2,26},{3,27},{4,28},{5,29},{6,30},{7,31},{8,0},{9,1... | collective-permute-start | bytes 196616 | tf_op jit(solution)/shard_map/ppermute | solution.py:286
  164.2 24.1 %collective-permute-start.11 = (bf16[4,2,2,80,128]{4,3,2,1,0:T(8,128)(2,1)S(1)}, bf16[4,2,2,80,128]{4,3,2,1,0:T(8,128)(2,1)S(1)}, u32[]{:S(2)}, u32[]{:S(2)}) collective-permute-start(bf16[4,2,2,80,128]{4,3,2,1,0:T(8,128)(2,1)S(1)} %pad_maximum_fusion.5), channel_id=1, source_target_pairs={{0,1},{1,0},{2,3},{3,2},{4,5},{5,4},{6,7},{7,6},{8,9},{9,8},{10,11... | collective-permute-start | bytes 983048 | tf_op jit(solution)/shard_map/ppermute | solution.py:286
  164.2 10.6 %collective-permute-start.31 = (bf16[64,512]{1,0:T(8,128)(2,1)S(1)}, bf16[64,512]{1,0:T(8,128)(2,1)S(1)}, u32[]{:S(2)}, u32[]{:S(2)}) collective-permute-start(bf16[64,512]{1,0:T(8,128)(2,1)S(1)} %get-tuple-element.69), channel_id=1, source_target_pairs={{0,16},{1,17},{2,18},{3,19},{4,20},{5,21},{6,22},{7,23},{8,24},{9,... | collective-permute-start | bytes 196616 | tf_op jit(solution)/shard_map/ppermute | solution.py:286
  164.3 10.6 %collective-permute-start.32 = (bf16[64,512]{1,0:T(8,128)(2,1)S(1)}, bf16[64,512]{1,0:T(8,128)(2,1)S(1)}, u32[]{:S(2)}, u32[]{:S(2)}) collective-permute-start(bf16[64,512]{1,0:T(8,128)(2,1)S(1)} %get-tuple-element.69), channel_id=1, source_target_pairs={{0,8},{1,9},{2,10},{3,11},{4,12},{5,13},{6,14},{7,15},{8,16},{9,17... | collective-permute-start | bytes 196616 | tf_op jit(solution)/shard_map/ppermute | solution.py:286
  164.9 7.6 %collective-permute-start.24 = (bf16[64,512]{1,0:T(8,128)(2,1)S(1)}, bf16[64,512]{1,0:T(8,128)(2,1)S(1)}, u32[]{:S(2)}, u32[]{:S(2)}) collective-permute-start(bf16[64,512]{1,0:T(8,128)(2,1)S(1)} %get-tuple-element.68), channel_id=1, source_target_pairs={{0,24},{1,25},{2,26},{3,27},{4,28},{5,29},{6,30},{7,31},{8,0},{9,1... | collective-permute-start | bytes 196616 | tf_op jit(solution)/shard_map/ppermute | solution.py:286
  168.2 7.1 %collective-permute-start.25 = (bf16[64,512]{1,0:T(8,128)(2,1)S(1)}, bf16[64,512]{1,0:T(8,128)(2,1)S(1)}, u32[]{:S(2)}, u32[]{:S(2)}) collective-permute-start(bf16[64,512]{1,0:T(8,128)(2,1)S(1)} %get-tuple-element.68), channel_id=1, source_target_pairs={{0,16},{1,17},{2,18},{3,19},{4,20},{5,21},{6,22},{7,23},{8,24},{9,... | collective-permute-start | bytes 196616 | tf_op jit(solution)/shard_map/ppermute | solution.py:286
  178.6 7.2 %collective-permute-start.27 = (bf16[4,64,512]{2,1,0:T(8,128)(2,1)S(1)}, bf16[4,64,512]{2,1,0:T(8,128)(2,1)S(1)}, u32[]{:S(2)}, u32[]{:S(2)}) collective-permute-start(bf16[4,64,512]{2,1,0:T(8,128)(2,1)S(1)} %constant_dynamic-slice_fusion.1), channel_id=1, source_target_pairs={{0,4},{1,5},{2,6},{3,7},{4,0},{5,1},{6,2},{7,3},{8,12},{9,13},{10,... | collective-permute-start | bytes 786440 | tf_op jit(solution)/shard_map/ppermute | solution.py:286
  180.3 7.5 %collective-permute-start.33 = (bf16[4,64,512]{2,1,0:T(8,128)(2,1)S(1)}, bf16[4,64,512]{2,1,0:T(8,128)(2,1)S(1)}, u32[]{:S(2)}, u32[]{:S(2)}) collective-permute-start(bf16[4,64,512]{2,1,0:T(8,128)(2,1)S(1)} %constant_dynamic-slice_fusion), channel_id=1, source_target_pairs={{0,2},{1,3},{2,0},{3,1},{4,6},{5,7},{6,4},{7,5},{8,10},{9,11},{10,... | collective-permute-start | bytes 786440 | tf_op jit(solution)/shard_map/ppermute | solution.py:286
  185.9 12.5 %collective-permute-start.28 = (bf16[4,2,64,512]{3,2,0,1:T(8,128)(2,1)S(1)}, bf16[4,2,64,512]{3,2,0,1:T(8,128)(2,1)S(1)}, u32[]{:S(2)}, u32[]{:S(2)}) collective-permute-start(bf16[4,2,64,512]{3,2,0,1:T(8,128)(2,1)S(1)} %pad_maximum_fusion.3), channel_id=1, source_target_pairs={{0,2},{1,3},{2,0},{3,1},{4,6},{5,7},{6,4},{7,5},{8,10},{9,11},{10,... | collective-permute-start | bytes 1572872 | tf_op jit(solution)/shard_map/ppermute | solution.py:286
  187.9 11.8 %collective-permute-start.34 = (bf16[4,2,64,512]{3,2,0,1:T(8,128)(2,1)S(1)}, bf16[4,2,64,512]{3,2,0,1:T(8,128)(2,1)S(1)}, u32[]{:S(2)}, u32[]{:S(2)}) collective-permute-start(bf16[4,2,64,512]{3,2,0,1:T(8,128)(2,1)S(1)} %pad_maximum_fusion.4), channel_id=1, source_target_pairs={{0,4},{1,5},{2,6},{3,7},{4,0},{5,1},{6,2},{7,3},{8,12},{9,13},{10,... | collective-permute-start | bytes 1572872 | tf_op jit(solution)/shard_map/ppermute | solution.py:286
  199.6 11.1 %collective-permute-start.29 = (bf16[4,2,2,64,512]{4,3,0,2,1:T(8,128)(2,1)}, bf16[4,2,2,64,512]{4,3,0,2,1:T(8,128)(2,1)}, u32[]{:S(2)}, u32[]{:S(2)}) collective-permute-start(bf16[4,2,2,64,512]{4,3,0,2,1:T(8,128)(2,1)} %pad_maximum_fusion), channel_id=1, source_target_pairs={{0,1},{1,0},{2,3},{3,2},{4,5},{5,4},{6,7},{7,6},{8,9},{9,8},{10,11... | collective-permute-start | bytes 3145736 | tf_op jit(solution)/shard_map/ppermute | solution.py:286
  200.9 11.5 %collective-permute-start.35 = (bf16[4,2,2,64,512]{4,3,0,2,1:T(8,128)(2,1)}, bf16[4,2,2,64,512]{4,3,0,2,1:T(8,128)(2,1)}, u32[]{:S(2)}, u32[]{:S(2)}) collective-permute-start(bf16[4,2,2,64,512]{4,3,0,2,1:T(8,128)(2,1)} %pad_maximum_fusion.1), channel_id=1, source_target_pairs={{0,1},{1,0},{2,3},{3,2},{4,5},{5,4},{6,7},{7,6},{8,9},{9,8},{10,11... | collective-permute-start | bytes 3145736 | tf_op jit(solution)/shard_map/ppermute | solution.py:286
  (36 other events, 189.7 us)

commit v2 on v0

v2 whole, which is shorter than its diff:
```python
import functools

import jax
import jax.numpy as jnp
from jax import lax
from jax.experimental import pallas as pl
from jax.experimental.pallas import tpu as pltpu
from jax.sharding import PartitionSpec as P

first_decay = 0.9
second_decay = 0.999
adam_epsilon = 1e-08
learn_rate = 0.01
first_fix = 1.0 - (0.9**10) ** 10
second_fix = 1.0 - (0.999**10) ** 10

LANES = 128
VMEM_MOST = 48 << 20
f32 = jnp.float32
bf16 = jnp.bfloat16


def adam_update(params, moment_one, moment_two, gradient):
    moment_one = first_decay * moment_one + (1.0 - first_decay) * gradient
    moment_two = second_decay * moment_two + (1.0 - second_decay) * gradient * gradient
    params = params - learn_rate * (moment_one / first_fix) / (
        jnp.sqrt(moment_two / second_fix) + adam_epsilon
    )
    return (params, moment_one, moment_two)


def call(kernel, outs, args, flops, name, smem=(), hbm=(), out_hbm=(), scratch=(), vmem=24 << 20):
    specs = [
        pl.BlockSpec(
            memory_space=pltpu.SMEM if i in smem else pl.ANY if i in hbm else pltpu.VMEM
        )
        for i in range(len(args))
    ]
    moved = sum(a.size * a.dtype.itemsize for a in list(args) + list(outs))
    return pl.pallas_call(
        kernel,
        out_shape=outs,
        in_specs=specs,
        out_specs=[
            pl.BlockSpec(memory_space=pl.ANY if i in out_hbm else pltpu.VMEM)
            for i in range(len(outs))
        ],
        scratch_shapes=list(scratch),
        compiler_params=pltpu.CompilerParams(vmem_limit_bytes=vmem),
        cost_estimate=pl.CostEstimate(flops=flops, bytes_accessed=moved, transcendentals=0),
        name=name,
    )(*args)


def one_hot(mask):
    return jnp.where(mask, 1.0, 0.0).astype(bf16)


def ways(rows):
    return 4 if rows % 64 == 0 else 1


def fold(index, rows):
    part = rows // ways(rows)
    block = jnp.zeros_like(index)
    for j in range(1, ways(rows)):
        block = block + jnp.where(index >= j * part, 1, 0)
    return block, index - block * part


def lay_beside(table, out_ref):
    rows, width = table.shape
    part = rows // ways(rows)
    for j in range(ways(rows)):
        out_ref[:, j * width : (j + 1) * width] = table[j * part : (j + 1) * part].astype(bf16)


def pick_rows(block, place, folded, width):
    part = folded.shape[0]
    hot = one_hot(place == lax.broadcasted_iota(jnp.int32, (place.shape[0], part), 1))
    both = jnp.dot(hot, folded[...], preferred_element_type=f32)
    out = both[:, :width]
    for j in range(1, both.shape[1] // width):
        out = jnp.where(block == j, both[:, j * width : (j + 1) * width], out)
    return out


def columns_of(lists):
    turned = jnp.transpose(lists)
    return jnp.concatenate([turned[:, i : i + 1] for i in range(lists.shape[0])], axis=0)


def fold_table_kernel(table_ref, out_ref):
    lay_beside(table_ref[...], out_ref)


def fold_table(table):
    rows, width = table.shape
    return call(
        fold_table_kernel,
        [jax.ShapeDtypeStruct((rows // ways(rows), ways(rows) * width), bf16)],
        [table],
        0,
        "fold_table",
    )[0]


def owner_pick_kernel(rows, req_ref, folded_ref, out_ref):
    slots, width = out_ref.shape
    column = columns_of(req_ref[:, 0, :])
    block, place = fold(column, rows)
    step = 512 if slots % 512 == 0 else slots
    for first in range(0, slots, step):
        at = slice(first, first + step)
        out_ref[at, :] = pick_rows(block[at], place[at], folded_ref, width).astype(bf16)


def hot_pick_kernel(ids_ref, slot_ref, table_ref, out_ref, folded):
    samples, fields = ids_ref.shape
    rows, width = table_ref.shape
    lay_beside(table_ref[...], folded)
    block, place = fold(jnp.where(slot_ref[...] < 0, ids_ref[...], -1), rows)
    for f in range(fields):
        out_ref[:, f * width : (f + 1) * width] = pick_rows(
            block[:, f : f + 1], place[:, f : f + 1], folded, width
        ).astype(bf16)


def store_halves(digits_ref, dims, order, sums, first, keep_ref, send_ref):
    shard = keep_ref.shape[-2]
    side = digits_ref[3]
    for j in range(sums.shape[0] // (2 * shard)):
        one = sums[2 * j * shard : (2 * j + 1) * shard]
        two = sums[(2 * j + 1) * shard : (2 * j + 2) * shard]
        chip = first // (2 * shard) + j
        digit = (chip // (dims[1] * dims[2]), chip // dims[2] % dims[1], chip % dims[2])
        at = tuple(
            lax.rem(digit[level] - digits_ref[level] + dims[level], dims[level])
            for level in order
        )
        keep_ref[at] = jnp.where(side == 0, one, two).astype(bf16)
        send_ref[at] = jnp.where(side == 0, two, one).astype(bf16)


def outer_sums(digits_ref, dims, order, left, right, keep_ref, send_ref):
    block = max(2 * keep_ref.shape[-2], 256)
    for first in range(0, left.shape[1], block):
        sums = lax.dot_general(
            left[:, first : first + block],
            right,
            (((0,), (0,)), ((), ())),
            preferred_element_type=f32,
        )
        store_halves(digits_ref, dims, order, sums, first, keep_ref, send_ref)


def start_copies(sems, pairs, first=0):
    copies = [
        pltpu.make_async_copy(source, target, sems.at[first + i])
        for i, (source, target) in enumerate(pairs)
    ]
    for copy in copies:
        copy.start()
    return copies


def forward_kernel(
    dims,
    order_a,
    order_b,
    digits_ref,
    slot_ref,
    fetched_ref,
    cross_bias_ref,
    hot_hbm,
    cot_hbm,
    down_hbm,
    up_hbm,
    bias_ref,
    keep_a_hbm,
    send_a_hbm,
    keep_b_hbm,
    send_b_hbm,
    grad_hbm,
    x0,
    gm,
    folded,
    hot_ref,
    cot_ref,
    down_ref,
    up_ref,
    keep_a,
    send_a,
    keep_b,
    send_b,
    grad_ref,
    sems,
):
    copies = start_copies(
        sems, ((hot_hbm, hot_ref), (cot_hbm, cot_ref), (up_hbm, up_ref), (down_hbm, down_ref))
    )
    samples, fields = slot_ref.shape
    slots, width = fetched_ref.shape
    lay_beside(fetched_ref[...], folded)
    block, place = fold(slot_ref[...], slots)
    for f in range(fields):
        cols = slice(f * width, (f + 1) * width)
        cold = pick_rows(block[:, f : f + 1], place[:, f : f + 1], folded, width)
        if f == 0:
            copies[0].wait()
            copies[1].wait()
        picked = cold + hot_ref[:, cols].astype(f32)
        x0[:, cols] = picked.astype(bf16)
        mix = (cot_ref[:, cols].astype(f32) * picked).astype(bf16)
        gm[:, cols] = mix
        bias_ref[f : f + 1, :] = jnp.sum(mix.astype(f32), axis=0, keepdims=True)
    copies[2].wait()
    grad_latent = lax.dot_general(
        gm[...], up_ref[...], (((1,), (1,)), ((), ())), preferred_element_type=f32
    ).astype(bf16)
    outer_sums(digits_ref, dims, order_a, x0, grad_latent, keep_a, send_a)
    done = start_copies(sems, ((send_a, send_a_hbm), (keep_a, keep_a_hbm)), 4)
    copies[3].wait()
    latent = jnp.dot(x0[...], down_ref[...], preferred_element_type=f32).astype(bf16)
    outer_sums(digits_ref, dims, order_b, gm, latent, keep_b, send_b)
    done += start_copies(sems, ((send_b, send_b_hbm), (keep_b, keep_b_hbm)), 6)
    step = 4 if fields % 4 == 0 else fields
    for f in range(fields):
        cols = slice(f * width, (f + 1) * width)
        mixing = (
            jnp.dot(latent, up_ref[:, cols], preferred_element_type=f32) + cross_bias_ref[:, cols]
        )
        back = lax.dot_general(
            grad_latent, down_ref[cols, :], (((1,), (1,)), ((), ())), preferred_element_type=f32
        )
        grad = cot_ref[:, cols].astype(f32) * (mixing + 1.0) + back
        grad_ref[:, cols] = grad.astype(bf16)
        if (f + 1) % step == 0:
            part = slice((f + 1 - step) * width, (f + 1) * width)
            done += start_copies(
                sems, ((grad_ref.at[:, part], grad_hbm.at[:, part]),), 8 + f // step
            )
    for copy in done:
        copy.wait()


def add_up(lists, total, grads, use):
    fields, samples = lists.shape
    unused, place = fold(lists, total)
    part = total // ways(total)
    width = grads.shape[1] // ways(total)
    step = 256 if part % 256 == 0 else part
    for first in range(0, part, step):
        spot = lax.broadcasted_iota(jnp.int32, (step, samples), 0) + first
        hot = jnp.concatenate(
            [one_hot(place[f : f + 1, :] == spot) for f in range(fields)], axis=1
        )
        sums = jnp.dot(hot, grads[...], preferred_element_type=f32)
        for j in range(ways(total)):
            use(j * part + first, sums[:, j * width : (j + 1) * width])


def lay_by_block(block, grad, grads, rows):
    width = grad.shape[1]
    for j in range(grads.shape[1] // width):
        grads[rows, j * width : (j + 1) * width] = jnp.where(block == j, grad, 0.0).astype(bf16)


def lay_all_by_block(index, total, grad_ref, grads):
    samples, fields = index.shape
    width = grad_ref.shape[1] // fields
    block, unused = fold(index, total)
    for f in range(fields):
        lay_by_block(
            block[:, f : f + 1],
            grad_ref[:, f * width : (f + 1) * width].astype(f32),
            grads,
            slice(f * samples, (f + 1) * samples),
        )


def hot_sums_kernel(dims, order, digits_ref, id_ref, id_rows_ref, grad_ref, keep_ref, send_ref, grads):
    hot_rows = 2 * keep_ref.size // keep_ref.shape[-1]
    lay_all_by_block(id_ref[...], hot_rows, grad_ref, grads)

    def use(first, sums):
        store_halves(digits_ref, dims, order, sums, first, keep_ref, send_ref)

    add_up(id_rows_ref[...], hot_rows, grads, use)


def cold_sums_kernel(slot_ref, slot_rows_ref, grad_ref, bias_ref, cold_ref, grads):
    fields = slot_ref.shape[1]
    devices, capacity, width = cold_ref.shape
    capacity -= fields
    slots = devices * capacity
    lay_all_by_block(slot_ref[...], slots, grad_ref, grads)

    def use(first, sums):
        sums = sums.astype(bf16)
        at, end = first, first + sums.shape[0]
        while at < end:
            owner, slot = at // capacity, at % capacity
            count = min(capacity - slot, end - at)
            cold_ref[owner, slot : slot + count, :] = sums[at - first : at - first + count]
            at += count

    add_up(slot_rows_ref[...], slots, grads, use)
    bias = bias_ref[...].astype(bf16)
    for owner in range(devices):
        cold_ref[owner, capacity:, :] = bias


def cold_adam_kernel(
    scale, req_ref, ret_ref, table_ref, m_ref, v_ref, new_ref, m_new_ref, v_new_ref, spread
):
    lists = req_ref.shape[0]
    rows, width = table_ref.shape
    req = req_ref[...]
    block, unused = fold(columns_of(req), rows)
    returned = ret_ref[...].astype(f32)
    for j in range(ways(rows)):
        spread[:, j * width : (j + 1) * width] = jnp.where(block == j, returned, 0.0).astype(bf16)
    unused, place = fold(req, rows)
    part = rows // ways(rows)
    step = 256 if part % 256 == 0 else part
    for first in range(0, part, step):
        spot = lax.broadcasted_iota(jnp.int32, (step, LANES), 0) + first
        hot = jnp.concatenate(
            [one_hot(place[i : i + 1, :] == spot) for i in range(lists)], axis=1
        )
        sums = jnp.dot(hot, spread[...], preferred_element_type=f32)
        for j in range(ways(rows)):
            at = slice(j * part + first, j * part + first + step)
            new_ref[at, :], m_new_ref[at, :], v_new_ref[at, :] = adam_update(
                table_ref[at, :],
                m_ref[at, :],
                v_ref[at, :],
                sums[:, j * width : (j + 1) * width] * scale,
            )


def place_kernel(dims, plan, digits_ref, *refs):
    sources = refs[: len(plan)]
    out, hot_out, hot_rows, sems = refs[-4:]
    shard = sources[0].shape[-2]
    half = out.shape[1] // 2
    copies = []
    hots = 0
    for ref, (cols, main, k, core) in zip(sources, plan):
        other = 3 - main
        for i in range(ref.shape[0]):
            for j in range(ref.shape[1]):
                turn = {0: j, main: k, other: i}
                digit = [
                    lax.rem(digits_ref[level] - turn[level] + dims[level], dims[level])
                    for level in range(3)
                ]
                chip = (digit[0] * dims[1] + digit[1]) * dims[2] + digit[2]
                side = lax.rem(digits_ref[3] + core, 2)
                row = pl.multiple_of((chip * 2 + side) * shard, shard)
                copies.append(
                    (ref.at[i, j, :, :half], out.at[pl.ds(row, shard), pl.ds(cols * half, half)])
                )
                if cols == 0:
                    hot_rows[hots] = ref[i, j, :, half:].astype(f32)
                    copies.append((hot_rows.at[hots], hot_out.at[pl.ds(row, shard), :]))
                    hots += 1
    for copy in start_copies(sems, copies):
        copy.wait()


def place(dims, plan, digits, sources, rank, devices, before):
    shard, split = sources[0].shape[-2:]
    rows = shard * devices
    before = list(before or ())
    hbm, vmem = pl.BlockSpec(memory_space=pl.ANY), pl.BlockSpec(memory_space=pltpu.VMEM)
    first = 1 + len(sources)
    blocks = [s.shape[0] * s.shape[1] for s in sources]
    hots = sum(b for b, p in zip(blocks, plan) if p[0] == 0)
    return pl.pallas_call(
        functools.partial(place_kernel, dims, tuple(plan)),
        out_shape=[
            jax.ShapeDtypeStruct((rows, 2 * rank), bf16),
            jax.ShapeDtypeStruct((rows, split - rank), f32),
        ],
        in_specs=[pl.BlockSpec(memory_space=pltpu.SMEM)]
        + [vmem] * len(sources)
        + [hbm] * len(before),
        out_specs=[hbm, hbm],
        input_output_aliases={first + i: i for i in range(len(before))},
        scratch_shapes=[
            pltpu.VMEM((hots, shard, split - rank), f32),
            pltpu.SemaphoreType.DMA((sum(blocks) + hots,)),
        ],
        compiler_params=pltpu.CompilerParams(vmem_limit_bytes=24 << 20),
        cost_estimate=pl.CostEstimate(
            flops=0, bytes_accessed=4 * rows * rank, transcendentals=0
        ),
        name="place",
    )(digits, *sources, *before)


def split_levels(devices):
    cores = 2 if devices % 2 == 0 else 1
    chips = devices // cores
    bits = chips.bit_length() - 1
    if chips != 1 << bits:
        return (chips, 1, 1, cores)
    low = bits // 3
    mid = (bits - low) // 2
    return (1 << (bits - low - mid), 1 << mid, 1 << low, cores)


def body(
    sizes,
    cotangent,
    hot_table,
    cold_table,
    cold_m,
    cold_v,
    cross_down,
    cross_up,
    cross_bias,
    dense_master,
    dense_m,
    dense_v,
    hot_ids,
    lookup_slot,
    fetch_rows,
):
    devices = lax.axis_size("dev")
    sample_count, fields = hot_ids.shape
    slab_rows, emb_width = cold_table.shape
    hot_rows = hot_table.shape[0]
    capacity = fetch_rows.shape[2]
    cross_width, rank = cross_down.shape
    shard = dense_master.shape[0]
    scale_mean = 1.0 / devices
    slots = devices * capacity
    lookups = sample_count * fields
    dims = sizes[:3]
    SDS = jax.ShapeDtypeStruct

    me = lax.axis_index("dev")
    strides = [1] * 4
    for i in (2, 1, 0):
        strides[i] = strides[i + 1] * sizes[i + 1]
    digits = jnp.stack([(me // strides[i]) % sizes[i] for i in range(4)]).astype(jnp.int32)

    def exchange(value, level, k):
        size, stride = sizes[level], strides[level]
        pairs = []
        for d in range(devices):
            digit = (d // stride) % size
            pairs.append((d, d + ((digit + k) % size - digit) * stride))
        return lax.ppermute(value, "dev", pairs)

    def swap(value):
        return exchange(value, 3, 1) if sizes[3] == 2 else None

    def all_to_all(value):
        return lax.all_to_all(value, "dev", split_axis=0, concat_axis=0, tiled=True)

    folded = fold_table(cold_table)
    (hot_x0,) = call(
        hot_pick_kernel,
        [SDS((sample_count, cross_width), bf16)],
        [hot_ids, lookup_slot, hot_table],
        40 * lookups * hot_rows * emb_width,
        "hot_pick",
        scratch=[pltpu.VMEM((hot_rows // ways(hot_rows), ways(hot_rows) * emb_width), bf16)],
    )
    requests = all_to_all(fetch_rows.reshape(devices, 1, capacity))
    req = requests.reshape(slots // LANES, LANES)
    (picked,) = call(
        functools.partial(owner_pick_kernel, slab_rows),
        [SDS((slots, emb_width), bf16)],
        [requests, folded],
        4 * slots * slab_rows * emb_width,
        "owner_pick",
    )
    fetched = all_to_all(picked.reshape(devices, capacity, emb_width)).reshape(slots, emb_width)

    order_a, order_b = (2, 1, 0), (1, 2, 0)
    shape_a = tuple(dims[i] for i in order_a) + (shard, rank)
    shape_b = tuple(dims[i] for i in order_b) + (shard, rank)
    bias_part, keep_a, send_a, keep_b, send_b, grad_input = call(
        functools.partial(forward_kernel, dims, order_a, order_b),
        [
            SDS((fields, emb_width), f32),
            SDS(shape_a, bf16),
            SDS(shape_a, bf16),
            SDS(shape_b, bf16),
            SDS(shape_b, bf16),
            SDS((sample_count, cross_width), bf16),
        ],
        [
            digits,
            lookup_slot,
            fetched,
            cross_bias.reshape(1, cross_width),
            hot_x0,
            cotangent,
            cross_down,
            cross_up,
        ],
        4 * lookups * slots * emb_width,
        "forward",
        smem=(0,),
        hbm=(4, 5, 6, 7),
        out_hbm=(1, 2, 3, 4, 5),
        scratch=[
            pltpu.VMEM((sample_count, cross_width), bf16),
            pltpu.VMEM((sample_count, cross_width), bf16),
            pltpu.VMEM((slots // ways(slots), ways(slots) * emb_width), bf16),
            pltpu.VMEM((sample_count, cross_width), bf16),
            pltpu.VMEM((sample_count, cross_width), bf16),
            pltpu.VMEM(cross_down.shape, bf16),
            pltpu.VMEM(cross_up.shape, bf16),
            pltpu.VMEM(shape_a, bf16),
            pltpu.VMEM(shape_a, bf16),
            pltpu.VMEM(shape_b, bf16),
            pltpu.VMEM(shape_b, bf16),
            pltpu.VMEM((sample_count, cross_width), bf16),
            pltpu.SemaphoreType.DMA((8 + fields,)),
        ],
        vmem=VMEM_MOST,
    )
    got_a = swap(send_a)
    got_b = swap(send_b)
    own_hot = hot_rows // devices
    shape_hot = tuple(dims[i] for i in order_a) + (own_hot, emb_width)
    hot_index = jnp.where(lookup_slot < 0, hot_ids, -1)
    keep_hot, send_hot = call(
        functools.partial(hot_sums_kernel, dims, order_a),
        [SDS(shape_hot, bf16), SDS(shape_hot, bf16)],
        [digits, hot_index, hot_index.T, grad_input],
        4 * lookups * hot_rows * emb_width,
        "hot_sums",
        smem=(0,),
        scratch=[pltpu.VMEM((lookups, ways(hot_rows) * emb_width), bf16)],
        vmem=VMEM_MOST,
    )
    got_hot = swap(send_hot)

    def add(terms, *at):
        return functools.reduce(
            lambda s, t: s + t, [t[skip + at].astype(f32) for t, skip in terms]
        )

    def pack(groups, *at):
        return jnp.concatenate([add(terms, *at) for terms in groups], axis=-1)

    def step_sends(groups, level):
        return [pack(groups, k).astype(bf16) for k in range(1, sizes[level])]

    def step_takes(groups, level, sends):
        later = [[(t, skip + (0,)) for t, skip in terms] for terms in groups]
        for k, send in enumerate(sends):
            got = exchange(send, level, k + 1)
            start = 0
            for terms, old in zip(later, groups):
                wide = old[0][0].shape[-1]
                terms.append((got[..., start : start + wide], ()))
                start += wide
        return later

    groups_b = [[(keep_b, ()), (got_b, ())]]
    groups_a = [[(keep_a, ()), (got_a, ())], [(keep_hot, ()), (got_hot, ())]]
    sends_b = step_sends(groups_b, order_b[0])
    sends_a = step_sends(groups_a, order_a[0])
    grad_input, sends_a, sends_b = lax.optimization_barrier((grad_input, sends_a, sends_b))
    groups_b = step_takes(groups_b, order_b[0], sends_b)
    groups_a = step_takes(groups_a, order_a[0], sends_a)
    whole = capacity % 16 == 0
    (parcel,) = call(
        cold_sums_kernel,
        [
            SDS(
                (devices, capacity + fields, emb_width) if whole else (1, slots + fields, emb_width),
                bf16,
            )
        ],
        [lookup_slot, lookup_slot.T, grad_input, bias_part],
        4 * lookups * slots * emb_width,
        "cold_sums",
        scratch=[pltpu.VMEM((lookups, ways(slots) * emb_width), bf16)],
        vmem=VMEM_MOST,
    )
    if not whole:
        parcel = jnp.concatenate(
            [
                parcel[0, :slots].reshape(devices, capacity, emb_width),
                jnp.broadcast_to(parcel[:, slots:], (devices, fields, emb_width)),
            ],
            axis=1,
        )
    arrived = all_to_all(parcel)
    groups_b = step_takes(groups_b, order_b[1], step_sends(groups_b, order_b[1]))
    groups_a = step_takes(groups_a, order_a[1], step_sends(groups_a, order_a[1]))
    groups = [groups_a[0], groups_b[0], groups_a[1]]
    sums = [pack(groups, k) for k in range(sizes[0])]

    returned = arrived[:, :capacity].reshape(slots, emb_width)
    like = SDS(cold_table.shape, f32)
    cold_new, cold_m_new, cold_v_new = call(
        functools.partial(cold_adam_kernel, scale_mean),
        [like] * 3,
        [req, returned, cold_table, cold_m, cold_v],
        4 * slots * slab_rows * emb_width,
        "cold_adam",
        scratch=[pltpu.VMEM((slots, ways(slab_rows) * emb_width), bf16)],
    )
    bias_grad = (
        jnp.sum(arrived[:, capacity:].astype(f32), axis=0) * scale_mean
    ).reshape(cross_width)

    later = [exchange(sums[k].astype(bf16), 0, k) for k in range(1, sizes[0])]
    later, cold_new, cold_m_new, cold_v_new, bias_grad = lax.optimization_barrier(
        (later, cold_new, cold_m_new, cold_v_new, bias_grad)
    )
    dense_own = sums[0]
    for got in later:
        dense_own = dense_own + got.astype(f32)

    master_new, dense_m_new, dense_v_new = adam_update(
        dense_master, dense_m, dense_v, dense_own[:, : 2 * rank] * scale_mean
    )
    weights = jnp.concatenate(
        [master_new[:, :rank], dense_own[:, 2 * rank :] * scale_mean, master_new[:, rank:]], axis=1
    ).astype(bf16)
    split = rank + emb_width
    along_z = [weights] + [exchange(weights, 0, k) for k in range(1, sizes[0])]
    plan, got = [], []
    for cols, (level, main) in enumerate(((1, 2), (2, 1))):
        block = jnp.stack([w[:, split:] if cols else w[:, :split] for w in along_z])
        block = jnp.stack(
            [block] + [exchange(block, level, k) for k in range(1, sizes[level])]
        )
        for k in range(sizes[main]):
            plan.append((cols, main, k))
            got.append(exchange(block, main, k) if k else block)

    def put(which, core, values, before):
        return place(
            dims, [plan[i] + (core,) for i in which], digits, values, rank, devices, before
        )

    near = [i for i, p in enumerate(plan) if p[2] == 0]
    far = [i for i, p in enumerate(plan) if p[2] > 0]
    outs = put(near, 0, [got[i] for i in near], None)
    outs = put(near, 1, [swap(got[i]) for i in near], outs)
    if far:
        values, outs = lax.optimization_barrier(([got[i] for i in far], outs))
        others = [swap(v) for v in values]
        outs = put(far, 0, values, outs)
        outs = put(far, 1, others, outs)
    new_weights, hot_grad = outs
    return (
        hot_grad,
        bias_grad,
        cold_new,
        cold_m_new,
        cold_v_new,
        master_new,
        dense_m_new,
        dense_v_new,
        new_weights,
    )


def solution(mesh):
    sizes = split_levels(mesh.shape["dev"])
    return jax.shard_map(
        functools.partial(body, sizes),
        mesh=mesh,
        in_specs=(
            P("dev", None),
            P(),
            P("dev", None),
            P("dev", None),
            P("dev", None),
            P(),
            P(),
            P(),
            P("dev", None),
            P("dev", None),
            P("dev", None),
            P("dev", None),
            P("dev", None),
            P("dev", None, None),
        ),
        out_specs=(
            P(),
            P(),
            P("dev", None),
            P("dev", None),
            P("dev", None),
            P("dev", None),
            P("dev", None),
            P("dev", None),
            P(),
        ),
        check_vma=False,
    )
```

time: 434 us -> 167 us (0.38)
  waiting for transfers between devices: 195 us -> 62.7 us
  other arithmetic: 94.9 us -> 13.3 us
  blocking collectives: 49.5 us -> 0 us
  Pallas kernels: 0 us -> 42.9 us
  local copies, waits for them, and re-layouts: 54.6 us -> 12.4 us
  starting transfers between devices: 15.9 us -> 34 us
  between operations: 14.4 us -> 1.25 us
  matrix products: 8.51 us -> 0 us
    psum x1 -> x0, waiting for transfers between devices: 193 us -> none  [body(): lax.psum((jnp.concatenate([down_part, up_part], axis=1), hot_part, bias_p...]
    scatter-add x3 -> x0, other arithmetic: 65.1 us -> none  [the longest x1 23.9 us: body(): cold_part = jnp.zeros((devices * capacity, emb_width), jnp.float32).at[co...]
    psum x1 -> x0, blocking collectives: 49.5 us -> none  [body(): lax.psum((jnp.concatenate([down_part, up_part], axis=1), hot_part, bias_p...]
    pallas_call x0 -> x11, Pallas kernels: none -> 42.9 us  [the longest x7 35.7 us: call(): pl.pallas_call(kernel, out_shape=outs, in_specs=specs, out_specs=[pl.Bloc...]
    ppermute x0 -> x21, waiting for transfers between devices: none -> 41.8 us  [exchange(): return lax.ppermute(value, 'dev', pairs)]
    gather x3 -> x0, local copies, waits for them, and re-layouts: 39.6 us -> none  [the longest x1 15 us: body(): jnp.take(hot_table, hot_ids, axis=0)]
    ppermute x0 -> x21, starting transfers between devices: none -> 20.5 us  [exchange(): return lax.ppermute(value, 'dev', pairs)]
    all_to_all x3, waiting for transfers between devices: 2.13 us -> 20.9 us  [all_to_all(): return lax.all_to_all(value, 'dev', split_axis=0, concat_axis=0, tiled=True)]
  transfers between devices with their start and end apart: 5 -> 24, of which waited for: 2 -> 13; matrix products, arithmetic and copies ran while one was open for 17% -> 9% of each run, Pallas kernels for 0% -> 15%
where the time goes in v2:
time: 167 us; the launch traced here: 166 us
  waiting for transfers between devices  62.7 us (38%)
  Pallas kernels  42.9 us (26%)
  starting transfers between devices  34 us (20%)
  other arithmetic  13.3 us (8%)
  local copies, waits for them, and re-layouts  12.4 us (7%)
    ppermute x21, waiting for transfers between devices, exchange(): return lax.ppermute(value, 'dev', pairs)  41.8 us
    pallas_call x7, Pallas kernels, call(): pl.pallas_call(kernel, out_shape=outs, in_specs=specs, out_specs=[pl.Bloc...  35.7 us
    all_to_all x3, waiting for transfers between devices, all_to_all(): return lax.all_to_all(value, 'dev', split_axis=0, concat_axis=0, tiled=True)  20.9 us
    ppermute x21, starting transfers between devices, exchange(): return lax.ppermute(value, 'dev', pairs)  20.5 us
    all_to_all x3, starting transfers between devices, all_to_all(): return lax.all_to_all(value, 'dev', split_axis=0, concat_axis=0, tiled=True)  13.5 us
    unnamed x36, local copies, waits for them, and re-layouts  10.4 us
    pallas_call x4, Pallas kernels, place(): pl.pallas_call(functools.partial(place_kernel, dims, tuple(plan)), out_sh...  7.23 us
    another operation x7, other arithmetic  6.44 us
  transfers between devices with their start and end apart: 24, of which 13 were waited for; matrix products, arithmetic and copies ran while one was open for 9% of the time, Pallas kernels for 15%

profile of v2, /device:TPU:0, one launch (start us, length us, event | category | flops | bytes accessed | tf_op | source)
XLA Modules:
  0.0 166.5 jit_solution(13310903886559042809)
XLA Ops:
  0.6 7.3 %all-to-all-start = ((s32[32,1,96]{2,1,0:T(1,128)}), s32[32,1,96]{2,1,0:T(1,128)S(1)}, u32[]{:S(2)}, u32[]{:S(2)}) async-start(s32[32,1,96]{2,1,0:T(1,128)} %bitcast.213), calls=%async_computation | async-start | bytes 32768 | tf_op jit(solution)/shard_map/all_to_all | solution.py:463
  10.9 4.1 %all-to-all-done.req_ref = s32[32,1,96]{2,1,0:T(1,128)S(1)} async-done(((s32[32,1,96]{2,1,0:T(1,128)}), s32[32,1,96]{2,1,0:T(1,128)S(1)}, u32[]{:S(2)}, u32[]{:S(2)}) %all-to-all-start) | async-done | bytes 12320 | tf_op jit(solution)/shard_map/all_to_all | solution.py:463
  15.0 3.4 %owner_pick.1 = bf16[3072,128]{1,0:T(8,128)(2,1)} custom-call(s32[32,1,96]{2,1,0:T(1,128)S(1)} %all-to-all-done.req_ref, bf16[512,512]{1,0:T(8,128)(2,1)S(1)} %fold_table.1.folded_ref), custom_call_target="tpu_custom_call" | custom-call | flops 3221225472 | bytes 1323008 | tf_op jit(solution)/shard_map/owner_pick/pallas_call | solution.py:40
  18.4 2.8 %all-to-all-start.1 = ((bf16[32,96,128]{2,1,0:T(8,128)(2,1)}), bf16[32,96,128]{2,1,0:T(8,128)(2,1)S(1)}, u32[]{:S(2)}, u32[]{:S(2)}) async-start(bf16[32,96,128]{2,1,0:T(8,128)(2,1)} %bitcast.5), calls=%async_computation.1 | async-start | bytes 1572864 | tf_op jit(solution)/shard_map/all_to_all | solution.py:463
  21.3 2.5 %hot_pick.1.hot_hbm = bf16[256,2048]{1,0:T(8,128)(2,1)S(1)} custom-call(s32[256,16]{1,0:T(8,128)S(1)} %copy.29.ids_ref, s32[256,16]{1,0:T(8,128)S(1)} %copy.31.slot_ref, bf16[2048,128]{1,0:T(8,128)(2,1)S(1)} %copy-done.6), custom_call_target="tpu_custom_call" | custom-call | flops 42949672960 | bytes 1605632 | tf_op jit(solution)/shard_map/hot_pick/pallas_call | solution.py:40
  24.9 16.8 %all-to-all-done.1 = bf16[32,96,128]{2,1,0:T(8,128)(2,1)S(1)} async-done(((bf16[32,96,128]{2,1,0:T(8,128)(2,1)}), bf16[32,96,128]{2,1,0:T(8,128)(2,1)S(1)}, u32[]{:S(2)}, u32[]{:S(2)}) %all-to-all-start.1) | async-done | bytes 786464 | tf_op jit(solution)/shard_map/all_to_all | solution.py:463
  41.7 12.4 %forward.1 = (f32[16,128]{1,0:T(8,128)S(1)}, bf16[2,2,4,64,512]{4,3,2,1,0:T(8,128)(2,1)S(1)}, bf16[2,2,4,64,512]{4,3,2,1,0:T(8,128)(2,1)}, bf16[2,2,4,64,512]{4,...) custom-call(s32[4]{0:T(128)S(1)} %pad_add_fusion.digits_ref, ...), custom_call_target="tpu_custom_call" | custom-call | flops 6442450944 | bytes 12353552 | tf_op jit(solution)/shard_map/forward/pallas_call | solution.py:40
  57.9 4.9 %hot_sums.1 = (bf16[2,2,4,64,128]{4,3,2,1,0:T(8,128)(2,1)S(1)}, bf16[2,2,4,64,128]{4,3,2,1,0:T(8,128)(2,1)S(1)}) custom-call(s32[4]{0:T(128)S(1)} %pad_add_fusion.digits_ref, s32[256,16]{1,0:T(8,128)S(1)} %copy.32.id_ref, s32[16,256]{1,0:T(8,128)S(1)} %bitcast.209, bf16[256,2048]{1,0:T(8,128)(2,1)S(1)} %copy-done.9), custom_call_target="tpu_custom_call" | custom-call | flops 4294967296 | bytes 1605648 | tf_op jit(solution)/shard_map/hot_sums/pallas_call | solution.py:40
  70.8 6.4 %cold_sums.1 = bf16[32,112,128]{2,1,0:T(8,128)(2,1)} custom-call(s32[256,16]{1,0:T(8,128)S(1)} %copy.31.slot_ref, s32[16,256]{1,0:T(8,128)S(1)} %bitcast.208, bf16[256,2048]{1,0:T(8,128)(2,1)S(1)} %copy-done.9, f32[16,128]{1,0:T(8,128)S(1)} %get-tuple-element.52.bias_ref), custom_call_target="tpu_custom_call" | custom-call | flops 6442450944 | bytes 2007040 | tf_op jit(solution)/shard_map/cold_sums/pallas_call | solution.py:40
  77.2 3.4 %all-to-all-start.2 = ((bf16[32,112,128]{2,1,0:T(8,128)(2,1)}), bf16[32,112,128]{2,1,0:T(8,128)(2,1)}, u32[]{:S(2)}, u32[]{:S(2)}) async-start(bf16[32,112,128]{2,1,0:T(8,128)(2,1)} %cold_sums.1), calls=%async_computation.2 | async-start | bytes 1835008 | tf_op jit(solution)/shard_map/all_to_all | solution.py:463
  81.9 1.8 %fusion.2 = bf16[4,64,512]{2,1,0:T(8,128)(2,1)} fusion(bf16[2,4,64,512]{3,2,1,0:T(8,128)(2,1)} %collective-permute-done.5, bf16[2,2,4,64,512]{4,3,2,1,0:T(8,128)(2,1)} %copy-done.11, bf16[2,2,4,64,512]{4,3,2,1,0:T(8,128)(2,1)S(1)} %get-tuple-element.47), kind=kLoop, calls=%fused_computation.8 | loop fusion | flops 786432 | bytes 1048576 | tf_op jit(solution)/shard_map/convert_element_type | solution.py:556
  85.2 5.9 %collective-permute-done.3 = bf16[2,4,64,640]{3,2,1,0:T(8,128)(2,1)} collective-permute-done((bf16[2,4,64,640]{3,2,1,0:T(8,128)(2,1)}, bf16[2,4,64,640]{3,2,1,0:T(8,128)(2,1)}, u32[]{:S(2)}, u32[]{:S(2)}) %collective-permute-start.3) | collective-permute-done | bytes 655392 | tf_op jit(solution)/shard_map/ppermute | solution.py:457
  94.5 5.9 %collective-permute-done.6 = bf16[4,64,512]{2,1,0:T(8,128)(2,1)} collective-permute-done((bf16[4,64,512]{2,1,0:T(8,128)(2,1)}, bf16[4,64,512]{2,1,0:T(8,128)(2,1)}, u32[]{:S(2)}, u32[]{:S(2)}) %collective-permute-start.6) | collective-permute-done | bytes 262176 | tf_op jit(solution)/shard_map/ppermute | solution.py:457
  105.0 2.0 %collective-permute-start.8 = (bf16[64,1152]{1,0:T(8,128)(2,1)S(1)}, bf16[64,1152]{1,0:T(8,128)(2,1)S(1)}, u32[]{:S(2)}, u32[]{:S(2)}) collective-permute-start(bf16[64,1152]{1,0:T(8,128)(2,1)S(1)} %pad_maximum_fusion.7), channel_id=1, source_target_pairs={{0,16},{1,17},{2,18},{3,19},{4,20},{5,21},{6,22},{7,23},{8,24},{9,... | collective-permute-start | bytes 442376 | tf_op jit(solution)/shard_map/ppermute | solution.py:457
  107.0 2.1 %collective-permute-start.9 = (bf16[64,1152]{1,0:T(8,128)(2,1)S(1)}, bf16[64,1152]{1,0:T(8,128)(2,1)S(1)}, u32[]{:S(2)}, u32[]{:S(2)}) collective-permute-start(bf16[64,1152]{1,0:T(8,128)(2,1)S(1)} %pad_maximum_fusion.8), channel_id=1, source_target_pairs={{0,24},{1,25},{2,26},{3,27},{4,28},{5,29},{6,30},{7,31},{8,0},{9,1... | collective-permute-start | bytes 442376 | tf_op jit(solution)/shard_map/ppermute | solution.py:457
  112.8 6.0 %cold_adam.1 = (f32[2048,128]{1,0:T(8,128)}, f32[2048,128]{1,0:T(8,128)}, f32[2048,128]{1,0:T(8,128)}) custom-call(s32[24,128]{1,0:T(8,128)S(1)} %reshape.155.req_ref, bf16[3072,128]{1,0:T(8,128)(2,1)S(1)} %bitcast.207, f32[2048,128]{1,0:T(8,128)S(1)} %copy-done.1, f32[2048,128]{1,0:T(8,128)S(1)} %copy-done.3, f32[2048,128]{1,0:T(8,128)S(1)} %copy-done.4), custom_call_target="tpu_custom_call" | custom-call | flops 3221225472 | bytes 7090176 | tf_op jit(solution)/shard_map/cold_adam/pallas_call | solution.py:40
  124.8 2.4 %collective-permute-done.12 = bf16[64,1152]{1,0:T(8,128)(2,1)S(1)} collective-permute-done((bf16[64,1152]{1,0:T(8,128)(2,1)S(1)}, bf16[64,1152]{1,0:T(8,128)(2,1)S(1)}, u32[]{:S(2)}, u32[]{:S(2)}) %collective-permute-start.12) | collective-permute-done | bytes 147488 | tf_op jit(solution)/shard_map/ppermute | solution.py:457
  127.2 8.6 %collective-permute-done.11 = bf16[64,1152]{1,0:T(8,128)(2,1)S(1)} collective-permute-done((bf16[64,1152]{1,0:T(8,128)(2,1)S(1)}, bf16[64,1152]{1,0:T(8,128)(2,1)S(1)}, u32[]{:S(2)}, u32[]{:S(2)}) %collective-permute-start.11) | collective-permute-done | bytes 147488 | tf_op jit(solution)/shard_map/ppermute | solution.py:457
  136.4 2.5 %collective-permute-start.15 = (bf16[4,64,512]{2,1,0:T(8,128)(2,1)S(1)}, bf16[4,64,512]{2,1,0:T(8,128)(2,1)S(1)}, u32[]{:S(2)}, u32[]{:S(2)}) collective-permute-start(bf16[4,64,512]{2,1,0:T(8,128)(2,1)S(1)} %get-tuple-element.94), channel_id=1, source_target_pairs={{0,2},{1,3},{2,0},{3,1},{4,6},{5,7},{6,4},{7,5},{8,10},{9,11},{10,... | collective-permute-start | bytes 786440 | tf_op jit(solution)/shard_map/ppermute | solution.py:457
  138.8 5.5 %collective-permute-done.13 = bf16[4,64,640]{2,1,0:T(8,128)(2,1)S(1)} collective-permute-done((bf16[4,64,640]{2,1,0:T(8,128)(2,1)S(1)}, bf16[4,64,640]{2,1,0:T(8,128)(2,1)S(1)}, u32[]{:S(2)}, u32[]{:S(2)}) %collective-permute-start.13) | collective-permute-done | bytes 327712 | tf_op jit(solution)/shard_map/ppermute | solution.py:457
  148.0 1.8 %place.4 = (bf16[2048,1024]{1,0:T(8,128)(2,1)}, f32[2048,128]{1,0:T(8,128)}) custom-call(s32[4]{0:T(128)S(1)} %pad_add_fusion.digits_ref, bf16[2,4,64,640]{3,2,1,0:T(8,128)(2,1)S(1)} %pad_maximum_fusion.1.refs_0_, bf16[2,4,64,512]{3,2,1,0:T(8,128)(2,1)S(1)} %pad_maximum_fusion.2.refs_1_), custom_call_target="tpu_custom_call" | custom-call | bytes 4194304 | tf_op jit(solution)/shard_map/place/pallas_call | solution.py:381
  149.8 1.8 %place.5 = (bf16[2048,1024]{1,0:T(8,128)(2,1)}, f32[2048,128]{1,0:T(8,128)}) custom-call(s32[4]{0:T(128)S(1)} %pad_add_fusion.digits_ref, bf16[2,4,64,640]{3,2,1,0:T(8,128)(2,1)S(1)} %collective-permute-done.17.refs_0_, bf16[2,4,64,512]{3,2,1,0:T(8,128)(2,1)S(1)} %collective-permute-done.18.refs_1_, ...), custom_call_target="tpu_custom_call", output_to_operand_aliasing={{0}: (3, {}), {1}: (4, {})} | custom-call | bytes 4194304 | tf_op jit(solution)/shard_map/place/pallas_call | solution.py:381
  151.6 8.8 %collective-permute-done.16.refs_1_ = bf16[2,4,64,512]{3,2,1,0:T(8,128)(2,1)S(1)} collective-permute-done((bf16[2,4,64,512]{3,2,1,0:T(8,128)(2,1)S(1)}, bf16[2,4,64,512]{3,2,1,0:T(8,128)(2,1)S(1)}, u32[]{:S(2)}, u32[]{:S(2)}) %collective-permute-start.16) | collective-permute-done | bytes 524320 | tf_op jit(solution)/shard_map/ppermute | solution.py:457
  164.5 1.8 %place.7 = (bf16[2048,1024]{1,0:T(8,128)(2,1)}, f32[2048,128]{1,0:T(8,128)}) custom-call(s32[4]{0:T(128)S(1)} %pad_add_fusion.digits_ref, bf16[2,4,64,640]{3,2,1,0:T(8,128)(2,1)S(1)} %collective-permute-done.19.refs_0_, bf16[2,4,64,512]{3,2,1,0:T(8,128)(2,1)S(1)} %collective-permute-done.20.refs_1_, ...), custom_call_target="tpu_custom_call", output_to_operand_aliasing={{0}: (3, {}), {1}: (4, {})} | custom-call | bytes 4194304 | tf_op jit(solution)/shard_map/place/pallas_call | solution.py:381
  (110 shorter events, 44.4 us)
Async XLA Ops:
  0.6 14.4 %all-to-all-start = ((s32[32,1,96]{2,1,0:T(1,128)}), s32[32,1,96]{2,1,0:T(1,128)S(1)}, u32[]{:S(2)}, u32[]{:S(2)}) async-start(s32[32,1,96]{2,1,0:T(1,128)} %bitcast.213), calls=%async_computation | async-start | bytes 32768 | tf_op jit(solution)/shard_map/all_to_all | solution.py:463
  18.4 23.2 %all-to-all-start.1 = ((bf16[32,96,128]{2,1,0:T(8,128)(2,1)}), bf16[32,96,128]{2,1,0:T(8,128)(2,1)S(1)}, u32[]{:S(2)}, u32[]{:S(2)}) async-start(bf16[32,96,128]{2,1,0:T(8,128)(2,1)} %bitcast.5), calls=%async_computation.1 | async-start | bytes 1572864 | tf_op jit(solution)/shard_map/all_to_all | solution.py:463
  56.0 8.4 %collective-permute-start = (bf16[2,2,4,64,512]{4,3,2,1,0:T(8,128)(2,1)}, bf16[2,2,4,64,512]{4,3,2,1,0:T(8,128)(2,1)}, u32[]{:S(2)}, u32[]{:S(2)}) collective-permute-start(bf16[2,2,4,64,512]{4,3,2,1,0:T(8,128)(2,1)} %get-tuple-element.43), channel_id=1, source_target_pairs={{0,1},{1,0},{2,3},{3,2},{4,5},{5,4},{6,7},{7,6},{8,9},{9,8},{10,11... | collective-permute-start | bytes 3145736 | tf_op jit(solution)/shard_map/ppermute | solution.py:457
  56.2 10.5 %collective-permute-start.2 = (bf16[2,2,4,64,512]{4,3,2,1,0:T(8,128)(2,1)}, bf16[2,2,4,64,512]{4,3,2,1,0:T(8,128)(2,1)S(1)}, u32[]{:S(2)}, u32[]{:S(2)}) collective-permute-start(bf16[2,2,4,64,512]{4,3,2,1,0:T(8,128)(2,1)} %copy-done.5), channel_id=1, source_target_pairs={{0,1},{1,0},{2,3},{3,2},{4,5},{5,4},{6,7},{7,6},{8,9},{9,8},{10,11... | collective-permute-start | bytes 3145736 | tf_op jit(solution)/shard_map/ppermute | solution.py:457
  62.8 1.6 collective-permute-start.1
  67.7 14.1 %collective-permute-start.5 = (bf16[2,4,64,512]{3,2,1,0:T(8,128)(2,1)S(1)}, bf16[2,4,64,512]{3,2,1,0:T(8,128)(2,1)}, u32[]{:S(2)}, u32[]{:S(2)}) collective-permute-start(bf16[2,4,64,512]{3,2,1,0:T(8,128)(2,1)S(1)} %fusion.1), channel_id=1, source_target_pairs={{0,4},{1,5},{2,6},{3,7},{4,0},{5,1},{6,2},{7,3},{8,12},{9,13},{10,... | collective-permute-start | bytes 1572872 | tf_op jit(solution)/shard_map/ppermute | solution.py:457
  69.4 21.7 %collective-permute-start.3 = (bf16[2,4,64,640]{3,2,1,0:T(8,128)(2,1)}, bf16[2,4,64,640]{3,2,1,0:T(8,128)(2,1)}, u32[]{:S(2)}, u32[]{:S(2)}) collective-permute-start(bf16[2,4,64,640]{3,2,1,0:T(8,128)(2,1)} %pad_maximum_fusion), channel_id=1, source_target_pairs={{0,2},{1,3},{2,0},{3,1},{4,6},{5,7},{6,4},{7,5},{8,10},{9,11},{10,... | collective-permute-start | bytes 1966088 | tf_op jit(solution)/shard_map/ppermute | solution.py:457
  77.2 31.9 %all-to-all-start.2 = ((bf16[32,112,128]{2,1,0:T(8,128)(2,1)}), bf16[32,112,128]{2,1,0:T(8,128)(2,1)}, u32[]{:S(2)}, u32[]{:S(2)}) async-start(bf16[32,112,128]{2,1,0:T(8,128)(2,1)} %cold_sums.1), calls=%async_computation.2 | async-start | bytes 1835008 | tf_op jit(solution)/shard_map/all_to_all | solution.py:463
  83.7 16.7 %collective-permute-start.6 = (bf16[4,64,512]{2,1,0:T(8,128)(2,1)}, bf16[4,64,512]{2,1,0:T(8,128)(2,1)}, u32[]{:S(2)}, u32[]{:S(2)}) collective-permute-start(bf16[4,64,512]{2,1,0:T(8,128)(2,1)} %fusion.2), channel_id=1, source_target_pairs={{0,2},{1,3},{2,0},{3,1},{4,6},{5,7},{6,4},{7,5},{8,10},{9,11},{10,... | collective-permute-start | bytes 786440 | tf_op jit(solution)/shard_map/ppermute | solution.py:457
  93.2 8.7 %collective-permute-start.4 = (bf16[4,64,640]{2,1,0:T(8,128)(2,1)S(1)}, bf16[4,64,640]{2,1,0:T(8,128)(2,1)S(1)}, u32[]{:S(2)}, u32[]{:S(2)}) collective-permute-start(bf16[4,64,640]{2,1,0:T(8,128)(2,1)S(1)} %pad_maximum_fusion.3), channel_id=1, source_target_pairs={{0,4},{1,5},{2,6},{3,7},{4,0},{5,1},{6,2},{7,3},{8,12},{9,13},{10,... | collective-permute-start | bytes 983048 | tf_op jit(solution)/shard_map/ppermute | solution.py:457
  104.0 16.3 %collective-permute-start.7 = (bf16[64,1152]{1,0:T(8,128)(2,1)S(1)}, bf16[64,1152]{1,0:T(8,128)(2,1)S(1)}, u32[]{:S(2)}, u32[]{:S(2)}) collective-permute-start(bf16[64,1152]{1,0:T(8,128)(2,1)S(1)} %pad_maximum_fusion.6), channel_id=1, source_target_pairs={{0,8},{1,9},{2,10},{3,11},{4,12},{5,13},{6,14},{7,15},{8,16},{9,17... | collective-permute-start | bytes 442376 | tf_op jit(solution)/shard_map/ppermute | solution.py:457
  105.0 15.3 %collective-permute-start.8 = (bf16[64,1152]{1,0:T(8,128)(2,1)S(1)}, bf16[64,1152]{1,0:T(8,128)(2,1)S(1)}, u32[]{:S(2)}, u32[]{:S(2)}) collective-permute-start(bf16[64,1152]{1,0:T(8,128)(2,1)S(1)} %pad_maximum_fusion.7), channel_id=1, source_target_pairs={{0,16},{1,17},{2,18},{3,19},{4,20},{5,21},{6,22},{7,23},{8,24},{9,... | collective-permute-start | bytes 442376 | tf_op jit(solution)/shard_map/ppermute | solution.py:457
  107.0 13.3 %collective-permute-start.9 = (bf16[64,1152]{1,0:T(8,128)(2,1)S(1)}, bf16[64,1152]{1,0:T(8,128)(2,1)S(1)}, u32[]{:S(2)}, u32[]{:S(2)}) collective-permute-start(bf16[64,1152]{1,0:T(8,128)(2,1)S(1)} %pad_maximum_fusion.8), channel_id=1, source_target_pairs={{0,24},{1,25},{2,26},{3,27},{4,28},{5,29},{6,30},{7,31},{8,0},{9,1... | collective-permute-start | bytes 442376 | tf_op jit(solution)/shard_map/ppermute | solution.py:457
  121.5 5.7 %collective-permute-start.12 = (bf16[64,1152]{1,0:T(8,128)(2,1)S(1)}, bf16[64,1152]{1,0:T(8,128)(2,1)S(1)}, u32[]{:S(2)}, u32[]{:S(2)}) collective-permute-start(bf16[64,1152]{1,0:T(8,128)(2,1)S(1)} %pad_maximum_fusion.9), channel_id=1, source_target_pairs={{0,24},{1,25},{2,26},{3,27},{4,28},{5,29},{6,30},{7,31},{8,0},{9,1... | collective-permute-start | bytes 442376 | tf_op jit(solution)/shard_map/ppermute | solution.py:457
  122.2 13.6 %collective-permute-start.11 = (bf16[64,1152]{1,0:T(8,128)(2,1)S(1)}, bf16[64,1152]{1,0:T(8,128)(2,1)S(1)}, u32[]{:S(2)}, u32[]{:S(2)}) collective-permute-start(bf16[64,1152]{1,0:T(8,128)(2,1)S(1)} %pad_maximum_fusion.9), channel_id=1, source_target_pairs={{0,16},{1,17},{2,18},{3,19},{4,20},{5,21},{6,22},{7,23},{8,24},{9,... | collective-permute-start | bytes 442376 | tf_op jit(solution)/shard_map/ppermute | solution.py:457
  123.2 12.6 %collective-permute-start.10 = (bf16[64,1152]{1,0:T(8,128)(2,1)S(1)}, bf16[64,1152]{1,0:T(8,128)(2,1)S(1)}, u32[]{:S(2)}, u32[]{:S(2)}) collective-permute-start(bf16[64,1152]{1,0:T(8,128)(2,1)S(1)} %pad_maximum_fusion.9), channel_id=1, source_target_pairs={{0,8},{1,9},{2,10},{3,11},{4,12},{5,13},{6,14},{7,15},{8,16},{9,17... | collective-permute-start | bytes 442376 | tf_op jit(solution)/shard_map/ppermute | solution.py:457
  135.9 8.4 %collective-permute-start.13 = (bf16[4,64,640]{2,1,0:T(8,128)(2,1)S(1)}, bf16[4,64,640]{2,1,0:T(8,128)(2,1)S(1)}, u32[]{:S(2)}, u32[]{:S(2)}) collective-permute-start(bf16[4,64,640]{2,1,0:T(8,128)(2,1)S(1)} %get-tuple-element.92), channel_id=1, source_target_pairs={{0,4},{1,5},{2,6},{3,7},{4,0},{5,1},{6,2},{7,3},{8,12},{9,13},{10,... | collective-permute-start | bytes 983048 | tf_op jit(solution)/shard_map/ppermute | solution.py:457
  136.4 9.6 %collective-permute-start.15 = (bf16[4,64,512]{2,1,0:T(8,128)(2,1)S(1)}, bf16[4,64,512]{2,1,0:T(8,128)(2,1)S(1)}, u32[]{:S(2)}, u32[]{:S(2)}) collective-permute-start(bf16[4,64,512]{2,1,0:T(8,128)(2,1)S(1)} %get-tuple-element.94), channel_id=1, source_target_pairs={{0,2},{1,3},{2,0},{3,1},{4,6},{5,7},{6,4},{7,5},{8,10},{9,11},{10,... | collective-permute-start | bytes 786440 | tf_op jit(solution)/shard_map/ppermute | solution.py:457
  144.4 5.4 %collective-permute-start.17 = (bf16[2,4,64,640]{3,2,1,0:T(8,128)(2,1)S(1)}, bf16[2,4,64,640]{3,2,1,0:T(8,128)(2,1)S(1)}, u32[]{:S(2)}, u32[]{:S(2)}) collective-permute-start(bf16[2,4,64,640]{3,2,1,0:T(8,128)(2,1)S(1)} %pad_maximum_fusion.1.refs_0_), channel_id=1, source_target_pairs={{0,1},{1,0},{2,3},{3,2},{4,5},{5,4},{6,7},{7,6},{8,9},{9,8},{10,11... | collective-permute-start | bytes 1966088 | tf_op jit(solution)/shard_map/ppermute | solution.py:457
  144.5 17.1 %collective-permute-start.14 = (bf16[2,4,64,640]{3,2,1,0:T(8,128)(2,1)S(1)}, bf16[2,4,64,640]{3,2,1,0:T(8,128)(2,1)S(1)}, u32[]{:S(2)}, u32[]{:S(2)}) collective-permute-start(bf16[2,4,64,640]{3,2,1,0:T(8,128)(2,1)S(1)} %pad_maximum_fusion.1.refs_0_), channel_id=1, source_target_pairs={{0,2},{1,3},{2,0},{3,1},{4,6},{5,7},{6,4},{7,5},{8,10},{9,11},{10,... | collective-permute-start | bytes 1966088 | tf_op jit(solution)/shard_map/ppermute | solution.py:457
  146.0 3.8 %collective-permute-start.18 = (bf16[2,4,64,512]{3,2,1,0:T(8,128)(2,1)S(1)}, bf16[2,4,64,512]{3,2,1,0:T(8,128)(2,1)S(1)}, u32[]{:S(2)}, u32[]{:S(2)}) collective-permute-start(bf16[2,4,64,512]{3,2,1,0:T(8,128)(2,1)S(1)} %pad_maximum_fusion.2.refs_1_), channel_id=1, source_target_pairs={{0,1},{1,0},{2,3},{3,2},{4,5},{5,4},{6,7},{7,6},{8,9},{9,8},{10,11... | collective-permute-start | bytes 1572872 | tf_op jit(solution)/shard_map/ppermute | solution.py:457
  146.2 14.2 %collective-permute-start.16 = (bf16[2,4,64,512]{3,2,1,0:T(8,128)(2,1)S(1)}, bf16[2,4,64,512]{3,2,1,0:T(8,128)(2,1)S(1)}, u32[]{:S(2)}, u32[]{:S(2)}) collective-permute-start(bf16[2,4,64,512]{3,2,1,0:T(8,128)(2,1)S(1)} %pad_maximum_fusion.2.refs_1_), channel_id=1, source_target_pairs={{0,4},{1,5},{2,6},{3,7},{4,0},{5,1},{6,2},{7,3},{8,12},{9,13},{10,... | collective-permute-start | bytes 1572872 | tf_op jit(solution)/shard_map/ppermute | solution.py:457
  161.6 2.9 %collective-permute-start.19 = (bf16[2,4,64,640]{3,2,1,0:T(8,128)(2,1)S(1)}, bf16[2,4,64,640]{3,2,1,0:T(8,128)(2,1)S(1)}, u32[]{:S(2)}, u32[]{:S(2)}) collective-permute-start(bf16[2,4,64,640]{3,2,1,0:T(8,128)(2,1)S(1)} %collective-permute-done.14.refs_0_), channel_id=1, source_target_pairs={{0,1},{1,0},{2,3},{3,2},{4,5},{5,4},{6,7},{7,6},{8,9},{9,8},{10,11... | collective-permute-start | bytes 1966088 | tf_op jit(solution)/shard_map/ppermute | solution.py:457
  161.6 2.8 %collective-permute-start.20 = (bf16[2,4,64,512]{3,2,1,0:T(8,128)(2,1)S(1)}, bf16[2,4,64,512]{3,2,1,0:T(8,128)(2,1)S(1)}, u32[]{:S(2)}, u32[]{:S(2)}) collective-permute-start(bf16[2,4,64,512]{3,2,1,0:T(8,128)(2,1)S(1)} %collective-permute-done.16.refs_1_), channel_id=1, source_target_pairs={{0,1},{1,0},{2,3},{3,2},{4,5},{5,4},{6,7},{7,6},{8,9},{9,8},{10,11... | collective-permute-start | bytes 1572872 | tf_op jit(solution)/shard_map/ppermute | solution.py:457
  (17 other events, 127.7 us)

commit v3 on v2

--- a/solution.py
+++ b/solution.py
@@ -85,6 +85,10 @@
     return out
 
 
+def stacked(columns, first, count):
+    return jnp.concatenate([columns[:, f : f + 1] for f in range(first, first + count)], axis=0)
+
+
 def columns_of(lists):
     turned = jnp.transpose(lists)
     return jnp.concatenate([turned[:, i : i + 1] for i in range(lists.shape[0])], axis=0)
@@ -109,7 +113,7 @@
     slots, width = out_ref.shape
     column = columns_of(req_ref[:, 0, :])
     block, place = fold(column, rows)
-    step = 512 if slots % 512 == 0 else slots
+    step = 1024 if slots % 1024 == 0 else slots
     for first in range(0, slots, step):
         at = slice(first, first + step)
         out_ref[at, :] = pick_rows(block[at], place[at], folded_ref, width).astype(bf16)
@@ -143,7 +147,7 @@
 
 
 def outer_sums(digits_ref, dims, order, left, right, keep_ref, send_ref):
-    block = max(2 * keep_ref.shape[-2], 256)
+    block = max(2 * keep_ref.shape[-2], min(left.shape[1], 1024))
     for first in range(0, left.shape[1], block):
         sums = lax.dot_general(
             left[:, first : first + block],
@@ -203,17 +207,22 @@
     slots, width = fetched_ref.shape
     lay_beside(fetched_ref[...], folded)
     block, place = fold(slot_ref[...], slots)
-    for f in range(fields):
-        cols = slice(f * width, (f + 1) * width)
-        cold = pick_rows(block[:, f : f + 1], place[:, f : f + 1], folded, width)
-        if f == 0:
+    group = 4 if fields % 4 == 0 else 1
+    for first in range(0, fields, group):
+        cold = pick_rows(
+            stacked(block, first, group), stacked(place, first, group), folded, width
+        )
+        if first == 0:
             copies[0].wait()
             copies[1].wait()
-        picked = cold + hot_ref[:, cols].astype(f32)
-        x0[:, cols] = picked.astype(bf16)
-        mix = (cot_ref[:, cols].astype(f32) * picked).astype(bf16)
-        gm[:, cols] = mix
-        bias_ref[f : f + 1, :] = jnp.sum(mix.astype(f32), axis=0, keepdims=True)
+        for i in range(group):
+            f = first + i
+            cols = slice(f * width, (f + 1) * width)
+            picked = cold[i * samples : (i + 1) * samples] + hot_ref[:, cols].astype(f32)
+            x0[:, cols] = picked.astype(bf16)
+            mix = (cot_ref[:, cols].astype(f32) * picked).astype(bf16)
+            gm[:, cols] = mix
+            bias_ref[f : f + 1, :] = jnp.sum(mix.astype(f32), axis=0, keepdims=True)
     copies[2].wait()
     grad_latent = lax.dot_general(
         gm[...], up_ref[...], (((1,), (1,)), ((), ())), preferred_element_type=f32
@@ -224,9 +233,8 @@
     latent = jnp.dot(x0[...], down_ref[...], preferred_element_type=f32).astype(bf16)
     outer_sums(digits_ref, dims, order_b, gm, latent, keep_b, send_b)
     done += start_copies(sems, ((send_b, send_b_hbm), (keep_b, keep_b_hbm)), 6)
-    step = 4 if fields % 4 == 0 else fields
-    for f in range(fields):
-        cols = slice(f * width, (f + 1) * width)
+    for first in range(0, fields, group):
+        cols = slice(first * width, (first + group) * width)
         mixing = (
             jnp.dot(latent, up_ref[:, cols], preferred_element_type=f32) + cross_bias_ref[:, cols]
         )
@@ -235,11 +243,9 @@
         )
         grad = cot_ref[:, cols].astype(f32) * (mixing + 1.0) + back
         grad_ref[:, cols] = grad.astype(bf16)
-        if (f + 1) % step == 0:
-            part = slice((f + 1 - step) * width, (f + 1) * width)
-            done += start_copies(
-                sems, ((grad_ref.at[:, part], grad_hbm.at[:, part]),), 8 + f // step
-            )
+        done += start_copies(
+            sems, ((grad_ref.at[:, cols], grad_hbm.at[:, cols]),), 8 + first // group
+        )
     for copy in done:
         copy.wait()
 
@@ -249,7 +255,7 @@
     unused, place = fold(lists, total)
     part = total // ways(total)
     width = grads.shape[1] // ways(total)
-    step = 256 if part % 256 == 0 else part
+    step = part
     for first in range(0, part, step):
         spot = lax.broadcasted_iota(jnp.int32, (step, samples), 0) + first
         hot = jnp.concatenate(
@@ -323,7 +329,7 @@
         spread[:, j * width : (j + 1) * width] = jnp.where(block == j, returned, 0.0).astype(bf16)
     unused, place = fold(req, rows)
     part = rows // ways(rows)
-    step = 256 if part % 256 == 0 else part
+    step = part
     for first in range(0, part, step):
         spot = lax.broadcasted_iota(jnp.int32, (step, LANES), 0) + first
         hot = jnp.concatenate(

time: 167 us -> 165 us (0.988)
  Pallas kernels: 42.9 us -> 38.3 us
  waiting for transfers between devices: 62.7 us -> 64.5 us
    pallas_call x7, Pallas kernels: 35.7 us -> 31 us  [call(): pl.pallas_call(kernel, out_shape=outs, in_specs=specs, out_specs=[pl.Bloc...]
    ppermute x21, waiting for transfers between devices: 41.8 us -> 43.5 us  [exchange(): return lax.ppermute(value, 'dev', pairs)]
  transfers between devices with their start and end apart: 24 -> 24, of which waited for: 13 -> 12; matrix products, arithmetic and copies ran while one was open for 9% -> 9% of each run, Pallas kernels for 15% -> 13%
where the time goes in v3:
time: 165 us; the launch traced here: 164 us
  waiting for transfers between devices  64.5 us (39%)
  Pallas kernels  38.3 us (23%)
  starting transfers between devices  34.7 us (21%)
  other arithmetic  13.3 us (8%)
  local copies, waits for them, and re-layouts  12.4 us (8%)
    ppermute x21, waiting for transfers between devices, exchange(): return lax.ppermute(value, 'dev', pairs)  43.5 us
    pallas_call x7, Pallas kernels, call(): pl.pallas_call(kernel, out_shape=outs, in_specs=specs, out_specs=[pl.Bloc...  31 us
    ppermute x21, starting transfers between devices, exchange(): return lax.ppermute(value, 'dev', pairs)  21.2 us
    all_to_all x3, waiting for transfers between devices, all_to_all(): return lax.all_to_all(value, 'dev', split_axis=0, concat_axis=0, tiled=True)  20.9 us
    all_to_all x3, starting transfers between devices, all_to_all(): return lax.all_to_all(value, 'dev', split_axis=0, concat_axis=0, tiled=True)  13.5 us
    unnamed x36, local copies, waits for them, and re-layouts  10.4 us
    pallas_call x4, Pallas kernels, place(): pl.pallas_call(functools.partial(place_kernel, dims, tuple(plan)), out_sh...  7.23 us
    another operation x7, other arithmetic  6.44 us
  transfers between devices with their start and end apart: 24, of which 12 were waited for; matrix products, arithmetic and copies ran while one was open for 9% of the time, Pallas kernels for 13%

profile of v3, /device:TPU:0, one launch (start us, length us, event | category | flops | bytes accessed | tf_op | source)
XLA Modules:
  0.0 164.4 jit_solution(208796875022742644)
XLA Ops:
  0.6 7.3 %all-to-all-start = ((s32[32,1,96]{2,1,0:T(1,128)}), s32[32,1,96]{2,1,0:T(1,128)S(1)}, u32[]{:S(2)}, u32[]{:S(2)}) async-start(s32[32,1,96]{2,1,0:T(1,128)} %bitcast.213), calls=%async_computation | async-start | bytes 32768 | tf_op jit(solution)/shard_map/all_to_all | solution.py:469
  10.9 4.1 %all-to-all-done.req_ref = s32[32,1,96]{2,1,0:T(1,128)S(1)} async-done(((s32[32,1,96]{2,1,0:T(1,128)}), s32[32,1,96]{2,1,0:T(1,128)S(1)}, u32[]{:S(2)}, u32[]{:S(2)}) %all-to-all-start) | async-done | bytes 12320 | tf_op jit(solution)/shard_map/all_to_all | solution.py:469
  15.0 3.4 %owner_pick.1 = bf16[3072,128]{1,0:T(8,128)(2,1)} custom-call(s32[32,1,96]{2,1,0:T(1,128)S(1)} %all-to-all-done.req_ref, bf16[512,512]{1,0:T(8,128)(2,1)S(1)} %fold_table.1.folded_ref), custom_call_target="tpu_custom_call" | custom-call | flops 3221225472 | bytes 1323008 | tf_op jit(solution)/shard_map/owner_pick/pallas_call | solution.py:40
  18.4 2.8 %all-to-all-start.1 = ((bf16[32,96,128]{2,1,0:T(8,128)(2,1)}), bf16[32,96,128]{2,1,0:T(8,128)(2,1)S(1)}, u32[]{:S(2)}, u32[]{:S(2)}) async-start(bf16[32,96,128]{2,1,0:T(8,128)(2,1)} %bitcast.5), calls=%async_computation.1 | async-start | bytes 1572864 | tf_op jit(solution)/shard_map/all_to_all | solution.py:469
  21.2 2.5 %hot_pick.1.hot_hbm = bf16[256,2048]{1,0:T(8,128)(2,1)S(1)} custom-call(s32[256,16]{1,0:T(8,128)S(1)} %copy.29.ids_ref, s32[256,16]{1,0:T(8,128)S(1)} %copy.31.slot_ref, bf16[2048,128]{1,0:T(8,128)(2,1)S(1)} %copy-done.6), custom_call_target="tpu_custom_call" | custom-call | flops 42949672960 | bytes 1605632 | tf_op jit(solution)/shard_map/hot_pick/pallas_call | solution.py:40
  24.8 16.8 %all-to-all-done.1 = bf16[32,96,128]{2,1,0:T(8,128)(2,1)S(1)} async-done(((bf16[32,96,128]{2,1,0:T(8,128)(2,1)}), bf16[32,96,128]{2,1,0:T(8,128)(2,1)S(1)}, u32[]{:S(2)}, u32[]{:S(2)}) %all-to-all-start.1) | async-done | bytes 786464 | tf_op jit(solution)/shard_map/all_to_all | solution.py:469
  41.6 11.3 %forward.1 = (f32[16,128]{1,0:T(8,128)S(1)}, bf16[2,2,4,64,512]{4,3,2,1,0:T(8,128)(2,1)S(1)}, bf16[2,2,4,64,512]{4,3,2,1,0:T(8,128)(2,1)}, bf16[2,2,4,64,512]{4,...) custom-call(s32[4]{0:T(128)S(1)} %pad_add_fusion.digits_ref, ...), custom_call_target="tpu_custom_call" | custom-call | flops 6442450944 | bytes 12353552 | tf_op jit(solution)/shard_map/forward/pallas_call | solution.py:40
  56.8 3.6 %hot_sums.1 = (bf16[2,2,4,64,128]{4,3,2,1,0:T(8,128)(2,1)S(1)}, bf16[2,2,4,64,128]{4,3,2,1,0:T(8,128)(2,1)S(1)}) custom-call(s32[4]{0:T(128)S(1)} %pad_add_fusion.digits_ref, s32[256,16]{1,0:T(8,128)S(1)} %copy.32.id_ref, s32[16,256]{1,0:T(8,128)S(1)} %bitcast.209, bf16[256,2048]{1,0:T(8,128)(2,1)S(1)} %copy-done.9), custom_call_target="tpu_custom_call" | custom-call | flops 4294967296 | bytes 1605648 | tf_op jit(solution)/shard_map/hot_sums/pallas_call | solution.py:40
  68.4 4.7 %cold_sums.1 = bf16[32,112,128]{2,1,0:T(8,128)(2,1)} custom-call(s32[256,16]{1,0:T(8,128)S(1)} %copy.31.slot_ref, s32[16,256]{1,0:T(8,128)S(1)} %bitcast.208, bf16[256,2048]{1,0:T(8,128)(2,1)S(1)} %copy-done.9, f32[16,128]{1,0:T(8,128)S(1)} %get-tuple-element.52.bias_ref), custom_call_target="tpu_custom_call" | custom-call | flops 6442450944 | bytes 2007040 | tf_op jit(solution)/shard_map/cold_sums/pallas_call | solution.py:40
  73.1 3.4 %all-to-all-start.2 = ((bf16[32,112,128]{2,1,0:T(8,128)(2,1)}), bf16[32,112,128]{2,1,0:T(8,128)(2,1)}, u32[]{:S(2)}, u32[]{:S(2)}) async-start(bf16[32,112,128]{2,1,0:T(8,128)(2,1)} %cold_sums.1), calls=%async_computation.2 | async-start | bytes 1835008 | tf_op jit(solution)/shard_map/all_to_all | solution.py:469
  76.5 3.3 %collective-permute-done.5 = bf16[2,4,64,512]{3,2,1,0:T(8,128)(2,1)} collective-permute-done((bf16[2,4,64,512]{3,2,1,0:T(8,128)(2,1)S(1)}, bf16[2,4,64,512]{3,2,1,0:T(8,128)(2,1)}, u32[]{:S(2)}, u32[]{:S(2)}) %collective-permute-start.5) | collective-permute-done | bytes 524320 | tf_op jit(solution)/shard_map/ppermute | solution.py:463
  79.7 1.8 %fusion.2 = bf16[4,64,512]{2,1,0:T(8,128)(2,1)} fusion(bf16[2,4,64,512]{3,2,1,0:T(8,128)(2,1)} %collective-permute-done.5, bf16[2,2,4,64,512]{4,3,2,1,0:T(8,128)(2,1)} %copy-done.11, bf16[2,2,4,64,512]{4,3,2,1,0:T(8,128)(2,1)S(1)} %get-tuple-element.47), kind=kLoop, calls=%fused_computation.8 | loop fusion | flops 786432 | bytes 1048576 | tf_op jit(solution)/shard_map/convert_element_type | solution.py:562
  81.6 2.6 %collective-permute-start.6 = (bf16[4,64,512]{2,1,0:T(8,128)(2,1)}, bf16[4,64,512]{2,1,0:T(8,128)(2,1)}, u32[]{:S(2)}, u32[]{:S(2)}) collective-permute-start(bf16[4,64,512]{2,1,0:T(8,128)(2,1)} %fusion.2), channel_id=1, source_target_pairs={{0,2},{1,3},{2,0},{3,1},{4,6},{5,7},{6,4},{7,5},{8,10},{9,11},{10,... | collective-permute-start | bytes 786440 | tf_op jit(solution)/shard_map/ppermute | solution.py:463
  84.2 5.6 %collective-permute-done.3 = bf16[2,4,64,640]{3,2,1,0:T(8,128)(2,1)} collective-permute-done((bf16[2,4,64,640]{3,2,1,0:T(8,128)(2,1)}, bf16[2,4,64,640]{3,2,1,0:T(8,128)(2,1)}, u32[]{:S(2)}, u32[]{:S(2)}) %collective-permute-start.3) | collective-permute-done | bytes 655392 | tf_op jit(solution)/shard_map/ppermute | solution.py:463
  93.4 5.6 %collective-permute-done.6 = bf16[4,64,512]{2,1,0:T(8,128)(2,1)} collective-permute-done((bf16[4,64,512]{2,1,0:T(8,128)(2,1)}, bf16[4,64,512]{2,1,0:T(8,128)(2,1)}, u32[]{:S(2)}, u32[]{:S(2)}) %collective-permute-start.6) | collective-permute-done | bytes 262176 | tf_op jit(solution)/shard_map/ppermute | solution.py:463
  104.6 2.7 %collective-permute-start.9 = (bf16[64,1152]{1,0:T(8,128)(2,1)S(1)}, bf16[64,1152]{1,0:T(8,128)(2,1)S(1)}, u32[]{:S(2)}, u32[]{:S(2)}) collective-permute-start(bf16[64,1152]{1,0:T(8,128)(2,1)S(1)} %pad_maximum_fusion.8), channel_id=1, source_target_pairs={{0,24},{1,25},{2,26},{3,27},{4,28},{5,29},{6,30},{7,31},{8,0},{9,1... | collective-permute-start | bytes 442376 | tf_op jit(solution)/shard_map/ppermute | solution.py:463
  111.0 5.5 %cold_adam.1 = (f32[2048,128]{1,0:T(8,128)}, f32[2048,128]{1,0:T(8,128)}, f32[2048,128]{1,0:T(8,128)}) custom-call(s32[24,128]{1,0:T(8,128)S(1)} %reshape.155.req_ref, bf16[3072,128]{1,0:T(8,128)(2,1)S(1)} %bitcast.207, f32[2048,128]{1,0:T(8,128)S(1)} %copy-done.1, f32[2048,128]{1,0:T(8,128)S(1)} %copy-done.3, f32[2048,128]{1,0:T(8,128)S(1)} %copy-done.4), custom_call_target="tpu_custom_call" | custom-call | flops 3221225472 | bytes 7090176 | tf_op jit(solution)/shard_map/cold_adam/pallas_call | solution.py:40
  120.8 1.9 %collective-permute-start.10 = (bf16[64,1152]{1,0:T(8,128)(2,1)S(1)}, bf16[64,1152]{1,0:T(8,128)(2,1)S(1)}, u32[]{:S(2)}, u32[]{:S(2)}) collective-permute-start(bf16[64,1152]{1,0:T(8,128)(2,1)S(1)} %pad_maximum_fusion.9), channel_id=1, source_target_pairs={{0,8},{1,9},{2,10},{3,11},{4,12},{5,13},{6,14},{7,15},{8,16},{9,17... | collective-permute-start | bytes 442376 | tf_op jit(solution)/shard_map/ppermute | solution.py:463
  122.8 1.9 %collective-permute-done.12 = bf16[64,1152]{1,0:T(8,128)(2,1)S(1)} collective-permute-done((bf16[64,1152]{1,0:T(8,128)(2,1)S(1)}, bf16[64,1152]{1,0:T(8,128)(2,1)S(1)}, u32[]{:S(2)}, u32[]{:S(2)}) %collective-permute-start.12) | collective-permute-done | bytes 147488 | tf_op jit(solution)/shard_map/ppermute | solution.py:463
  124.7 8.8 %collective-permute-done.11 = bf16[64,1152]{1,0:T(8,128)(2,1)S(1)} collective-permute-done((bf16[64,1152]{1,0:T(8,128)(2,1)S(1)}, bf16[64,1152]{1,0:T(8,128)(2,1)S(1)}, u32[]{:S(2)}, u32[]{:S(2)}) %collective-permute-start.11) | collective-permute-done | bytes 147488 | tf_op jit(solution)/shard_map/ppermute | solution.py:463
  134.0 2.4 %collective-permute-start.15 = (bf16[4,64,512]{2,1,0:T(8,128)(2,1)S(1)}, bf16[4,64,512]{2,1,0:T(8,128)(2,1)S(1)}, u32[]{:S(2)}, u32[]{:S(2)}) collective-permute-start(bf16[4,64,512]{2,1,0:T(8,128)(2,1)S(1)} %get-tuple-element.94), channel_id=1, source_target_pairs={{0,2},{1,3},{2,0},{3,1},{4,6},{5,7},{6,4},{7,5},{8,10},{9,11},{10,... | collective-permute-start | bytes 786440 | tf_op jit(solution)/shard_map/ppermute | solution.py:463
  136.4 5.8 %collective-permute-done.13 = bf16[4,64,640]{2,1,0:T(8,128)(2,1)S(1)} collective-permute-done((bf16[4,64,640]{2,1,0:T(8,128)(2,1)S(1)}, bf16[4,64,640]{2,1,0:T(8,128)(2,1)S(1)}, u32[]{:S(2)}, u32[]{:S(2)}) %collective-permute-start.13) | collective-permute-done | bytes 327712 | tf_op jit(solution)/shard_map/ppermute | solution.py:463
  147.2 1.8 %place.5 = (bf16[2048,1024]{1,0:T(8,128)(2,1)}, f32[2048,128]{1,0:T(8,128)}) custom-call(s32[4]{0:T(128)S(1)} %pad_add_fusion.digits_ref, bf16[2,4,64,640]{3,2,1,0:T(8,128)(2,1)S(1)} %collective-permute-done.17.refs_0_, bf16[2,4,64,512]{3,2,1,0:T(8,128)(2,1)S(1)} %collective-permute-done.18.refs_1_, ...), custom_call_target="tpu_custom_call", output_to_operand_aliasing={{0}: (3, {}), {1}: (4, {})} | custom-call | bytes 4194304 | tf_op jit(solution)/shard_map/place/pallas_call | solution.py:387
  149.0 8.8 %collective-permute-done.16.refs_1_ = bf16[2,4,64,512]{3,2,1,0:T(8,128)(2,1)S(1)} collective-permute-done((bf16[2,4,64,512]{3,2,1,0:T(8,128)(2,1)S(1)}, bf16[2,4,64,512]{3,2,1,0:T(8,128)(2,1)S(1)}, u32[]{:S(2)}, u32[]{:S(2)}) %collective-permute-start.16) | collective-permute-done | bytes 524320 | tf_op jit(solution)/shard_map/ppermute | solution.py:463
  (110 shorter events, 44.7 us)
Async XLA Ops:
  0.6 14.4 %all-to-all-start = ((s32[32,1,96]{2,1,0:T(1,128)}), s32[32,1,96]{2,1,0:T(1,128)S(1)}, u32[]{:S(2)}, u32[]{:S(2)}) async-start(s32[32,1,96]{2,1,0:T(1,128)} %bitcast.213), calls=%async_computation | async-start | bytes 32768 | tf_op jit(solution)/shard_map/all_to_all | solution.py:469
  18.4 23.2 %all-to-all-start.1 = ((bf16[32,96,128]{2,1,0:T(8,128)(2,1)}), bf16[32,96,128]{2,1,0:T(8,128)(2,1)S(1)}, u32[]{:S(2)}, u32[]{:S(2)}) async-start(bf16[32,96,128]{2,1,0:T(8,128)(2,1)} %bitcast.5), calls=%async_computation.1 | async-start | bytes 1572864 | tf_op jit(solution)/shard_map/all_to_all | solution.py:469
  54.9 7.2 %collective-permute-start = (bf16[2,2,4,64,512]{4,3,2,1,0:T(8,128)(2,1)}, bf16[2,2,4,64,512]{4,3,2,1,0:T(8,128)(2,1)}, u32[]{:S(2)}, u32[]{:S(2)}) collective-permute-start(bf16[2,2,4,64,512]{4,3,2,1,0:T(8,128)(2,1)} %get-tuple-element.43), channel_id=1, source_target_pairs={{0,1},{1,0},{2,3},{3,2},{4,5},{5,4},{6,7},{7,6},{8,9},{9,8},{10,11... | collective-permute-start | bytes 3145736 | tf_op jit(solution)/shard_map/ppermute | solution.py:463
  55.1 9.2 %collective-permute-start.2 = (bf16[2,2,4,64,512]{4,3,2,1,0:T(8,128)(2,1)}, bf16[2,2,4,64,512]{4,3,2,1,0:T(8,128)(2,1)S(1)}, u32[]{:S(2)}, u32[]{:S(2)}) collective-permute-start(bf16[2,2,4,64,512]{4,3,2,1,0:T(8,128)(2,1)} %copy-done.5), channel_id=1, source_target_pairs={{0,1},{1,0},{2,3},{3,2},{4,5},{5,4},{6,7},{7,6},{8,9},{9,8},{10,11... | collective-permute-start | bytes 3145736 | tf_op jit(solution)/shard_map/ppermute | solution.py:463
  60.4 1.6 collective-permute-start.1
  65.4 14.4 %collective-permute-start.5 = (bf16[2,4,64,512]{3,2,1,0:T(8,128)(2,1)S(1)}, bf16[2,4,64,512]{3,2,1,0:T(8,128)(2,1)}, u32[]{:S(2)}, u32[]{:S(2)}) collective-permute-start(bf16[2,4,64,512]{3,2,1,0:T(8,128)(2,1)S(1)} %fusion.1), channel_id=1, source_target_pairs={{0,4},{1,5},{2,6},{3,7},{4,0},{5,1},{6,2},{7,3},{8,12},{9,13},{10,... | collective-permute-start | bytes 1572872 | tf_op jit(solution)/shard_map/ppermute | solution.py:463
  67.0 22.9 %collective-permute-start.3 = (bf16[2,4,64,640]{3,2,1,0:T(8,128)(2,1)}, bf16[2,4,64,640]{3,2,1,0:T(8,128)(2,1)}, u32[]{:S(2)}, u32[]{:S(2)}) collective-permute-start(bf16[2,4,64,640]{3,2,1,0:T(8,128)(2,1)} %pad_maximum_fusion), channel_id=1, source_target_pairs={{0,2},{1,3},{2,0},{3,1},{4,6},{5,7},{6,4},{7,5},{8,10},{9,11},{10,... | collective-permute-start | bytes 1966088 | tf_op jit(solution)/shard_map/ppermute | solution.py:463
  73.1 34.3 %all-to-all-start.2 = ((bf16[32,112,128]{2,1,0:T(8,128)(2,1)}), bf16[32,112,128]{2,1,0:T(8,128)(2,1)}, u32[]{:S(2)}, u32[]{:S(2)}) async-start(bf16[32,112,128]{2,1,0:T(8,128)(2,1)} %cold_sums.1), calls=%async_computation.2 | async-start | bytes 1835008 | tf_op jit(solution)/shard_map/all_to_all | solution.py:469
  81.6 17.5 %collective-permute-start.6 = (bf16[4,64,512]{2,1,0:T(8,128)(2,1)}, bf16[4,64,512]{2,1,0:T(8,128)(2,1)}, u32[]{:S(2)}, u32[]{:S(2)}) collective-permute-start(bf16[4,64,512]{2,1,0:T(8,128)(2,1)} %fusion.2), channel_id=1, source_target_pairs={{0,2},{1,3},{2,0},{3,1},{4,6},{5,7},{6,4},{7,5},{8,10},{9,11},{10,... | collective-permute-start | bytes 786440 | tf_op jit(solution)/shard_map/ppermute | solution.py:463
  91.9 8.5 %collective-permute-start.4 = (bf16[4,64,640]{2,1,0:T(8,128)(2,1)S(1)}, bf16[4,64,640]{2,1,0:T(8,128)(2,1)S(1)}, u32[]{:S(2)}, u32[]{:S(2)}) collective-permute-start(bf16[4,64,640]{2,1,0:T(8,128)(2,1)S(1)} %pad_maximum_fusion.3), channel_id=1, source_target_pairs={{0,4},{1,5},{2,6},{3,7},{4,0},{5,1},{6,2},{7,3},{8,12},{9,13},{10,... | collective-permute-start | bytes 983048 | tf_op jit(solution)/shard_map/ppermute | solution.py:463
  102.6 15.5 %collective-permute-start.7 = (bf16[64,1152]{1,0:T(8,128)(2,1)S(1)}, bf16[64,1152]{1,0:T(8,128)(2,1)S(1)}, u32[]{:S(2)}, u32[]{:S(2)}) collective-permute-start(bf16[64,1152]{1,0:T(8,128)(2,1)S(1)} %pad_maximum_fusion.6), channel_id=1, source_target_pairs={{0,8},{1,9},{2,10},{3,11},{4,12},{5,13},{6,14},{7,15},{8,16},{9,17... | collective-permute-start | bytes 442376 | tf_op jit(solution)/shard_map/ppermute | solution.py:463
  103.6 14.4 %collective-permute-start.8 = (bf16[64,1152]{1,0:T(8,128)(2,1)S(1)}, bf16[64,1152]{1,0:T(8,128)(2,1)S(1)}, u32[]{:S(2)}, u32[]{:S(2)}) collective-permute-start(bf16[64,1152]{1,0:T(8,128)(2,1)S(1)} %pad_maximum_fusion.7), channel_id=1, source_target_pairs={{0,16},{1,17},{2,18},{3,19},{4,20},{5,21},{6,22},{7,23},{8,24},{9,... | collective-permute-start | bytes 442376 | tf_op jit(solution)/shard_map/ppermute | solution.py:463
  104.6 13.4 %collective-permute-start.9 = (bf16[64,1152]{1,0:T(8,128)(2,1)S(1)}, bf16[64,1152]{1,0:T(8,128)(2,1)S(1)}, u32[]{:S(2)}, u32[]{:S(2)}) collective-permute-start(bf16[64,1152]{1,0:T(8,128)(2,1)S(1)} %pad_maximum_fusion.8), channel_id=1, source_target_pairs={{0,24},{1,25},{2,26},{3,27},{4,28},{5,29},{6,30},{7,31},{8,0},{9,1... | collective-permute-start | bytes 442376 | tf_op jit(solution)/shard_map/ppermute | solution.py:463
  119.2 5.5 %collective-permute-start.12 = (bf16[64,1152]{1,0:T(8,128)(2,1)S(1)}, bf16[64,1152]{1,0:T(8,128)(2,1)S(1)}, u32[]{:S(2)}, u32[]{:S(2)}) collective-permute-start(bf16[64,1152]{1,0:T(8,128)(2,1)S(1)} %pad_maximum_fusion.9), channel_id=1, source_target_pairs={{0,24},{1,25},{2,26},{3,27},{4,28},{5,29},{6,30},{7,31},{8,0},{9,1... | collective-permute-start | bytes 442376 | tf_op jit(solution)/shard_map/ppermute | solution.py:463
  120.3 13.1 %collective-permute-start.11 = (bf16[64,1152]{1,0:T(8,128)(2,1)S(1)}, bf16[64,1152]{1,0:T(8,128)(2,1)S(1)}, u32[]{:S(2)}, u32[]{:S(2)}) collective-permute-start(bf16[64,1152]{1,0:T(8,128)(2,1)S(1)} %pad_maximum_fusion.9), channel_id=1, source_target_pairs={{0,16},{1,17},{2,18},{3,19},{4,20},{5,21},{6,22},{7,23},{8,24},{9,... | collective-permute-start | bytes 442376 | tf_op jit(solution)/shard_map/ppermute | solution.py:463
  120.8 12.6 %collective-permute-start.10 = (bf16[64,1152]{1,0:T(8,128)(2,1)S(1)}, bf16[64,1152]{1,0:T(8,128)(2,1)S(1)}, u32[]{:S(2)}, u32[]{:S(2)}) collective-permute-start(bf16[64,1152]{1,0:T(8,128)(2,1)S(1)} %pad_maximum_fusion.9), channel_id=1, source_target_pairs={{0,8},{1,9},{2,10},{3,11},{4,12},{5,13},{6,14},{7,15},{8,16},{9,17... | collective-permute-start | bytes 442376 | tf_op jit(solution)/shard_map/ppermute | solution.py:463
  133.6 8.7 %collective-permute-start.13 = (bf16[4,64,640]{2,1,0:T(8,128)(2,1)S(1)}, bf16[4,64,640]{2,1,0:T(8,128)(2,1)S(1)}, u32[]{:S(2)}, u32[]{:S(2)}) collective-permute-start(bf16[4,64,640]{2,1,0:T(8,128)(2,1)S(1)} %get-tuple-element.92), channel_id=1, source_target_pairs={{0,4},{1,5},{2,6},{3,7},{4,0},{5,1},{6,2},{7,3},{8,12},{9,13},{10,... | collective-permute-start | bytes 983048 | tf_op jit(solution)/shard_map/ppermute | solution.py:463
  134.0 9.3 %collective-permute-start.15 = (bf16[4,64,512]{2,1,0:T(8,128)(2,1)S(1)}, bf16[4,64,512]{2,1,0:T(8,128)(2,1)S(1)}, u32[]{:S(2)}, u32[]{:S(2)}) collective-permute-start(bf16[4,64,512]{2,1,0:T(8,128)(2,1)S(1)} %get-tuple-element.94), channel_id=1, source_target_pairs={{0,2},{1,3},{2,0},{3,1},{4,6},{5,7},{6,4},{7,5},{8,10},{9,11},{10,... | collective-permute-start | bytes 786440 | tf_op jit(solution)/shard_map/ppermute | solution.py:463
  142.3 4.9 %collective-permute-start.17 = (bf16[2,4,64,640]{3,2,1,0:T(8,128)(2,1)S(1)}, bf16[2,4,64,640]{3,2,1,0:T(8,128)(2,1)S(1)}, u32[]{:S(2)}, u32[]{:S(2)}) collective-permute-start(bf16[2,4,64,640]{3,2,1,0:T(8,128)(2,1)S(1)} %pad_maximum_fusion.1.refs_0_), channel_id=1, source_target_pairs={{0,1},{1,0},{2,3},{3,2},{4,5},{5,4},{6,7},{7,6},{8,9},{9,8},{10,11... | collective-permute-start | bytes 1966088 | tf_op jit(solution)/shard_map/ppermute | solution.py:463
  142.4 17.1 %collective-permute-start.14 = (bf16[2,4,64,640]{3,2,1,0:T(8,128)(2,1)S(1)}, bf16[2,4,64,640]{3,2,1,0:T(8,128)(2,1)S(1)}, u32[]{:S(2)}, u32[]{:S(2)}) collective-permute-start(bf16[2,4,64,640]{3,2,1,0:T(8,128)(2,1)S(1)} %pad_maximum_fusion.1.refs_0_), channel_id=1, source_target_pairs={{0,2},{1,3},{2,0},{3,1},{4,6},{5,7},{6,4},{7,5},{8,10},{9,11},{10,... | collective-permute-start | bytes 1966088 | tf_op jit(solution)/shard_map/ppermute | solution.py:463
  143.4 3.8 %collective-permute-start.18 = (bf16[2,4,64,512]{3,2,1,0:T(8,128)(2,1)S(1)}, bf16[2,4,64,512]{3,2,1,0:T(8,128)(2,1)S(1)}, u32[]{:S(2)}, u32[]{:S(2)}) collective-permute-start(bf16[2,4,64,512]{3,2,1,0:T(8,128)(2,1)S(1)} %pad_maximum_fusion.2.refs_1_), channel_id=1, source_target_pairs={{0,1},{1,0},{2,3},{3,2},{4,5},{5,4},{6,7},{7,6},{8,9},{9,8},{10,11... | collective-permute-start | bytes 1572872 | tf_op jit(solution)/shard_map/ppermute | solution.py:463
  143.6 14.2 %collective-permute-start.16 = (bf16[2,4,64,512]{3,2,1,0:T(8,128)(2,1)S(1)}, bf16[2,4,64,512]{3,2,1,0:T(8,128)(2,1)S(1)}, u32[]{:S(2)}, u32[]{:S(2)}) collective-permute-start(bf16[2,4,64,512]{3,2,1,0:T(8,128)(2,1)S(1)} %pad_maximum_fusion.2.refs_1_), channel_id=1, source_target_pairs={{0,4},{1,5},{2,6},{3,7},{4,0},{5,1},{6,2},{7,3},{8,12},{9,13},{10,... | collective-permute-start | bytes 1572872 | tf_op jit(solution)/shard_map/ppermute | solution.py:463
  159.5 2.9 %collective-permute-start.19 = (bf16[2,4,64,640]{3,2,1,0:T(8,128)(2,1)S(1)}, bf16[2,4,64,640]{3,2,1,0:T(8,128)(2,1)S(1)}, u32[]{:S(2)}, u32[]{:S(2)}) collective-permute-start(bf16[2,4,64,640]{3,2,1,0:T(8,128)(2,1)S(1)} %collective-permute-done.14.refs_0_), channel_id=1, source_target_pairs={{0,1},{1,0},{2,3},{3,2},{4,5},{5,4},{6,7},{7,6},{8,9},{9,8},{10,11... | collective-permute-start | bytes 1966088 | tf_op jit(solution)/shard_map/ppermute | solution.py:463
  159.5 2.8 %collective-permute-start.20 = (bf16[2,4,64,512]{3,2,1,0:T(8,128)(2,1)S(1)}, bf16[2,4,64,512]{3,2,1,0:T(8,128)(2,1)S(1)}, u32[]{:S(2)}, u32[]{:S(2)}) collective-permute-start(bf16[2,4,64,512]{3,2,1,0:T(8,128)(2,1)S(1)} %collective-permute-done.16.refs_1_), channel_id=1, source_target_pairs={{0,1},{1,0},{2,3},{3,2},{4,5},{5,4},{6,7},{7,6},{8,9},{9,8},{10,11... | collective-permute-start | bytes 1572872 | tf_op jit(solution)/shard_map/ppermute | solution.py:463
  (17 other events, 124.6 us)

commit v4 on v3

--- a/solution.py
+++ b/solution.py
@@ -575,6 +575,8 @@
     groups_b = [[(keep_b, ()), (got_b, ())]]
     groups_a = [[(keep_a, ()), (got_a, ())], [(keep_hot, ()), (got_hot, ())]]
     sends_b = step_sends(groups_b, order_b[0])
+    sends_b, got_hot = lax.optimization_barrier((sends_b, got_hot))
+    groups_a[1] = [(keep_hot, ()), (got_hot, ())]
     sends_a = step_sends(groups_a, order_a[0])
     grad_input, sends_a, sends_b = lax.optimization_barrier((grad_input, sends_a, sends_b))
     groups_b = step_takes(groups_b, order_b[0], sends_b)

time: 165 us -> 163 us (0.988)
  other arithmetic: 13.3 us -> 15.3 us
  local copies, waits for them, and re-layouts: 12.4 us -> 10.4 us
  starting transfers between devices: 34.7 us -> 32.7 us
    convert_element_type x2, other arithmetic: 1.98 us -> 3.99 us  [step_sends(): return [pack(groups, k).astype(bf16) for k in range(1, sizes[level])]]
    ppermute x21, starting transfers between devices: 21.2 us -> 19.2 us  [exchange(): return lax.ppermute(value, 'dev', pairs)]
    unnamed x36, local copies, waits for them, and re-layouts: 10.4 us -> 8.5 us
  transfers between devices with their start and end apart: 24 -> 24, of which waited for: 12 -> 12; matrix products, arithmetic and copies ran while one was open for 9% -> 10% of each run, Pallas kernels for 13% -> 13%
where the time goes in v4:
time: 163 us; the launch traced here: 162 us
  waiting for transfers between devices  64.7 us (40%)
  Pallas kernels  38.2 us (23%)
  starting transfers between devices  32.7 us (20%)
  other arithmetic  15.3 us (9%)
  local copies, waits for them, and re-layouts  10.4 us (6%)
    ppermute x21, waiting for transfers between devices, exchange(): return lax.ppermute(value, 'dev', pairs)  43.7 us
    pallas_call x7, Pallas kernels, call(): pl.pallas_call(kernel, out_shape=outs, in_specs=specs, out_specs=[pl.Bloc...  31 us
    all_to_all x3, waiting for transfers between devices, all_to_all(): return lax.all_to_all(value, 'dev', split_axis=0, concat_axis=0, tiled=True)  20.9 us
    ppermute x21, starting transfers between devices, exchange(): return lax.ppermute(value, 'dev', pairs)  19.2 us
    all_to_all x3, starting transfers between devices, all_to_all(): return lax.all_to_all(value, 'dev', split_axis=0, concat_axis=0, tiled=True)  13.5 us
    unnamed x36, local copies, waits for them, and re-layouts  8.5 us
    pallas_call x4, Pallas kernels, place(): pl.pallas_call(functools.partial(place_kernel, dims, tuple(plan)), out_sh...  7.23 us
    another operation x7, other arithmetic  6.36 us
  transfers between devices with their start and end apart: 24, of which 12 were waited for; matrix products, arithmetic and copies ran while one was open for 10% of the time, Pallas kernels for 13%

profile of v4, /device:TPU:0, one launch (start us, length us, event | category | flops | bytes accessed | tf_op | source)
XLA Modules:
  0.0 162.5 jit_solution(17226393943604026973)
XLA Ops:
  0.6 7.3 %all-to-all-start = ((s32[32,1,96]{2,1,0:T(1,128)}), s32[32,1,96]{2,1,0:T(1,128)S(1)}, u32[]{:S(2)}, u32[]{:S(2)}) async-start(s32[32,1,96]{2,1,0:T(1,128)} %bitcast.213), calls=%async_computation | async-start | bytes 32768 | tf_op jit(solution)/shard_map/all_to_all | solution.py:469
  10.9 4.1 %all-to-all-done.req_ref = s32[32,1,96]{2,1,0:T(1,128)S(1)} async-done(((s32[32,1,96]{2,1,0:T(1,128)}), s32[32,1,96]{2,1,0:T(1,128)S(1)}, u32[]{:S(2)}, u32[]{:S(2)}) %all-to-all-start) | async-done | bytes 12320 | tf_op jit(solution)/shard_map/all_to_all | solution.py:469
  15.0 3.4 %owner_pick.1 = bf16[3072,128]{1,0:T(8,128)(2,1)} custom-call(s32[32,1,96]{2,1,0:T(1,128)S(1)} %all-to-all-done.req_ref, bf16[512,512]{1,0:T(8,128)(2,1)S(1)} %fold_table.1.folded_ref), custom_call_target="tpu_custom_call" | custom-call | flops 3221225472 | bytes 1323008 | tf_op jit(solution)/shard_map/owner_pick/pallas_call | solution.py:40
  18.4 2.8 %all-to-all-start.1 = ((bf16[32,96,128]{2,1,0:T(8,128)(2,1)}), bf16[32,96,128]{2,1,0:T(8,128)(2,1)S(1)}, u32[]{:S(2)}, u32[]{:S(2)}) async-start(bf16[32,96,128]{2,1,0:T(8,128)(2,1)} %bitcast.5), calls=%async_computation.1 | async-start | bytes 1572864 | tf_op jit(solution)/shard_map/all_to_all | solution.py:469
  21.2 2.5 %hot_pick.1.hot_hbm = bf16[256,2048]{1,0:T(8,128)(2,1)S(1)} custom-call(s32[256,16]{1,0:T(8,128)S(1)} %copy.29.ids_ref, s32[256,16]{1,0:T(8,128)S(1)} %copy.31.slot_ref, bf16[2048,128]{1,0:T(8,128)(2,1)S(1)} %copy-done.5), custom_call_target="tpu_custom_call" | custom-call | flops 42949672960 | bytes 1605632 | tf_op jit(solution)/shard_map/hot_pick/pallas_call | solution.py:40
  24.8 16.8 %all-to-all-done.1 = bf16[32,96,128]{2,1,0:T(8,128)(2,1)S(1)} async-done(((bf16[32,96,128]{2,1,0:T(8,128)(2,1)}), bf16[32,96,128]{2,1,0:T(8,128)(2,1)S(1)}, u32[]{:S(2)}, u32[]{:S(2)}) %all-to-all-start.1) | async-done | bytes 786464 | tf_op jit(solution)/shard_map/all_to_all | solution.py:469
  41.6 11.3 %forward.1 = (f32[16,128]{1,0:T(8,128)S(1)}, bf16[2,2,4,64,512]{4,3,2,1,0:T(8,128)(2,1)S(1)}, bf16[2,2,4,64,512]{4,3,2,1,0:T(8,128)(2,1)}, bf16[2,2,4,64,512]{4,...) custom-call(s32[4]{0:T(128)S(1)} %pad_add_fusion.digits_ref, ...), custom_call_target="tpu_custom_call" | custom-call | flops 6442450944 | bytes 12353552 | tf_op jit(solution)/shard_map/forward/pallas_call | solution.py:40
  55.7 3.6 %hot_sums.1 = (bf16[2,2,4,64,128]{4,3,2,1,0:T(8,128)(2,1)S(1)}, bf16[2,2,4,64,128]{4,3,2,1,0:T(8,128)(2,1)S(1)}) custom-call(s32[4]{0:T(128)S(1)} %pad_add_fusion.digits_ref, s32[256,16]{1,0:T(8,128)S(1)} %copy.32.id_ref, s32[16,256]{1,0:T(8,128)S(1)} %bitcast.209, bf16[256,2048]{1,0:T(8,128)(2,1)S(1)} %copy-done.8), custom_call_target="tpu_custom_call" | custom-call | flops 4294967296 | bytes 1605648 | tf_op jit(solution)/shard_map/hot_sums/pallas_call | solution.py:40
  59.4 2.1 %fusion.1 = bf16[2,4,64,512]{3,2,1,0:T(8,128)(2,1)} fusion(bf16[2,2,4,64,512]{4,3,2,1,0:T(8,128)(2,1)} %collective-permute-done.1, bf16[2,2,4,64,512]{4,3,2,1,0:T(8,128)(2,1)S(1)} %get-tuple-element.48), kind=kLoop, calls=%fused_computation.5 | loop fusion | flops 1048576 | bytes 1572864 | tf_op jit(solution)/shard_map/convert_element_type | solution.py:562
  66.7 4.7 %cold_sums.1 = bf16[32,112,128]{2,1,0:T(8,128)(2,1)} custom-call(s32[256,16]{1,0:T(8,128)S(1)} %copy.31.slot_ref, s32[16,256]{1,0:T(8,128)S(1)} %bitcast.208, bf16[256,2048]{1,0:T(8,128)(2,1)S(1)} %copy-done.9, f32[16,128]{1,0:T(8,128)S(1)} %get-tuple-element.56.bias_ref), custom_call_target="tpu_custom_call" | custom-call | flops 6442450944 | bytes 2007040 | tf_op jit(solution)/shard_map/cold_sums/pallas_call | solution.py:40
  71.4 3.4 %all-to-all-start.2 = ((bf16[32,112,128]{2,1,0:T(8,128)(2,1)}), bf16[32,112,128]{2,1,0:T(8,128)(2,1)}, u32[]{:S(2)}, u32[]{:S(2)}) async-start(bf16[32,112,128]{2,1,0:T(8,128)(2,1)} %cold_sums.1), calls=%async_computation.2 | async-start | bytes 1835008 | tf_op jit(solution)/shard_map/all_to_all | solution.py:469
  74.7 3.9 %collective-permute-done.5 = bf16[2,4,64,512]{3,2,1,0:T(8,128)(2,1)S(1)} collective-permute-done((bf16[2,4,64,512]{3,2,1,0:T(8,128)(2,1)}, bf16[2,4,64,512]{3,2,1,0:T(8,128)(2,1)S(1)}, u32[]{:S(2)}, u32[]{:S(2)}) %collective-permute-start.5) | collective-permute-done | bytes 524320 | tf_op jit(solution)/shard_map/ppermute | solution.py:463
  78.6 1.9 %fusion.2 = bf16[4,64,512]{2,1,0:T(8,128)(2,1)} fusion(bf16[2,4,64,512]{3,2,1,0:T(8,128)(2,1)S(1)} %collective-permute-done.5, bf16[2,2,4,64,512]{4,3,2,1,0:T(8,128)(2,1)} %collective-permute-done.1, bf16[2,2,4,64,512]{4,3,2,1,0:T(8,128)(2,1)S(1)} %get-tuple-element.48), kind=kLoop, calls=%fused_computation.8 | loop fusion | flops 786432 | bytes 1048576 | tf_op jit(solution)/shard_map/convert_element_type | solution.py:562
  80.6 2.3 %collective-permute-start.6 = (bf16[4,64,512]{2,1,0:T(8,128)(2,1)}, bf16[4,64,512]{2,1,0:T(8,128)(2,1)}, u32[]{:S(2)}, u32[]{:S(2)}) collective-permute-start(bf16[4,64,512]{2,1,0:T(8,128)(2,1)} %fusion.2), channel_id=1, source_target_pairs={{0,2},{1,3},{2,0},{3,1},{4,6},{5,7},{6,4},{7,5},{8,10},{9,11},{10,... | collective-permute-start | bytes 786440 | tf_op jit(solution)/shard_map/ppermute | solution.py:463
  82.9 5.2 %collective-permute-done.3 = bf16[2,4,64,640]{3,2,1,0:T(8,128)(2,1)} collective-permute-done((bf16[2,4,64,640]{3,2,1,0:T(8,128)(2,1)}, bf16[2,4,64,640]{3,2,1,0:T(8,128)(2,1)}, u32[]{:S(2)}, u32[]{:S(2)}) %collective-permute-start.3) | collective-permute-done | bytes 655392 | tf_op jit(solution)/shard_map/ppermute | solution.py:463
  91.6 6.2 %collective-permute-done.6 = bf16[4,64,512]{2,1,0:T(8,128)(2,1)} collective-permute-done((bf16[4,64,512]{2,1,0:T(8,128)(2,1)}, bf16[4,64,512]{2,1,0:T(8,128)(2,1)}, u32[]{:S(2)}, u32[]{:S(2)}) %collective-permute-start.6) | collective-permute-done | bytes 262176 | tf_op jit(solution)/shard_map/ppermute | solution.py:463
  103.4 2.8 %collective-permute-start.9 = (bf16[64,1152]{1,0:T(8,128)(2,1)S(1)}, bf16[64,1152]{1,0:T(8,128)(2,1)S(1)}, u32[]{:S(2)}, u32[]{:S(2)}) collective-permute-start(bf16[64,1152]{1,0:T(8,128)(2,1)S(1)} %pad_maximum_fusion.8), channel_id=1, source_target_pairs={{0,24},{1,25},{2,26},{3,27},{4,28},{5,29},{6,30},{7,31},{8,0},{9,1... | collective-permute-start | bytes 442376 | tf_op jit(solution)/shard_map/ppermute | solution.py:463
  109.8 5.5 %cold_adam.1 = (f32[2048,128]{1,0:T(8,128)}, f32[2048,128]{1,0:T(8,128)}, f32[2048,128]{1,0:T(8,128)}) custom-call(s32[24,128]{1,0:T(8,128)S(1)} %reshape.155.req_ref, bf16[3072,128]{1,0:T(8,128)(2,1)S(1)} %bitcast.207, f32[2048,128]{1,0:T(8,128)S(1)} %copy-done.1, f32[2048,128]{1,0:T(8,128)S(1)} %copy-done.3, f32[2048,128]{1,0:T(8,128)S(1)} %copy-done.4), custom_call_target="tpu_custom_call" | custom-call | flops 3221225472 | bytes 7090176 | tf_op jit(solution)/shard_map/cold_adam/pallas_call | solution.py:40
  120.1 1.9 %collective-permute-start.10 = (bf16[64,1152]{1,0:T(8,128)(2,1)S(1)}, bf16[64,1152]{1,0:T(8,128)(2,1)S(1)}, u32[]{:S(2)}, u32[]{:S(2)}) collective-permute-start(bf16[64,1152]{1,0:T(8,128)(2,1)S(1)} %pad_maximum_fusion.9), channel_id=1, source_target_pairs={{0,8},{1,9},{2,10},{3,11},{4,12},{5,13},{6,14},{7,15},{8,16},{9,17... | collective-permute-start | bytes 442376 | tf_op jit(solution)/shard_map/ppermute | solution.py:463
  123.3 9.0 %collective-permute-done.11 = bf16[64,1152]{1,0:T(8,128)(2,1)S(1)} collective-permute-done((bf16[64,1152]{1,0:T(8,128)(2,1)S(1)}, bf16[64,1152]{1,0:T(8,128)(2,1)S(1)}, u32[]{:S(2)}, u32[]{:S(2)}) %collective-permute-start.11) | collective-permute-done | bytes 147488 | tf_op jit(solution)/shard_map/ppermute | solution.py:463
  134.4 5.9 %collective-permute-done.13 = bf16[4,64,640]{2,1,0:T(8,128)(2,1)S(1)} collective-permute-done((bf16[4,64,640]{2,1,0:T(8,128)(2,1)S(1)}, bf16[4,64,640]{2,1,0:T(8,128)(2,1)S(1)}, u32[]{:S(2)}, u32[]{:S(2)}) %collective-permute-start.13) | collective-permute-done | bytes 327712 | tf_op jit(solution)/shard_map/ppermute | solution.py:463
  144.7 1.8 %place.5 = (bf16[2048,1024]{1,0:T(8,128)(2,1)}, f32[2048,128]{1,0:T(8,128)}) custom-call(s32[4]{0:T(128)S(1)} %pad_add_fusion.digits_ref, bf16[2,4,64,640]{3,2,1,0:T(8,128)(2,1)S(1)} %collective-permute-done.17.refs_0_, bf16[2,4,64,512]{3,2,1,0:T(8,128)(2,1)S(1)} %collective-permute-done.18.refs_1_, ...), custom_call_target="tpu_custom_call", output_to_operand_aliasing={{0}: (3, {}), {1}: (4, {})} | custom-call | bytes 4194304 | tf_op jit(solution)/shard_map/place/pallas_call | solution.py:387
  146.5 10.0 %collective-permute-done.16.refs_1_ = bf16[2,4,64,512]{3,2,1,0:T(8,128)(2,1)S(1)} collective-permute-done((bf16[2,4,64,512]{3,2,1,0:T(8,128)(2,1)S(1)}, bf16[2,4,64,512]{3,2,1,0:T(8,128)(2,1)S(1)}, u32[]{:S(2)}, u32[]{:S(2)}) %collective-permute-start.16) | collective-permute-done | bytes 524320 | tf_op jit(solution)/shard_map/ppermute | solution.py:463
  160.5 1.8 %place.7 = (bf16[2048,1024]{1,0:T(8,128)(2,1)}, f32[2048,128]{1,0:T(8,128)}) custom-call(s32[4]{0:T(128)S(1)} %pad_add_fusion.digits_ref, bf16[2,4,64,640]{3,2,1,0:T(8,128)(2,1)S(1)} %collective-permute-done.19.refs_0_, bf16[2,4,64,512]{3,2,1,0:T(8,128)(2,1)S(1)} %collective-permute-done.20.refs_1_, ...), custom_call_target="tpu_custom_call", output_to_operand_aliasing={{0}: (3, {}), {1}: (4, {})} | custom-call | bytes 4194304 | tf_op jit(solution)/shard_map/place/pallas_call | solution.py:387
  (110 shorter events, 41.1 us)
Async XLA Ops:
  0.6 14.4 %all-to-all-start = ((s32[32,1,96]{2,1,0:T(1,128)}), s32[32,1,96]{2,1,0:T(1,128)S(1)}, u32[]{:S(2)}, u32[]{:S(2)}) async-start(s32[32,1,96]{2,1,0:T(1,128)} %bitcast.213), calls=%async_computation | async-start | bytes 32768 | tf_op jit(solution)/shard_map/all_to_all | solution.py:469
  18.4 23.2 %all-to-all-start.1 = ((bf16[32,96,128]{2,1,0:T(8,128)(2,1)}), bf16[32,96,128]{2,1,0:T(8,128)(2,1)S(1)}, u32[]{:S(2)}, u32[]{:S(2)}) async-start(bf16[32,96,128]{2,1,0:T(8,128)(2,1)} %bitcast.5), calls=%async_computation.1 | async-start | bytes 1572864 | tf_op jit(solution)/shard_map/all_to_all | solution.py:469
  53.9 5.5 %collective-permute-start.1 = (bf16[2,2,4,64,512]{4,3,2,1,0:T(8,128)(2,1)}, bf16[2,2,4,64,512]{4,3,2,1,0:T(8,128)(2,1)}, u32[]{:S(2)}, u32[]{:S(2)}) collective-permute-start(bf16[2,2,4,64,512]{4,3,2,1,0:T(8,128)(2,1)} %get-tuple-element.49), channel_id=1, source_target_pairs={{0,1},{1,0},{2,3},{3,2},{4,5},{5,4},{6,7},{7,6},{8,9},{9,8},{10,11... | collective-permute-start | bytes 3145736 | tf_op jit(solution)/shard_map/ppermute | solution.py:463
  53.9 7.7 %collective-permute-start = (bf16[2,2,4,64,512]{4,3,2,1,0:T(8,128)(2,1)}, bf16[2,2,4,64,512]{4,3,2,1,0:T(8,128)(2,1)}, u32[]{:S(2)}, u32[]{:S(2)}) collective-permute-start(bf16[2,2,4,64,512]{4,3,2,1,0:T(8,128)(2,1)} %get-tuple-element.45), channel_id=1, source_target_pairs={{0,1},{1,0},{2,3},{3,2},{4,5},{5,4},{6,7},{7,6},{8,9},{9,8},{10,11... | collective-permute-start | bytes 3145736 | tf_op jit(solution)/shard_map/ppermute | solution.py:463
  59.3 2.2 %collective-permute-start.2 = (bf16[2,2,4,64,128]{4,3,2,1,0:T(8,128)(2,1)S(1)}, bf16[2,2,4,64,128]{4,3,2,1,0:T(8,128)(2,1)S(1)}, u32[]{:S(2)}, u32[]{:S(2)}) collective-permute-start(bf16[2,2,4,64,128]{4,3,2,1,0:T(8,128)(2,1)S(1)} %get-tuple-element.50), channel_id=1, source_target_pairs={{0,1},{1,0},{2,3},{3,2},{4,5},{5,4},{6,7},{7,6},{8,9},{9,8},{10,11... | collective-permute-start | bytes 786440 | tf_op jit(solution)/shard_map/ppermute | solution.py:463
  63.7 14.9 %collective-permute-start.5 = (bf16[2,4,64,512]{3,2,1,0:T(8,128)(2,1)}, bf16[2,4,64,512]{3,2,1,0:T(8,128)(2,1)S(1)}, u32[]{:S(2)}, u32[]{:S(2)}) collective-permute-start(bf16[2,4,64,512]{3,2,1,0:T(8,128)(2,1)} %fusion.1), channel_id=1, source_target_pairs={{0,4},{1,5},{2,6},{3,7},{4,0},{5,1},{6,2},{7,3},{8,12},{9,13},{10,... | collective-permute-start | bytes 1572872 | tf_op jit(solution)/shard_map/ppermute | solution.py:463
  65.3 22.8 %collective-permute-start.3 = (bf16[2,4,64,640]{3,2,1,0:T(8,128)(2,1)}, bf16[2,4,64,640]{3,2,1,0:T(8,128)(2,1)}, u32[]{:S(2)}, u32[]{:S(2)}) collective-permute-start(bf16[2,4,64,640]{3,2,1,0:T(8,128)(2,1)} %pad_maximum_fusion), channel_id=1, source_target_pairs={{0,2},{1,3},{2,0},{3,1},{4,6},{5,7},{6,4},{7,5},{8,10},{9,11},{10,... | collective-permute-start | bytes 1966088 | tf_op jit(solution)/shard_map/ppermute | solution.py:463
  71.4 34.8 %all-to-all-start.2 = ((bf16[32,112,128]{2,1,0:T(8,128)(2,1)}), bf16[32,112,128]{2,1,0:T(8,128)(2,1)}, u32[]{:S(2)}, u32[]{:S(2)}) async-start(bf16[32,112,128]{2,1,0:T(8,128)(2,1)} %cold_sums.1), calls=%async_computation.2 | async-start | bytes 1835008 | tf_op jit(solution)/shard_map/all_to_all | solution.py:469
  80.6 17.3 %collective-permute-start.6 = (bf16[4,64,512]{2,1,0:T(8,128)(2,1)}, bf16[4,64,512]{2,1,0:T(8,128)(2,1)}, u32[]{:S(2)}, u32[]{:S(2)}) collective-permute-start(bf16[4,64,512]{2,1,0:T(8,128)(2,1)} %fusion.2), channel_id=1, source_target_pairs={{0,2},{1,3},{2,0},{3,1},{4,6},{5,7},{6,4},{7,5},{8,10},{9,11},{10,... | collective-permute-start | bytes 786440 | tf_op jit(solution)/shard_map/ppermute | solution.py:463
  90.1 9.6 %collective-permute-start.4 = (bf16[4,64,640]{2,1,0:T(8,128)(2,1)S(1)}, bf16[4,64,640]{2,1,0:T(8,128)(2,1)S(1)}, u32[]{:S(2)}, u32[]{:S(2)}) collective-permute-start(bf16[4,64,640]{2,1,0:T(8,128)(2,1)S(1)} %pad_maximum_fusion.3), channel_id=1, source_target_pairs={{0,4},{1,5},{2,6},{3,7},{4,0},{5,1},{6,2},{7,3},{8,12},{9,13},{10,... | collective-permute-start | bytes 983048 | tf_op jit(solution)/shard_map/ppermute | solution.py:463
  101.8 15.0 %collective-permute-start.7 = (bf16[64,1152]{1,0:T(8,128)(2,1)S(1)}, bf16[64,1152]{1,0:T(8,128)(2,1)S(1)}, u32[]{:S(2)}, u32[]{:S(2)}) collective-permute-start(bf16[64,1152]{1,0:T(8,128)(2,1)S(1)} %pad_maximum_fusion.6), channel_id=1, source_target_pairs={{0,8},{1,9},{2,10},{3,11},{4,12},{5,13},{6,14},{7,15},{8,16},{9,17... | collective-permute-start | bytes 442376 | tf_op jit(solution)/shard_map/ppermute | solution.py:463
  102.3 14.5 %collective-permute-start.8 = (bf16[64,1152]{1,0:T(8,128)(2,1)S(1)}, bf16[64,1152]{1,0:T(8,128)(2,1)S(1)}, u32[]{:S(2)}, u32[]{:S(2)}) collective-permute-start(bf16[64,1152]{1,0:T(8,128)(2,1)S(1)} %pad_maximum_fusion.7), channel_id=1, source_target_pairs={{0,16},{1,17},{2,18},{3,19},{4,20},{5,21},{6,22},{7,23},{8,24},{9,... | collective-permute-start | bytes 442376 | tf_op jit(solution)/shard_map/ppermute | solution.py:463
  103.4 13.5 %collective-permute-start.9 = (bf16[64,1152]{1,0:T(8,128)(2,1)S(1)}, bf16[64,1152]{1,0:T(8,128)(2,1)S(1)}, u32[]{:S(2)}, u32[]{:S(2)}) collective-permute-start(bf16[64,1152]{1,0:T(8,128)(2,1)S(1)} %pad_maximum_fusion.8), channel_id=1, source_target_pairs={{0,24},{1,25},{2,26},{3,27},{4,28},{5,29},{6,30},{7,31},{8,0},{9,1... | collective-permute-start | bytes 442376 | tf_op jit(solution)/shard_map/ppermute | solution.py:463
  118.0 5.3 %collective-permute-start.12 = (bf16[64,1152]{1,0:T(8,128)(2,1)S(1)}, bf16[64,1152]{1,0:T(8,128)(2,1)S(1)}, u32[]{:S(2)}, u32[]{:S(2)}) collective-permute-start(bf16[64,1152]{1,0:T(8,128)(2,1)S(1)} %pad_maximum_fusion.9), channel_id=1, source_target_pairs={{0,24},{1,25},{2,26},{3,27},{4,28},{5,29},{6,30},{7,31},{8,0},{9,1... | collective-permute-start | bytes 442376 | tf_op jit(solution)/shard_map/ppermute | solution.py:463
  119.0 13.3 %collective-permute-start.11 = (bf16[64,1152]{1,0:T(8,128)(2,1)S(1)}, bf16[64,1152]{1,0:T(8,128)(2,1)S(1)}, u32[]{:S(2)}, u32[]{:S(2)}) collective-permute-start(bf16[64,1152]{1,0:T(8,128)(2,1)S(1)} %pad_maximum_fusion.9), channel_id=1, source_target_pairs={{0,16},{1,17},{2,18},{3,19},{4,20},{5,21},{6,22},{7,23},{8,24},{9,... | collective-permute-start | bytes 442376 | tf_op jit(solution)/shard_map/ppermute | solution.py:463
  120.1 12.2 %collective-permute-start.10 = (bf16[64,1152]{1,0:T(8,128)(2,1)S(1)}, bf16[64,1152]{1,0:T(8,128)(2,1)S(1)}, u32[]{:S(2)}, u32[]{:S(2)}) collective-permute-start(bf16[64,1152]{1,0:T(8,128)(2,1)S(1)} %pad_maximum_fusion.9), channel_id=1, source_target_pairs={{0,8},{1,9},{2,10},{3,11},{4,12},{5,13},{6,14},{7,15},{8,16},{9,17... | collective-permute-start | bytes 442376 | tf_op jit(solution)/shard_map/ppermute | solution.py:463
  132.4 7.9 %collective-permute-start.13 = (bf16[4,64,640]{2,1,0:T(8,128)(2,1)S(1)}, bf16[4,64,640]{2,1,0:T(8,128)(2,1)S(1)}, u32[]{:S(2)}, u32[]{:S(2)}) collective-permute-start(bf16[4,64,640]{2,1,0:T(8,128)(2,1)S(1)} %get-tuple-element.96), channel_id=1, source_target_pairs={{0,4},{1,5},{2,6},{3,7},{4,0},{5,1},{6,2},{7,3},{8,12},{9,13},{10,... | collective-permute-start | bytes 983048 | tf_op jit(solution)/shard_map/ppermute | solution.py:463
  133.6 8.5 %collective-permute-start.15 = (bf16[4,64,512]{2,1,0:T(8,128)(2,1)S(1)}, bf16[4,64,512]{2,1,0:T(8,128)(2,1)S(1)}, u32[]{:S(2)}, u32[]{:S(2)}) collective-permute-start(bf16[4,64,512]{2,1,0:T(8,128)(2,1)S(1)} %get-tuple-element.98), channel_id=1, source_target_pairs={{0,2},{1,3},{2,0},{3,1},{4,6},{5,7},{6,4},{7,5},{8,10},{9,11},{10,... | collective-permute-start | bytes 786440 | tf_op jit(solution)/shard_map/ppermute | solution.py:463
  140.4 4.3 %collective-permute-start.17 = (bf16[2,4,64,640]{3,2,1,0:T(8,128)(2,1)S(1)}, bf16[2,4,64,640]{3,2,1,0:T(8,128)(2,1)S(1)}, u32[]{:S(2)}, u32[]{:S(2)}) collective-permute-start(bf16[2,4,64,640]{3,2,1,0:T(8,128)(2,1)S(1)} %pad_maximum_fusion.1.refs_0_), channel_id=1, source_target_pairs={{0,1},{1,0},{2,3},{3,2},{4,5},{5,4},{6,7},{7,6},{8,9},{9,8},{10,11... | collective-permute-start | bytes 1966088 | tf_op jit(solution)/shard_map/ppermute | solution.py:463
  140.5 17.1 %collective-permute-start.14 = (bf16[2,4,64,640]{3,2,1,0:T(8,128)(2,1)S(1)}, bf16[2,4,64,640]{3,2,1,0:T(8,128)(2,1)S(1)}, u32[]{:S(2)}, u32[]{:S(2)}) collective-permute-start(bf16[2,4,64,640]{3,2,1,0:T(8,128)(2,1)S(1)} %pad_maximum_fusion.1.refs_0_), channel_id=1, source_target_pairs={{0,2},{1,3},{2,0},{3,1},{4,6},{5,7},{6,4},{7,5},{8,10},{9,11},{10,... | collective-permute-start | bytes 1966088 | tf_op jit(solution)/shard_map/ppermute | solution.py:463
  142.1 2.5 %collective-permute-start.18 = (bf16[2,4,64,512]{3,2,1,0:T(8,128)(2,1)S(1)}, bf16[2,4,64,512]{3,2,1,0:T(8,128)(2,1)S(1)}, u32[]{:S(2)}, u32[]{:S(2)}) collective-permute-start(bf16[2,4,64,512]{3,2,1,0:T(8,128)(2,1)S(1)} %pad_maximum_fusion.2.refs_1_), channel_id=1, source_target_pairs={{0,1},{1,0},{2,3},{3,2},{4,5},{5,4},{6,7},{7,6},{8,9},{9,8},{10,11... | collective-permute-start | bytes 1572872 | tf_op jit(solution)/shard_map/ppermute | solution.py:463
  142.3 14.2 %collective-permute-start.16 = (bf16[2,4,64,512]{3,2,1,0:T(8,128)(2,1)S(1)}, bf16[2,4,64,512]{3,2,1,0:T(8,128)(2,1)S(1)}, u32[]{:S(2)}, u32[]{:S(2)}) collective-permute-start(bf16[2,4,64,512]{3,2,1,0:T(8,128)(2,1)S(1)} %pad_maximum_fusion.2.refs_1_), channel_id=1, source_target_pairs={{0,4},{1,5},{2,6},{3,7},{4,0},{5,1},{6,2},{7,3},{8,12},{9,13},{10,... | collective-permute-start | bytes 1572872 | tf_op jit(solution)/shard_map/ppermute | solution.py:463
  157.6 2.9 %collective-permute-start.19 = (bf16[2,4,64,640]{3,2,1,0:T(8,128)(2,1)S(1)}, bf16[2,4,64,640]{3,2,1,0:T(8,128)(2,1)S(1)}, u32[]{:S(2)}, u32[]{:S(2)}) collective-permute-start(bf16[2,4,64,640]{3,2,1,0:T(8,128)(2,1)S(1)} %collective-permute-done.14.refs_0_), channel_id=1, source_target_pairs={{0,1},{1,0},{2,3},{3,2},{4,5},{5,4},{6,7},{7,6},{8,9},{9,8},{10,11... | collective-permute-start | bytes 1966088 | tf_op jit(solution)/shard_map/ppermute | solution.py:463
  157.6 2.8 %collective-permute-start.20 = (bf16[2,4,64,512]{3,2,1,0:T(8,128)(2,1)S(1)}, bf16[2,4,64,512]{3,2,1,0:T(8,128)(2,1)S(1)}, u32[]{:S(2)}, u32[]{:S(2)}) collective-permute-start(bf16[2,4,64,512]{3,2,1,0:T(8,128)(2,1)S(1)} %collective-permute-done.16.refs_1_), channel_id=1, source_target_pairs={{0,1},{1,0},{2,3},{3,2},{4,5},{5,4},{6,7},{7,6},{8,9},{9,8},{10,11... | collective-permute-start | bytes 1572872 | tf_op jit(solution)/shard_map/ppermute | solution.py:463
  (17 other events, 131.8 us)

commit v5 on v4

--- a/solution.py
+++ b/solution.py
@@ -579,8 +579,8 @@
     groups_a[1] = [(keep_hot, ()), (got_hot, ())]
     sends_a = step_sends(groups_a, order_a[0])
     grad_input, sends_a, sends_b = lax.optimization_barrier((grad_input, sends_a, sends_b))
+    groups_a = step_takes(groups_a, order_a[0], sends_a)
     groups_b = step_takes(groups_b, order_b[0], sends_b)
-    groups_a = step_takes(groups_a, order_a[0], sends_a)
     whole = capacity % 16 == 0
     (parcel,) = call(
         cold_sums_kernel,
@@ -625,8 +625,8 @@
     ).reshape(cross_width)
 
     later = [exchange(sums[k].astype(bf16), 0, k) for k in range(1, sizes[0])]
-    later, cold_new, cold_m_new, cold_v_new, bias_grad = lax.optimization_barrier(
-        (later, cold_new, cold_m_new, cold_v_new, bias_grad)
+    later[-1], cold_new, cold_m_new, cold_v_new, bias_grad = lax.optimization_barrier(
+        (later[-1], cold_new, cold_m_new, cold_v_new, bias_grad)
     )
     dense_own = sums[0]
     for got in later:

time: 163 us -> 163 us (level)
  no operation moved by 1% of the time
where the time goes in v5:
time: 163 us; the launch traced here: 162 us
  waiting for transfers between devices  65 us (40%)
  Pallas kernels  38.2 us (23%)
  starting transfers between devices  31.9 us (20%)
  other arithmetic  15.2 us (9%)
  local copies, waits for them, and re-layouts  10.4 us (6%)
    ppermute x21, waiting for transfers between devices, exchange(): return lax.ppermute(value, 'dev', pairs)  44.1 us
    pallas_call x7, Pallas kernels, call(): pl.pallas_call(kernel, out_shape=outs, in_specs=specs, out_specs=[pl.Bloc...  31 us
    all_to_all x3, waiting for transfers between devices, all_to_all(): return lax.all_to_all(value, 'dev', split_axis=0, concat_axis=0, tiled=True)  20.9 us
    ppermute x21, starting transfers between devices, exchange(): return lax.ppermute(value, 'dev', pairs)  18.5 us
    all_to_all x3, starting transfers between devices, all_to_all(): return lax.all_to_all(value, 'dev', split_axis=0, concat_axis=0, tiled=True)  13.5 us
    unnamed x36, local copies, waits for them, and re-layouts  8.5 us
    pallas_call x4, Pallas kernels, place(): pl.pallas_call(functools.partial(place_kernel, dims, tuple(plan)), out_sh...  7.23 us
    another operation x7, other arithmetic  6.36 us
  transfers between devices with their start and end apart: 24, of which 12 were waited for; matrix products, arithmetic and copies ran while one was open for 10% of the time, Pallas kernels for 13%

profile of v5, /device:TPU:0, one launch (start us, length us, event | category | flops | bytes accessed | tf_op | source)
XLA Modules:
  0.0 162.1 jit_solution(12814389761318119792)
XLA Ops:
  0.6 7.3 %all-to-all-start = ((s32[32,1,96]{2,1,0:T(1,128)}), s32[32,1,96]{2,1,0:T(1,128)S(1)}, u32[]{:S(2)}, u32[]{:S(2)}) async-start(s32[32,1,96]{2,1,0:T(1,128)} %bitcast.213), calls=%async_computation | async-start | bytes 32768 | tf_op jit(solution)/shard_map/all_to_all | solution.py:469
  10.9 4.1 %all-to-all-done.req_ref = s32[32,1,96]{2,1,0:T(1,128)S(1)} async-done(((s32[32,1,96]{2,1,0:T(1,128)}), s32[32,1,96]{2,1,0:T(1,128)S(1)}, u32[]{:S(2)}, u32[]{:S(2)}) %all-to-all-start) | async-done | bytes 12320 | tf_op jit(solution)/shard_map/all_to_all | solution.py:469
  15.0 3.4 %owner_pick.1 = bf16[3072,128]{1,0:T(8,128)(2,1)} custom-call(s32[32,1,96]{2,1,0:T(1,128)S(1)} %all-to-all-done.req_ref, bf16[512,512]{1,0:T(8,128)(2,1)S(1)} %fold_table.1.folded_ref), custom_call_target="tpu_custom_call" | custom-call | flops 3221225472 | bytes 1323008 | tf_op jit(solution)/shard_map/owner_pick/pallas_call | solution.py:40
  18.4 2.8 %all-to-all-start.1 = ((bf16[32,96,128]{2,1,0:T(8,128)(2,1)}), bf16[32,96,128]{2,1,0:T(8,128)(2,1)S(1)}, u32[]{:S(2)}, u32[]{:S(2)}) async-start(bf16[32,96,128]{2,1,0:T(8,128)(2,1)} %bitcast.5), calls=%async_computation.1 | async-start | bytes 1572864 | tf_op jit(solution)/shard_map/all_to_all | solution.py:469
  21.2 2.5 %hot_pick.1.hot_hbm = bf16[256,2048]{1,0:T(8,128)(2,1)S(1)} custom-call(s32[256,16]{1,0:T(8,128)S(1)} %copy.29.ids_ref, s32[256,16]{1,0:T(8,128)S(1)} %copy.31.slot_ref, bf16[2048,128]{1,0:T(8,128)(2,1)S(1)} %copy-done.5), custom_call_target="tpu_custom_call" | custom-call | flops 42949672960 | bytes 1605632 | tf_op jit(solution)/shard_map/hot_pick/pallas_call | solution.py:40
  24.8 16.8 %all-to-all-done.1 = bf16[32,96,128]{2,1,0:T(8,128)(2,1)S(1)} async-done(((bf16[32,96,128]{2,1,0:T(8,128)(2,1)}), bf16[32,96,128]{2,1,0:T(8,128)(2,1)S(1)}, u32[]{:S(2)}, u32[]{:S(2)}) %all-to-all-start.1) | async-done | bytes 786464 | tf_op jit(solution)/shard_map/all_to_all | solution.py:469
  41.6 11.3 %forward.1 = (f32[16,128]{1,0:T(8,128)S(1)}, bf16[2,2,4,64,512]{4,3,2,1,0:T(8,128)(2,1)S(1)}, bf16[2,2,4,64,512]{4,3,2,1,0:T(8,128)(2,1)}, bf16[2,2,4,64,512]{4,...) custom-call(s32[4]{0:T(128)S(1)} %pad_add_fusion.digits_ref, ...), custom_call_target="tpu_custom_call" | custom-call | flops 6442450944 | bytes 12353552 | tf_op jit(solution)/shard_map/forward/pallas_call | solution.py:40
  55.7 3.6 %hot_sums.1 = (bf16[2,2,4,64,128]{4,3,2,1,0:T(8,128)(2,1)S(1)}, bf16[2,2,4,64,128]{4,3,2,1,0:T(8,128)(2,1)S(1)}) custom-call(s32[4]{0:T(128)S(1)} %pad_add_fusion.digits_ref, s32[256,16]{1,0:T(8,128)S(1)} %copy.32.id_ref, s32[16,256]{1,0:T(8,128)S(1)} %bitcast.209, bf16[256,2048]{1,0:T(8,128)(2,1)S(1)} %copy-done.8), custom_call_target="tpu_custom_call" | custom-call | flops 4294967296 | bytes 1605648 | tf_op jit(solution)/shard_map/hot_sums/pallas_call | solution.py:40
  59.4 2.1 %fusion.1 = bf16[2,4,64,512]{3,2,1,0:T(8,128)(2,1)} fusion(bf16[2,2,4,64,512]{4,3,2,1,0:T(8,128)(2,1)} %collective-permute-done.1, bf16[2,2,4,64,512]{4,3,2,1,0:T(8,128)(2,1)S(1)} %get-tuple-element.46), kind=kLoop, calls=%fused_computation.5 | loop fusion | flops 1048576 | bytes 1572864 | tf_op jit(solution)/shard_map/convert_element_type | solution.py:562
  66.7 4.7 %cold_sums.1 = bf16[32,112,128]{2,1,0:T(8,128)(2,1)} custom-call(s32[256,16]{1,0:T(8,128)S(1)} %copy.31.slot_ref, s32[16,256]{1,0:T(8,128)S(1)} %bitcast.208, bf16[256,2048]{1,0:T(8,128)(2,1)S(1)} %copy-done.9, f32[16,128]{1,0:T(8,128)S(1)} %get-tuple-element.54.bias_ref), custom_call_target="tpu_custom_call" | custom-call | flops 6442450944 | bytes 2007040 | tf_op jit(solution)/shard_map/cold_sums/pallas_call | solution.py:40
  71.4 3.4 %all-to-all-start.2 = ((bf16[32,112,128]{2,1,0:T(8,128)(2,1)}), bf16[32,112,128]{2,1,0:T(8,128)(2,1)}, u32[]{:S(2)}, u32[]{:S(2)}) async-start(bf16[32,112,128]{2,1,0:T(8,128)(2,1)} %cold_sums.1), calls=%async_computation.2 | async-start | bytes 1835008 | tf_op jit(solution)/shard_map/all_to_all | solution.py:469
  74.7 3.9 %collective-permute-done.5 = bf16[2,4,64,512]{3,2,1,0:T(8,128)(2,1)S(1)} collective-permute-done((bf16[2,4,64,512]{3,2,1,0:T(8,128)(2,1)}, bf16[2,4,64,512]{3,2,1,0:T(8,128)(2,1)S(1)}, u32[]{:S(2)}, u32[]{:S(2)}) %collective-permute-start.5) | collective-permute-done | bytes 524320 | tf_op jit(solution)/shard_map/ppermute | solution.py:463
  78.6 1.9 %fusion.2 = bf16[4,64,512]{2,1,0:T(8,128)(2,1)} fusion(bf16[2,4,64,512]{3,2,1,0:T(8,128)(2,1)S(1)} %collective-permute-done.5, bf16[2,2,4,64,512]{4,3,2,1,0:T(8,128)(2,1)} %collective-permute-done.1, bf16[2,2,4,64,512]{4,3,2,1,0:T(8,128)(2,1)S(1)} %get-tuple-element.46), kind=kLoop, calls=%fused_computation.8 | loop fusion | flops 786432 | bytes 1048576 | tf_op jit(solution)/shard_map/convert_element_type | solution.py:562
  80.6 2.3 %collective-permute-start.6 = (bf16[4,64,512]{2,1,0:T(8,128)(2,1)}, bf16[4,64,512]{2,1,0:T(8,128)(2,1)}, u32[]{:S(2)}, u32[]{:S(2)}) collective-permute-start(bf16[4,64,512]{2,1,0:T(8,128)(2,1)} %fusion.2), channel_id=1, source_target_pairs={{0,2},{1,3},{2,0},{3,1},{4,6},{5,7},{6,4},{7,5},{8,10},{9,11},{10,... | collective-permute-start | bytes 786440 | tf_op jit(solution)/shard_map/ppermute | solution.py:463
  82.9 5.2 %collective-permute-done.3 = bf16[2,4,64,640]{3,2,1,0:T(8,128)(2,1)} collective-permute-done((bf16[2,4,64,640]{3,2,1,0:T(8,128)(2,1)}, bf16[2,4,64,640]{3,2,1,0:T(8,128)(2,1)}, u32[]{:S(2)}, u32[]{:S(2)}) %collective-permute-start.3) | collective-permute-done | bytes 655392 | tf_op jit(solution)/shard_map/ppermute | solution.py:463
  91.6 6.2 %collective-permute-done.6 = bf16[4,64,512]{2,1,0:T(8,128)(2,1)} collective-permute-done((bf16[4,64,512]{2,1,0:T(8,128)(2,1)}, bf16[4,64,512]{2,1,0:T(8,128)(2,1)}, u32[]{:S(2)}, u32[]{:S(2)}) %collective-permute-start.6) | collective-permute-done | bytes 262176 | tf_op jit(solution)/shard_map/ppermute | solution.py:463
  102.1 2.7 %collective-permute-start.9 = (bf16[64,1152]{1,0:T(8,128)(2,1)S(1)}, bf16[64,1152]{1,0:T(8,128)(2,1)S(1)}, u32[]{:S(2)}, u32[]{:S(2)}) collective-permute-start(bf16[64,1152]{1,0:T(8,128)(2,1)S(1)} %pad_maximum_fusion.8), channel_id=1, source_target_pairs={{0,24},{1,25},{2,26},{3,27},{4,28},{5,29},{6,30},{7,31},{8,0},{9,1... | collective-permute-start | bytes 442376 | tf_op jit(solution)/shard_map/ppermute | solution.py:463
  108.8 5.5 %cold_adam.1 = (f32[2048,128]{1,0:T(8,128)}, f32[2048,128]{1,0:T(8,128)}, f32[2048,128]{1,0:T(8,128)}) custom-call(s32[24,128]{1,0:T(8,128)S(1)} %reshape.155.req_ref, bf16[3072,128]{1,0:T(8,128)(2,1)S(1)} %bitcast.207, f32[2048,128]{1,0:T(8,128)S(1)} %copy-done.1, f32[2048,128]{1,0:T(8,128)S(1)} %copy-done.3, f32[2048,128]{1,0:T(8,128)S(1)} %copy-done.4), custom_call_target="tpu_custom_call" | custom-call | flops 3221225472 | bytes 7090176 | tf_op jit(solution)/shard_map/cold_adam/pallas_call | solution.py:40
  116.9 3.9 %collective-permute-start.12 = (bf16[64,1152]{1,0:T(8,128)(2,1)S(1)}, bf16[64,1152]{1,0:T(8,128)(2,1)S(1)}, u32[]{:S(2)}, u32[]{:S(2)}) collective-permute-start(bf16[64,1152]{1,0:T(8,128)(2,1)S(1)} %pad_maximum_fusion.9), channel_id=1, source_target_pairs={{0,24},{1,25},{2,26},{3,27},{4,28},{5,29},{6,30},{7,31},{8,0},{9,1... | collective-permute-start | bytes 442376 | tf_op jit(solution)/shard_map/ppermute | solution.py:463
  121.5 3.1 %collective-permute-done.12 = bf16[64,1152]{1,0:T(8,128)(2,1)S(1)} collective-permute-done((bf16[64,1152]{1,0:T(8,128)(2,1)S(1)}, bf16[64,1152]{1,0:T(8,128)(2,1)S(1)}, u32[]{:S(2)}, u32[]{:S(2)}) %collective-permute-start.12) | collective-permute-done | bytes 147488 | tf_op jit(solution)/shard_map/ppermute | solution.py:463
  124.5 7.0 %collective-permute-done.11 = bf16[64,1152]{1,0:T(8,128)(2,1)S(1)} collective-permute-done((bf16[64,1152]{1,0:T(8,128)(2,1)S(1)}, bf16[64,1152]{1,0:T(8,128)(2,1)S(1)}, u32[]{:S(2)}, u32[]{:S(2)}) %collective-permute-start.11) | collective-permute-done | bytes 147488 | tf_op jit(solution)/shard_map/ppermute | solution.py:463
  133.8 6.1 %collective-permute-done.13 = bf16[4,64,640]{2,1,0:T(8,128)(2,1)S(1)} collective-permute-done((bf16[4,64,640]{2,1,0:T(8,128)(2,1)S(1)}, bf16[4,64,640]{2,1,0:T(8,128)(2,1)S(1)}, u32[]{:S(2)}, u32[]{:S(2)}) %collective-permute-start.13) | collective-permute-done | bytes 327712 | tf_op jit(solution)/shard_map/ppermute | solution.py:463
  144.0 1.8 %place.5 = (bf16[2048,1024]{1,0:T(8,128)(2,1)}, f32[2048,128]{1,0:T(8,128)}) custom-call(s32[4]{0:T(128)S(1)} %pad_add_fusion.digits_ref, bf16[2,4,64,640]{3,2,1,0:T(8,128)(2,1)S(1)} %collective-permute-done.17.refs_0_, bf16[2,4,64,512]{3,2,1,0:T(8,128)(2,1)S(1)} %collective-permute-done.18.refs_1_, ...), custom_call_target="tpu_custom_call", output_to_operand_aliasing={{0}: (3, {}), {1}: (4, {})} | custom-call | bytes 4194304 | tf_op jit(solution)/shard_map/place/pallas_call | solution.py:387
  145.8 10.2 %collective-permute-done.16.refs_1_ = bf16[2,4,64,512]{3,2,1,0:T(8,128)(2,1)S(1)} collective-permute-done((bf16[2,4,64,512]{3,2,1,0:T(8,128)(2,1)S(1)}, bf16[2,4,64,512]{3,2,1,0:T(8,128)(2,1)S(1)}, u32[]{:S(2)}, u32[]{:S(2)}) %collective-permute-start.16) | collective-permute-done | bytes 524320 | tf_op jit(solution)/shard_map/ppermute | solution.py:463
  (110 shorter events, 39.1 us)
Async XLA Ops:
  0.6 14.4 %all-to-all-start = ((s32[32,1,96]{2,1,0:T(1,128)}), s32[32,1,96]{2,1,0:T(1,128)S(1)}, u32[]{:S(2)}, u32[]{:S(2)}) async-start(s32[32,1,96]{2,1,0:T(1,128)} %bitcast.213), calls=%async_computation | async-start | bytes 32768 | tf_op jit(solution)/shard_map/all_to_all | solution.py:469
  18.4 23.2 %all-to-all-start.1 = ((bf16[32,96,128]{2,1,0:T(8,128)(2,1)}), bf16[32,96,128]{2,1,0:T(8,128)(2,1)S(1)}, u32[]{:S(2)}, u32[]{:S(2)}) async-start(bf16[32,96,128]{2,1,0:T(8,128)(2,1)} %bitcast.5), calls=%async_computation.1 | async-start | bytes 1572864 | tf_op jit(solution)/shard_map/all_to_all | solution.py:469
  53.9 5.5 %collective-permute-start.1 = (bf16[2,2,4,64,512]{4,3,2,1,0:T(8,128)(2,1)}, bf16[2,2,4,64,512]{4,3,2,1,0:T(8,128)(2,1)}, u32[]{:S(2)}, u32[]{:S(2)}) collective-permute-start(bf16[2,2,4,64,512]{4,3,2,1,0:T(8,128)(2,1)} %get-tuple-element.47), channel_id=1, source_target_pairs={{0,1},{1,0},{2,3},{3,2},{4,5},{5,4},{6,7},{7,6},{8,9},{9,8},{10,11... | collective-permute-start | bytes 3145736 | tf_op jit(solution)/shard_map/ppermute | solution.py:463
  53.9 7.7 %collective-permute-start = (bf16[2,2,4,64,512]{4,3,2,1,0:T(8,128)(2,1)}, bf16[2,2,4,64,512]{4,3,2,1,0:T(8,128)(2,1)}, u32[]{:S(2)}, u32[]{:S(2)}) collective-permute-start(bf16[2,2,4,64,512]{4,3,2,1,0:T(8,128)(2,1)} %get-tuple-element.43), channel_id=1, source_target_pairs={{0,1},{1,0},{2,3},{3,2},{4,5},{5,4},{6,7},{7,6},{8,9},{9,8},{10,11... | collective-permute-start | bytes 3145736 | tf_op jit(solution)/shard_map/ppermute | solution.py:463
  59.3 2.2 %collective-permute-start.2 = (bf16[2,2,4,64,128]{4,3,2,1,0:T(8,128)(2,1)S(1)}, bf16[2,2,4,64,128]{4,3,2,1,0:T(8,128)(2,1)S(1)}, u32[]{:S(2)}, u32[]{:S(2)}) collective-permute-start(bf16[2,2,4,64,128]{4,3,2,1,0:T(8,128)(2,1)S(1)} %get-tuple-element.48), channel_id=1, source_target_pairs={{0,1},{1,0},{2,3},{3,2},{4,5},{5,4},{6,7},{7,6},{8,9},{9,8},{10,11... | collective-permute-start | bytes 786440 | tf_op jit(solution)/shard_map/ppermute | solution.py:463
  63.7 14.9 %collective-permute-start.5 = (bf16[2,4,64,512]{3,2,1,0:T(8,128)(2,1)}, bf16[2,4,64,512]{3,2,1,0:T(8,128)(2,1)S(1)}, u32[]{:S(2)}, u32[]{:S(2)}) collective-permute-start(bf16[2,4,64,512]{3,2,1,0:T(8,128)(2,1)} %fusion.1), channel_id=1, source_target_pairs={{0,4},{1,5},{2,6},{3,7},{4,0},{5,1},{6,2},{7,3},{8,12},{9,13},{10,... | collective-permute-start | bytes 1572872 | tf_op jit(solution)/shard_map/ppermute | solution.py:463
  65.3 22.8 %collective-permute-start.3 = (bf16[2,4,64,640]{3,2,1,0:T(8,128)(2,1)}, bf16[2,4,64,640]{3,2,1,0:T(8,128)(2,1)}, u32[]{:S(2)}, u32[]{:S(2)}) collective-permute-start(bf16[2,4,64,640]{3,2,1,0:T(8,128)(2,1)} %pad_maximum_fusion), channel_id=1, source_target_pairs={{0,2},{1,3},{2,0},{3,1},{4,6},{5,7},{6,4},{7,5},{8,10},{9,11},{10,... | collective-permute-start | bytes 1966088 | tf_op jit(solution)/shard_map/ppermute | solution.py:463
  71.4 33.7 %all-to-all-start.2 = ((bf16[32,112,128]{2,1,0:T(8,128)(2,1)}), bf16[32,112,128]{2,1,0:T(8,128)(2,1)}, u32[]{:S(2)}, u32[]{:S(2)}) async-start(bf16[32,112,128]{2,1,0:T(8,128)(2,1)} %cold_sums.1), calls=%async_computation.2 | async-start | bytes 1835008 | tf_op jit(solution)/shard_map/all_to_all | solution.py:469
  80.6 17.3 %collective-permute-start.6 = (bf16[4,64,512]{2,1,0:T(8,128)(2,1)}, bf16[4,64,512]{2,1,0:T(8,128)(2,1)}, u32[]{:S(2)}, u32[]{:S(2)}) collective-permute-start(bf16[4,64,512]{2,1,0:T(8,128)(2,1)} %fusion.2), channel_id=1, source_target_pairs={{0,2},{1,3},{2,0},{3,1},{4,6},{5,7},{6,4},{7,5},{8,10},{9,11},{10,... | collective-permute-start | bytes 786440 | tf_op jit(solution)/shard_map/ppermute | solution.py:463
  90.1 9.6 %collective-permute-start.4 = (bf16[4,64,640]{2,1,0:T(8,128)(2,1)S(1)}, bf16[4,64,640]{2,1,0:T(8,128)(2,1)S(1)}, u32[]{:S(2)}, u32[]{:S(2)}) collective-permute-start(bf16[4,64,640]{2,1,0:T(8,128)(2,1)S(1)} %pad_maximum_fusion.3), channel_id=1, source_target_pairs={{0,4},{1,5},{2,6},{3,7},{4,0},{5,1},{6,2},{7,3},{8,12},{9,13},{10,... | collective-permute-start | bytes 983048 | tf_op jit(solution)/shard_map/ppermute | solution.py:463
  101.8 14.0 %collective-permute-start.8 = (bf16[64,1152]{1,0:T(8,128)(2,1)S(1)}, bf16[64,1152]{1,0:T(8,128)(2,1)S(1)}, u32[]{:S(2)}, u32[]{:S(2)}) collective-permute-start(bf16[64,1152]{1,0:T(8,128)(2,1)S(1)} %pad_maximum_fusion.7), channel_id=1, source_target_pairs={{0,16},{1,17},{2,18},{3,19},{4,20},{5,21},{6,22},{7,23},{8,24},{9,... | collective-permute-start | bytes 442376 | tf_op jit(solution)/shard_map/ppermute | solution.py:463
  102.1 13.7 %collective-permute-start.9 = (bf16[64,1152]{1,0:T(8,128)(2,1)S(1)}, bf16[64,1152]{1,0:T(8,128)(2,1)S(1)}, u32[]{:S(2)}, u32[]{:S(2)}) collective-permute-start(bf16[64,1152]{1,0:T(8,128)(2,1)S(1)} %pad_maximum_fusion.8), channel_id=1, source_target_pairs={{0,24},{1,25},{2,26},{3,27},{4,28},{5,29},{6,30},{7,31},{8,0},{9,1... | collective-permute-start | bytes 442376 | tf_op jit(solution)/shard_map/ppermute | solution.py:463
  104.8 11.0 %collective-permute-start.7 = (bf16[64,1152]{1,0:T(8,128)(2,1)S(1)}, bf16[64,1152]{1,0:T(8,128)(2,1)S(1)}, u32[]{:S(2)}, u32[]{:S(2)}) collective-permute-start(bf16[64,1152]{1,0:T(8,128)(2,1)S(1)} %pad_maximum_fusion.6), channel_id=1, source_target_pairs={{0,8},{1,9},{2,10},{3,11},{4,12},{5,13},{6,14},{7,15},{8,16},{9,17... | collective-permute-start | bytes 442376 | tf_op jit(solution)/shard_map/ppermute | solution.py:463
  116.9 7.6 %collective-permute-start.12 = (bf16[64,1152]{1,0:T(8,128)(2,1)S(1)}, bf16[64,1152]{1,0:T(8,128)(2,1)S(1)}, u32[]{:S(2)}, u32[]{:S(2)}) collective-permute-start(bf16[64,1152]{1,0:T(8,128)(2,1)S(1)} %pad_maximum_fusion.9), channel_id=1, source_target_pairs={{0,24},{1,25},{2,26},{3,27},{4,28},{5,29},{6,30},{7,31},{8,0},{9,1... | collective-permute-start | bytes 442376 | tf_op jit(solution)/shard_map/ppermute | solution.py:463
  120.8 10.8 %collective-permute-start.11 = (bf16[64,1152]{1,0:T(8,128)(2,1)S(1)}, bf16[64,1152]{1,0:T(8,128)(2,1)S(1)}, u32[]{:S(2)}, u32[]{:S(2)}) collective-permute-start(bf16[64,1152]{1,0:T(8,128)(2,1)S(1)} %pad_maximum_fusion.9), channel_id=1, source_target_pairs={{0,16},{1,17},{2,18},{3,19},{4,20},{5,21},{6,22},{7,23},{8,24},{9,... | collective-permute-start | bytes 442376 | tf_op jit(solution)/shard_map/ppermute | solution.py:463
  120.8 10.8 %collective-permute-start.10 = (bf16[64,1152]{1,0:T(8,128)(2,1)S(1)}, bf16[64,1152]{1,0:T(8,128)(2,1)S(1)}, u32[]{:S(2)}, u32[]{:S(2)}) collective-permute-start(bf16[64,1152]{1,0:T(8,128)(2,1)S(1)} %pad_maximum_fusion.9), channel_id=1, source_target_pairs={{0,8},{1,9},{2,10},{3,11},{4,12},{5,13},{6,14},{7,15},{8,16},{9,17... | collective-permute-start | bytes 442376 | tf_op jit(solution)/shard_map/ppermute | solution.py:463
  131.7 8.3 %collective-permute-start.13 = (bf16[4,64,640]{2,1,0:T(8,128)(2,1)S(1)}, bf16[4,64,640]{2,1,0:T(8,128)(2,1)S(1)}, u32[]{:S(2)}, u32[]{:S(2)}) collective-permute-start(bf16[4,64,640]{2,1,0:T(8,128)(2,1)S(1)} %get-tuple-element.92), channel_id=1, source_target_pairs={{0,4},{1,5},{2,6},{3,7},{4,0},{5,1},{6,2},{7,3},{8,12},{9,13},{10,... | collective-permute-start | bytes 983048 | tf_op jit(solution)/shard_map/ppermute | solution.py:463
  132.8 8.7 %collective-permute-start.15 = (bf16[4,64,512]{2,1,0:T(8,128)(2,1)S(1)}, bf16[4,64,512]{2,1,0:T(8,128)(2,1)S(1)}, u32[]{:S(2)}, u32[]{:S(2)}) collective-permute-start(bf16[4,64,512]{2,1,0:T(8,128)(2,1)S(1)} %get-tuple-element.94), channel_id=1, source_target_pairs={{0,2},{1,3},{2,0},{3,1},{4,6},{5,7},{6,4},{7,5},{8,10},{9,11},{10,... | collective-permute-start | bytes 786440 | tf_op jit(solution)/shard_map/ppermute | solution.py:463
  140.0 4.0 %collective-permute-start.17 = (bf16[2,4,64,640]{3,2,1,0:T(8,128)(2,1)S(1)}, bf16[2,4,64,640]{3,2,1,0:T(8,128)(2,1)S(1)}, u32[]{:S(2)}, u32[]{:S(2)}) collective-permute-start(bf16[2,4,64,640]{3,2,1,0:T(8,128)(2,1)S(1)} %pad_maximum_fusion.1.refs_0_), channel_id=1, source_target_pairs={{0,1},{1,0},{2,3},{3,2},{4,5},{5,4},{6,7},{7,6},{8,9},{9,8},{10,11... | collective-permute-start | bytes 1966088 | tf_op jit(solution)/shard_map/ppermute | solution.py:463
  140.1 17.1 %collective-permute-start.14 = (bf16[2,4,64,640]{3,2,1,0:T(8,128)(2,1)S(1)}, bf16[2,4,64,640]{3,2,1,0:T(8,128)(2,1)S(1)}, u32[]{:S(2)}, u32[]{:S(2)}) collective-permute-start(bf16[2,4,64,640]{3,2,1,0:T(8,128)(2,1)S(1)} %pad_maximum_fusion.1.refs_0_), channel_id=1, source_target_pairs={{0,2},{1,3},{2,0},{3,1},{4,6},{5,7},{6,4},{7,5},{8,10},{9,11},{10,... | collective-permute-start | bytes 1966088 | tf_op jit(solution)/shard_map/ppermute | solution.py:463
  141.6 2.3 %collective-permute-start.18 = (bf16[2,4,64,512]{3,2,1,0:T(8,128)(2,1)S(1)}, bf16[2,4,64,512]{3,2,1,0:T(8,128)(2,1)S(1)}, u32[]{:S(2)}, u32[]{:S(2)}) collective-permute-start(bf16[2,4,64,512]{3,2,1,0:T(8,128)(2,1)S(1)} %pad_maximum_fusion.2.refs_1_), channel_id=1, source_target_pairs={{0,1},{1,0},{2,3},{3,2},{4,5},{5,4},{6,7},{7,6},{8,9},{9,8},{10,11... | collective-permute-start | bytes 1572872 | tf_op jit(solution)/shard_map/ppermute | solution.py:463
  141.8 14.2 %collective-permute-start.16 = (bf16[2,4,64,512]{3,2,1,0:T(8,128)(2,1)S(1)}, bf16[2,4,64,512]{3,2,1,0:T(8,128)(2,1)S(1)}, u32[]{:S(2)}, u32[]{:S(2)}) collective-permute-start(bf16[2,4,64,512]{3,2,1,0:T(8,128)(2,1)S(1)} %pad_maximum_fusion.2.refs_1_), channel_id=1, source_target_pairs={{0,4},{1,5},{2,6},{3,7},{4,0},{5,1},{6,2},{7,3},{8,12},{9,13},{10,... | collective-permute-start | bytes 1572872 | tf_op jit(solution)/shard_map/ppermute | solution.py:463
  157.2 2.9 %collective-permute-start.19 = (bf16[2,4,64,640]{3,2,1,0:T(8,128)(2,1)S(1)}, bf16[2,4,64,640]{3,2,1,0:T(8,128)(2,1)S(1)}, u32[]{:S(2)}, u32[]{:S(2)}) collective-permute-start(bf16[2,4,64,640]{3,2,1,0:T(8,128)(2,1)S(1)} %collective-permute-done.14.refs_0_), channel_id=1, source_target_pairs={{0,1},{1,0},{2,3},{3,2},{4,5},{5,4},{6,7},{7,6},{8,9},{9,8},{10,11... | collective-permute-start | bytes 1966088 | tf_op jit(solution)/shard_map/ppermute | solution.py:463
  157.2 2.8 %collective-permute-start.20 = (bf16[2,4,64,512]{3,2,1,0:T(8,128)(2,1)S(1)}, bf16[2,4,64,512]{3,2,1,0:T(8,128)(2,1)S(1)}, u32[]{:S(2)}, u32[]{:S(2)}) collective-permute-start(bf16[2,4,64,512]{3,2,1,0:T(8,128)(2,1)S(1)} %collective-permute-done.16.refs_1_), channel_id=1, source_target_pairs={{0,1},{1,0},{2,3},{3,2},{4,5},{5,4},{6,7},{7,6},{8,9},{9,8},{10,11... | collective-permute-start | bytes 1572872 | tf_op jit(solution)/shard_map/ppermute | solution.py:463
  (17 other events, 130.8 us)
